TPU v7x, 256 devices: a whole 4x4x8 slice. The times are simulated.
256 devices in a mesh: inst: 32 (over x_hi, z, core), tp: 8 (over y, x_lo).
Axes of the slice: x: 4 (x_hi: 2, x_lo: 2; x = x_hi * 2 + x_lo), y: 4, z: 8, core: 2. Of those that a mesh axis runs over, the one named last changes fastest.
Arguments:
- step_tokens: bfloat16 [4, 256, 2048], P(None, 'inst'), may hold values from -6 to 6
- delta_state: float32 [256, 16, 128, 128], P('inst', 'tp'), may hold values from -4 to 4
- kv_pages: bfloat16 [2048, 2, 64, 256], P('inst', None, 'tp'), may hold values from -240 to 240
- page_table: int32 [256, 8], P('inst'), may hold values from 0 to 63, as said below
- lengths: int32 [256], replicated, may hold values from 1 to 508
- moves: int32 [4, 16, 4], replicated, may hold values from 0 to 31, as said below
- delta_norm: bfloat16 [2048], replicated, may hold values from 0.25 to 1.75
- head_norm: bfloat16 [128], replicated, may hold values from 0.25 to 1.75
- w_qk: bfloat16 [2048, 2, 1024], P(None, None, 'tp'), may hold values from -0.125 to 0.125
- w_vz: bfloat16 [2048, 2, 2048], P(None, None, 'tp'), may hold values from -0.125 to 0.125
- w_ba: bfloat16 [2048, 2, 16], P(None, None, 'tp'), may hold values from -0.125 to 0.125
- a_log: float32 [16], P('tp'), may hold values from -2 to 1.5
- dt_bias: float32 [16], P('tp'), may hold values from -2 to 1
- w_out: bfloat16 [2048, 2048], P('tp'), may hold values from -0.125 to 0.125
- att_norm: bfloat16 [2048], replicated, may hold values from 0.25 to 1.75
- qk_norm: bfloat16 [2, 256], replicated, may hold values from 0.25 to 1.75
- w_q: bfloat16 [2048, 2048], P(None, 'tp'), may hold values from -0.125 to 0.125
- w_kv: bfloat16 [2048, 2, 256], replicated, may hold values from -0.125 to 0.125
- w_o: bfloat16 [2048, 2048], P('tp'), may hold values from -0.125 to 0.125
Outputs:
- mixed: bfloat16 [4, 256, 2048], P(None, 'inst')
- final_state: float32 [256, 16, 128, 128], P('inst', 'tp')
- final_pages: bfloat16 [2048, 2, 64, 256], P('inst', None, 'tp')
Inputs may be any that keep to these rules, and one draw needn't show every extreme that they name: Each instance's rows of page_table hold each of 0 to 63 once. `moves`: within one step the 16 source instances and the 16 destination instances are 32 distinct instances; columns 1 and 3 are slots below 8.
All inputs are finite; a program needn't handle non-finite values.
Results may differ from a plain program's by a relative error of at most 0.04.
Values may be sent and summed in bfloat16 or wider, within the bound.
No kernel may reach another device: no remote copies, remote signals or barrier semaphores. Data moves between devices by JAX's collectives and lax.ppermute only.
A program may use at most 128 MiB of HBM per device.

v0:
```python
import jax
import jax.numpy as jnp
from jax import lax
from jax.sharding import PartitionSpec as P

HV = 16
HK = 8
DK = 128
DV = 128
HD = 256
STEPS = 4


def merged(shard, axis, join):
    gathered = jax.tree.map(
        lambda a, kind: lax.all_gather(a.astype(kind), axis),
        shard,
        (jnp.bfloat16, jnp.bfloat16, jnp.bfloat16),
    )

    def take(source):
        return jax.tree.map(
            lambda a, own: lax.dynamic_index_in_dim(a, source, 0, False).astype(own.dtype),
            gathered,
            shard,
        )

    return lax.fori_loop(
        1, lax.axis_size(axis), lambda source, state: join(state, take(source)), take(0)
    )


def rms_norm(values, gain_vec):
    scale = lax.rsqrt(jnp.mean(values * values, axis=-1, keepdims=True) + 1e-06)
    return values * scale * gain_vec.astype(jnp.float32)


def unit_heads(values):
    return values * lax.rsqrt(jnp.sum(values * values, axis=-1, keepdims=True) + 1e-06)


def combine_parts(first, second):
    highest = jnp.maximum(first[0], second[0])
    first_scale = jnp.exp(first[0] - highest)
    second_scale = jnp.exp(second[0] - highest)
    return (
        highest,
        first[1] * first_scale + second[1] * second_scale,
        first[2] * first_scale[..., None] + second[2] * second_scale[..., None],
    )


def add_branch(partial_value, residual):
    return residual + lax.psum(partial_value, "tp")


def move_lengths(context, pair_rows, slot_count):
    source = pair_rows[:, 0] * slot_count + pair_rows[:, 1]
    target = pair_rows[:, 2] * slot_count + pair_rows[:, 3]
    context = context.at[target].set(context[source])
    return context.at[source].set(jnp.zeros_like(context[source]))


def migrate_here(states, kv_pool, page_table, pair_rows, my_inst):
    source_hit = pair_rows[:, 0] == my_inst
    target_hit = pair_rows[:, 2] == my_inst
    is_source = jnp.any(source_hit)
    is_target = jnp.any(target_hit)
    out_slot = jnp.sum(jnp.where(source_hit, pair_rows[:, 1], 0))
    in_slot = jnp.sum(jnp.where(target_hit, pair_rows[:, 3], 0))
    from_inst = jnp.sum(jnp.where(target_hit, pair_rows[:, 0], 0))
    out_state = jnp.where(is_source, states[out_slot], jnp.zeros_like(states[out_slot]))
    out_pages = jnp.where(
        is_source, kv_pool[page_table[out_slot]], jnp.zeros_like(kv_pool[page_table[out_slot]])
    )
    every_state = lax.all_gather(out_state[None], "inst", axis=0, tiled=True)
    every_pages = lax.all_gather(out_pages[None], "inst", axis=0, tiled=True)
    got_state = every_state[from_inst]
    got_pages = every_pages[from_inst]
    states = states.at[in_slot].set(jnp.where(is_target, got_state, states[in_slot]))
    states = states.at[out_slot].set(
        jnp.where(is_source, jnp.zeros_like(out_state), states[out_slot])
    )
    target_pages = page_table[in_slot]
    kv_pool = kv_pool.at[target_pages].set(jnp.where(is_target, got_pages, kv_pool[target_pages]))
    return (states, kv_pool)


def delta_local(hidden, states, delta_norm, head_norm, w_qk, w_vz, w_ba, a_log, dt_bias, w_out):
    row_count = hidden.shape[0]
    keys_local = w_qk.shape[2] // DK
    values_local = w_vz.shape[2] // DV
    normed = rms_norm(hidden, delta_norm).astype(jnp.bfloat16)
    pair_qk = jnp.einsum("bd,dtc->btc", normed, w_qk, preferred_element_type=jnp.float32)
    pair_vz = jnp.einsum("bd,dtc->btc", normed, w_vz, preferred_element_type=jnp.float32)
    pair_ba = jnp.einsum("bd,dtc->btc", normed, w_ba, preferred_element_type=jnp.float32)
    group_size = HV // HK
    queries = jnp.repeat(
        unit_heads(pair_qk[:, 0].reshape(row_count, keys_local, DK)), group_size, axis=1
    ) * DK ** (-0.5)
    key_dirs = jnp.repeat(
        unit_heads(pair_qk[:, 1].reshape(row_count, keys_local, DK)), group_size, axis=1
    )
    values = pair_vz[:, 0].reshape(row_count, values_local, DV)
    gate_z = pair_vz[:, 1].reshape(row_count, values_local, DV)
    write_rate = jax.nn.sigmoid(pair_ba[:, 0])
    decays = jnp.exp(-jnp.exp(a_log) * jax.nn.softplus(pair_ba[:, 1] + dt_bias))
    states = states * decays[:, :, None, None]
    recalled = jnp.einsum("bhk,bhkv->bhv", key_dirs, states, precision=lax.Precision.HIGHEST)
    update = write_rate[:, :, None] * (values - recalled)
    states = states + key_dirs[:, :, :, None] * update[:, :, None, :]
    readout = jnp.einsum("bhk,bhkv->bhv", queries, states, precision=lax.Precision.HIGHEST)
    readout = rms_norm(readout, head_norm) * jax.nn.silu(gate_z)
    readout = readout.astype(jnp.bfloat16).reshape(row_count, values_local * DV)
    return (jnp.dot(readout, w_out, preferred_element_type=jnp.float32), states)


def attend_local(
    hidden, kv_pool, own_lengths, page_table, att_norm, qk_norm, w_q, w_kv, w_o, my_part
):
    row_count = hidden.shape[0]
    rows_part = kv_pool.shape[2]
    page_len = rows_part * lax.axis_size("tp")
    pages_req = page_table.shape[1]
    heads_local = w_q.shape[1] // HD
    normed = rms_norm(hidden, att_norm).astype(jnp.bfloat16)
    queries = jnp.dot(normed, w_q, preferred_element_type=jnp.float32).reshape(
        row_count, heads_local, HD
    )
    queries = (
        rms_norm(queries, qk_norm[0]).astype(jnp.bfloat16).reshape(row_count, heads_local * HD)
    )
    every_query = lax.all_gather(queries, "tp", axis=1, tiled=True).reshape(row_count, -1, HD)
    kv_new = jnp.einsum("bd,dtc->btc", normed, w_kv, preferred_element_type=jnp.float32)
    new_entry = jnp.stack([rms_norm(kv_new[:, 0], qk_norm[1]), kv_new[:, 1]], axis=1).astype(
        jnp.bfloat16
    )
    slot_ids = jnp.arange(row_count)
    page_of = page_table[slot_ids, own_lengths // page_len]
    offset = own_lengths % page_len
    holder = offset // rows_part
    row_index = offset % rows_part
    current = kv_pool[page_of, :, row_index, :]
    kv_pool = kv_pool.at[page_of, :, row_index, :].set(
        jnp.where((holder == my_part)[:, None, None], new_entry, current)
    )
    context_kv = kv_pool[page_table]
    key_rows = context_kv[:, :, 0].reshape(row_count, -1, HD)
    value_rows = context_kv[:, :, 1].reshape(row_count, -1, HD)
    positions = (
        jnp.arange(pages_req)[:, None] * page_len
        + my_part * rows_part
        + jnp.arange(rows_part)[None, :]
    ).reshape(-1)
    visible = positions[None, :] <= own_lengths[:, None]
    scores = (
        jnp.einsum("bqh,bph->bqp", every_query, key_rows, preferred_element_type=jnp.float32)
        / float(HD) ** 0.5
    )
    scores = jnp.where(visible[:, None, :], scores, -1e30)
    highest = jnp.max(scores, axis=-1)
    weights = jnp.where(visible[:, None, :], jnp.exp(scores - highest[..., None]), 0.0)
    weight_sum = jnp.sum(weights, axis=-1)
    weighted = jnp.einsum(
        "bqp,bph->bqh", weights.astype(jnp.bfloat16), value_rows, preferred_element_type=jnp.float32
    )
    highest, weight_sum, weighted = merged((highest, weight_sum, weighted), "tp", combine_parts)
    head_out = (weighted / weight_sum[..., None]).astype(jnp.bfloat16)
    own_heads = lax.dynamic_slice_in_dim(head_out, my_part * heads_local, heads_local, 1).reshape(
        row_count, heads_local * HD
    )
    return (jnp.dot(own_heads, w_o, preferred_element_type=jnp.float32), kv_pool)


def body(
    step_tokens,
    delta_state,
    kv_pages,
    page_table,
    lengths,
    moves,
    delta_norm,
    head_norm,
    w_qk,
    w_vz,
    w_ba,
    a_log,
    dt_bias,
    w_out,
    att_norm,
    qk_norm,
    w_q,
    w_kv,
    w_o,
):
    slot_count = step_tokens.shape[1]
    my_inst = lax.axis_index("inst")
    my_part = lax.axis_index("tp")
    states = delta_state
    kv_pool = kv_pages
    context = lengths
    outputs = []
    for step_index in range(STEPS):
        pair_rows = moves[step_index]
        states, kv_pool = migrate_here(states, kv_pool, page_table, pair_rows, my_inst)
        context = move_lengths(context, pair_rows, slot_count)
        hidden = step_tokens[step_index].astype(jnp.float32)
        partial_value, states = delta_local(
            hidden, states, delta_norm, head_norm, w_qk, w_vz, w_ba, a_log, dt_bias, w_out
        )
        hidden = add_branch(partial_value, hidden)
        own_lengths = lax.dynamic_slice_in_dim(context, my_inst * slot_count, slot_count)
        partial_value, kv_pool = attend_local(
            hidden, kv_pool, own_lengths, page_table, att_norm, qk_norm, w_q, w_kv, w_o, my_part
        )
        hidden = add_branch(partial_value, hidden)
        outputs.append(hidden.astype(jnp.bfloat16))
        context = context + 1
    return (jnp.stack(outputs), states, kv_pool)


def solution(mesh):
    in_specs = (
        P(None, "inst", None),
        P("inst", "tp", None, None),
        P("inst", None, "tp", None),
        P("inst", None),
        P(),
        P(),
        P(),
        P(),
        P(None, None, "tp"),
        P(None, None, "tp"),
        P(None, None, "tp"),
        P("tp"),
        P("tp"),
        P("tp", None),
        P(),
        P(),
        P(None, "tp"),
        P(),
        P("tp", None),
    )
    out_specs = (P(None, "inst", None), P("inst", "tp", None, None), P("inst", None, "tp", None))
    return jax.shard_map(body, mesh=mesh, in_specs=in_specs, out_specs=out_specs, check_vma=False)
```

profile of v0, /device:TPU:32, one launch (start us, length us, event | category | flops | bytes accessed | tf_op | source)
XLA Modules:
  0.0 1237.5 jit_solution(428659019396718616)
XLA Ops:
  26.4 78.9 %all-gather.25.cloned.1.call-done = f32[32,2,128,128]{3,2,1,0:T(8,128)} async-done(((f32[1,2,128,128]{3,2,1,0:T(8,128)}), f32[32,2,128,128]{3,2,1,0:T(8,128)}) %all-gather.25.cloned.1.call-update) | async-done | bytes 4194320 | tf_op jit(solution)/shard_map/all_gather | solution.py:76
  122.8 73.6 %all-gather.27.cloned.1.call-done = f32[32,2,128,128]{3,2,1,0:T(8,128)} async-done(((f32[1,2,128,128]{3,2,1,0:T(8,128)}), f32[32,2,128,128]{3,2,1,0:T(8,128)}) %all-gather.27.cloned.1.call-update) | async-done | bytes 4194320 | tf_op jit(solution)/shard_map/all_gather | solution.py:76
  214.3 73.1 %all-gather.29.cloned.1.call-done = f32[32,2,128,128]{3,2,1,0:T(8,128)} async-done(((f32[1,2,128,128]{3,2,1,0:T(8,128)}), f32[32,2,128,128]{3,2,1,0:T(8,128)}) %all-gather.29.cloned.1.call-update) | async-done | bytes 4194320 | tf_op jit(solution)/shard_map/all_gather | solution.py:76
  327.2 51.3 %all-gather.31.cloned.1.call-done = f32[32,2,128,128]{3,2,1,0:T(8,128)} async-done(((f32[1,2,128,128]{3,2,1,0:T(8,128)}), f32[32,2,128,128]{3,2,1,0:T(8,128)}) %all-gather.31.cloned.1.call-update) | async-done | bytes 4194320 | tf_op jit(solution)/shard_map/all_gather | solution.py:76
  388.5 69.1 %all-gather.33.cloned.1.call-done = bf16[256,2,8,256]{3,2,1,0:T(8,128)(2,1)} async-done(((bf16[8,2,8,256]{3,2,1,0:T(8,128)(2,1)}), bf16[256,2,8,256]{3,2,1,0:T(8,128)(2,1)}) %all-gather.33.cloned.1.call-update) | async-done | bytes 2097168 | tf_op jit(solution)/shard_map/all_gather | solution.py:77
  464.9 72.6 %all-reduce.7.cloned.1.call-done = (f32[8,2048]{1,0:T(8,128)}, f32[8,2048]{1,0:T(8,128)}, f32[8,2048]{1,0:T(8,128)}, f32[8,2048]{1,0:T(8,128)}) async-done(((f32[8,2048]{1,0:T(8,128)}, f32[8,2048]{1,0:T(8,128)}, f32[8,2048]{1,0:T(8,128)}, f32[8,2048]{1,0:T(8,128)}), (f32[8,2048]{1,0:T(8,128)}, f32[8,2048]{1,0:T(8,128)}, f32[8,2048]{1,0:T(8,128)}, f32[8,2048]{1,0:T(8,128)})) %all-reduce.7.cloned.1.call-update) | async-done | bytes 262160 | tf_op jit(solution)/shard_map/psum | solution.py:54
  543.7 28.1 %all_gather.93 = bf16[8,2048]{1,0:T(8,128)(2,1)S(1)} all-gather(bf16[8,256]{1,0:T(8,128)(2,1)S(1)} %get-tuple-element.1018), channel_id=1, replica_groups=mesh['inst'=32,'tp'=8] {'tp'}, dimensions={1}, use_global_device_ids=true | all-gather | bytes 36864 | tf_op jit(solution)/shard_map/all_gather | solution.py:133
  581.1 24.6 %all-gather.2 = bf16[64,8]{1,0:T(8,128)(2,1)S(1)} all-gather(bf16[8,8]{1,0:T(8,128)(2,1)S(1)} %fusion.89), channel_id=4, replica_groups=mesh['inst'=32,'tp'=8] {'tp'}, dimensions={0}, use_global_device_ids=true | all-gather | bytes 1152 | tf_op jit(solution)/shard_map/all_gather | solution.py:16
  608.7 28.7 %all-gather.3 = bf16[64,8,256]{2,1,0:T(8,128)(2,1)S(1)} all-gather(bf16[8,8,256]{2,1,0:T(8,128)(2,1)S(1)} %convolution_convert_fusion.3), channel_id=5, replica_groups=mesh['inst'=32,'tp'=8] {'tp'}, dimensions={0}, use_global_device_ids=true | all-gather | bytes 294912 | tf_op jit(solution)/shard_map/all_gather | solution.py:16
  639.2 24.6 %all-gather.1 = bf16[64,8]{1,0:T(8,128)(2,1)S(1)} all-gather(bf16[8,8]{1,0:T(8,128)(2,1)S(1)} %convert_element_type.513), channel_id=3, replica_groups=mesh['inst'=32,'tp'=8] {'tp'}, dimensions={0}, use_global_device_ids=true | all-gather | bytes 1152 | tf_op jit(solution)/shard_map/all_gather | solution.py:16
  672.0 28.2 %all_gather.100 = bf16[8,2048]{1,0:T(8,128)(2,1)S(1)} all-gather(bf16[8,256]{1,0:T(8,128)(2,1)} %get-tuple-element.1019), channel_id=1, replica_groups=mesh['inst'=32,'tp'=8] {'tp'}, dimensions={1}, use_global_device_ids=true | all-gather | bytes 36864 | tf_op jit(solution)/shard_map/all_gather | solution.py:133
  700.2 28.2 %all_gather.107 = bf16[8,2048]{1,0:T(8,128)(2,1)S(1)} all-gather(bf16[8,256]{1,0:T(8,128)(2,1)} %get-tuple-element.1020), channel_id=1, replica_groups=mesh['inst'=32,'tp'=8] {'tp'}, dimensions={1}, use_global_device_ids=true | all-gather | bytes 36864 | tf_op jit(solution)/shard_map/all_gather | solution.py:133
  728.4 28.5 %all_gather.114 = bf16[8,2048]{1,0:T(8,128)(2,1)S(1)} all-gather(bf16[8,256]{1,0:T(8,128)(2,1)} %get-tuple-element.1021), channel_id=1, replica_groups=mesh['inst'=32,'tp'=8] {'tp'}, dimensions={1}, use_global_device_ids=true | all-gather | bytes 36864 | tf_op jit(solution)/shard_map/all_gather | solution.py:133
  776.5 24.6 %all-gather.6 = bf16[64,8]{1,0:T(8,128)(2,1)S(1)} all-gather(bf16[8,8]{1,0:T(8,128)(2,1)S(1)} %fusion.91), channel_id=8, replica_groups=mesh['inst'=32,'tp'=8] {'tp'}, dimensions={0}, use_global_device_ids=true | all-gather | bytes 1152 | tf_op jit(solution)/shard_map/all_gather | solution.py:16
  801.1 24.6 %all-gather.5 = bf16[64,8]{1,0:T(8,128)(2,1)S(1)} all-gather(bf16[8,8]{1,0:T(8,128)(2,1)S(1)} %convert_element_type.533), channel_id=7, replica_groups=mesh['inst'=32,'tp'=8] {'tp'}, dimensions={0}, use_global_device_ids=true | all-gather | bytes 1152 | tf_op jit(solution)/shard_map/all_gather | solution.py:16
  828.7 28.7 %all-gather.7 = bf16[64,8,256]{2,1,0:T(8,128)(2,1)S(1)} all-gather(bf16[8,8,256]{2,1,0:T(8,128)(2,1)S(1)} %convolution_convert_fusion.2), channel_id=9, replica_groups=mesh['inst'=32,'tp'=8] {'tp'}, dimensions={0}, use_global_device_ids=true | all-gather | bytes 294912 | tf_op jit(solution)/shard_map/all_gather | solution.py:16
  867.2 39.8 %all-gather.37.cloned.1.call-done = bf16[256,2,8,256]{3,2,1,0:T(8,128)(2,1)} async-done(((bf16[8,2,8,256]{3,2,1,0:T(8,128)(2,1)}), bf16[256,2,8,256]{3,2,1,0:T(8,128)(2,1)}) %all-gather.37.cloned.1.call-update) | async-done | bytes 2097168 | tf_op jit(solution)/shard_map/all_gather | solution.py:77
  925.0 24.7 %all-gather.10 = bf16[64,8]{1,0:T(8,128)(2,1)S(1)} all-gather(bf16[8,8]{1,0:T(8,128)(2,1)S(1)} %fusion.93), channel_id=12, replica_groups=mesh['inst'=32,'tp'=8] {'tp'}, dimensions={0}, use_global_device_ids=true | all-gather | bytes 1152 | tf_op jit(solution)/shard_map/all_gather | solution.py:16
  949.6 24.6 %all-gather.9 = bf16[64,8]{1,0:T(8,128)(2,1)S(1)} all-gather(bf16[8,8]{1,0:T(8,128)(2,1)S(1)} %convert_element_type.553), channel_id=11, replica_groups=mesh['inst'=32,'tp'=8] {'tp'}, dimensions={0}, use_global_device_ids=true | all-gather | bytes 1152 | tf_op jit(solution)/shard_map/all_gather | solution.py:16
  977.3 28.9 %all-gather.11 = bf16[64,8,256]{2,1,0:T(8,128)(2,1)S(1)} all-gather(bf16[8,8,256]{2,1,0:T(8,128)(2,1)S(1)} %convolution_convert_fusion.1), channel_id=13, replica_groups=mesh['inst'=32,'tp'=8] {'tp'}, dimensions={0}, use_global_device_ids=true | all-gather | bytes 294912 | tf_op jit(solution)/shard_map/all_gather | solution.py:16
  1016.0 35.4 %all-gather.39.cloned.1.call-done = bf16[256,2,8,256]{3,2,1,0:T(8,128)(2,1)} async-done(((bf16[8,2,8,256]{3,2,1,0:T(8,128)(2,1)}), bf16[256,2,8,256]{3,2,1,0:T(8,128)(2,1)}) %all-gather.39.cloned.1.call-update) | async-done | bytes 2097168 | tf_op jit(solution)/shard_map/all_gather | solution.py:77
  1067.3 29.1 %all-gather.15 = bf16[64,8,256]{2,1,0:T(8,128)(2,1)S(1)} all-gather(bf16[8,8,256]{2,1,0:T(8,128)(2,1)S(1)} %convolution_convert_fusion), channel_id=17, replica_groups=mesh['inst'=32,'tp'=8] {'tp'}, dimensions={0}, use_global_device_ids=true | all-gather | bytes 294912 | tf_op jit(solution)/shard_map/all_gather | solution.py:16
  1096.4 24.6 %all-gather.14 = bf16[64,8]{1,0:T(8,128)(2,1)S(1)} all-gather(bf16[8,8]{1,0:T(8,128)(2,1)S(1)} %fusion.95), channel_id=16, replica_groups=mesh['inst'=32,'tp'=8] {'tp'}, dimensions={0}, use_global_device_ids=true | all-gather | bytes 1152 | tf_op jit(solution)/shard_map/all_gather | solution.py:16
  1156.1 72.4 %all-reduce.5.cloned.1.call-done = (f32[8,2048]{1,0:T(8,128)}, f32[8,2048]{1,0:T(8,128)}, f32[8,2048]{1,0:T(8,128)}, f32[8,2048]{1,0:T(8,128)}) async-done(((f32[8,2048]{1,0:T(8,128)}, f32[8,2048]{1,0:T(8,128)}, f32[8,2048]{1,0:T(8,128)}, f32[8,2048]{1,0:T(8,128)}), (f32[8,2048]{1,0:T(8,128)}, f32[8,2048]{1,0:T(8,128)}, f32[8,2048]{1,0:T(8,128)}, f32[8,2048]{1,0:T(8,128)})) %all-reduce.5.cloned.1.call-update) | async-done | bytes 262160 | tf_op jit(solution)/shard_map/psum | solution.py:54
  (470 shorter events, 256.5 us)
Async XLA Ops:
  7.3 98.0 %all-gather.25.cloned.1.call-start = ((), (), s32[]{:S(2)}) async-start(), calls=%async_computation | async-start | bytes 4325376 | tf_op jit(solution)/shard_map/all_gather | solution.py:76
  16.3 180.2 %all-gather.27.cloned.1.call-start = ((), (), s32[]{:S(2)}) async-start(), calls=%async_computation.1 | async-start | bytes 4325376 | tf_op jit(solution)/shard_map/all_gather | solution.py:76
  25.0 80.2 %copy-start.11 = (f32[8,2,128,128]{3,2,1,0:T(8,128)S(1)}, f32[8,2,128,128]{3,2,1,0:T(8,128)}, u32[]{:S(2)}) copy-start(f32[8,2,128,128]{3,2,1,0:T(8,128)} %copy.476) | copy-start | bytes 3145732
  112.7 174.6 %all-gather.29.cloned.1.call-start = ((), (), s32[]{:S(2)}) async-start(), calls=%async_computation.2 | async-start | bytes 4325376 | tf_op jit(solution)/shard_map/all_gather | solution.py:76
  203.7 174.8 %all-gather.31.cloned.1.call-start = ((), (), s32[]{:S(2)}) async-start(), calls=%async_computation.3 | async-start | bytes 4325376 | tf_op jit(solution)/shard_map/all_gather | solution.py:76
  294.8 162.8 %all-gather.33.cloned.1.call-start = ((), (), s32[]{:S(2)}) async-start(), calls=%async_computation.4 | async-start | bytes 2162688 | tf_op jit(solution)/shard_map/all_gather | solution.py:77
  296.9 89.4 %copy-start.30 = (s32[8]{0:T(128)}, s32[8]{0:T(128)S(1)}, u32[]{:S(2)}) copy-start(s32[8]{0:T(128)S(1)} %get-tuple-element.1004) | copy-start | bytes 100
  299.9 237.6 %all-reduce.7.cloned.1.call-start = ((), (), s32[]{:S(2)}) async-start(), calls=%async_computation.9 | async-start | bytes 524288 | tf_op jit(solution)/shard_map/psum | solution.py:54
  385.1 154.7 %copy-start.10 = (bf16[2048,256]{1,0:T(8,128)(2,1)S(1)}, bf16[2048,256]{1,0:T(8,128)(2,1)}, u32[]{:S(2)}) copy-start(bf16[2048,256]{1,0:T(8,128)(2,1)} %param.59) | copy-start | bytes 3145732
  386.2 371.6 %all-gather.35.cloned.1.call-start = ((), (), s32[]{:S(2)}) async-start(), calls=%async_computation.5 | async-start | bytes 2162688 | tf_op jit(solution)/shard_map/all_gather | solution.py:77
  580.4 176.5 %copy-start.6 = (bf16[256,2048]{1,0:T(8,128)(2,1)S(1)}, bf16[256,2048]{1,0:T(8,128)(2,1)}, u32[]{:S(2)}) copy-start(bf16[256,2048]{1,0:T(8,128)(2,1)} %param.61) | copy-start | bytes 3145732
  608.6 298.4 %all-gather.37.cloned.1.call-start = ((), (), s32[]{:S(2)}) async-start(), calls=%async_computation.6 | async-start | bytes 2162688 | tf_op jit(solution)/shard_map/all_gather | solution.py:77
  828.6 222.8 %all-gather.39.cloned.1.call-start = ((), (), s32[]{:S(2)}) async-start(), calls=%async_computation.7 | async-start | bytes 2162688 | tf_op jit(solution)/shard_map/all_gather | solution.py:77
  858.0 56.6 %copy-start.25 = (bf16[8,1,256]{2,0,1:T(8,128)(2,1)S(1)}, bf16[8,1,256]{2,0,1:T(8,128)(2,1)}, u32[]{:S(2)}) copy-start(bf16[8,1,256]{2,0,1:T(8,128)(2,1)} %get-tuple-element.1028) | copy-start | bytes 12292
  858.0 56.6 %copy-start.27 = (bf16[8,1,256]{2,0,1:T(8,128)(2,1)S(1)}, bf16[8,1,256]{2,0,1:T(8,128)(2,1)}, u32[]{:S(2)}) copy-start(bf16[8,1,256]{2,0,1:T(8,128)(2,1)} %slice.849) | copy-start | bytes 12292
  858.0 56.6 %copy-start.38 = (pred[8]{0:T(512)(128)(4,1)S(1)}, pred[8]{0:T(512)(128)(4,1)}, u32[]{:S(2)}) copy-start(pred[8]{0:T(512)(128)(4,1)} %get-tuple-element.955) | copy-start | bytes 28
  924.7 128.2 %copy-start.31 = (s32[8]{0:T(128)S(1)}, s32[8]{0:T(128)}, u32[]{:S(2)}) copy-start(s32[8]{0:T(128)} %copy-done.30) | copy-start | bytes 100
  977.2 251.3 %all-reduce.5.cloned.1.call-start = ((), (), s32[]{:S(2)}) async-start(), calls=%async_computation.8 | async-start | bytes 524288 | tf_op jit(solution)/shard_map/psum | solution.py:54
  1006.9 52.0 %copy-start.24 = (bf16[8,1,256]{2,0,1:T(8,128)(2,1)S(1)}, bf16[8,1,256]{2,0,1:T(8,128)(2,1)}, u32[]{:S(2)}) copy-start(bf16[8,1,256]{2,0,1:T(8,128)(2,1)} %get-tuple-element.1026) | copy-start | bytes 12292
  1006.9 52.0 %copy-start.26 = (bf16[8,1,256]{2,0,1:T(8,128)(2,1)S(1)}, bf16[8,1,256]{2,0,1:T(8,128)(2,1)}, u32[]{:S(2)}) copy-start(bf16[8,1,256]{2,0,1:T(8,128)(2,1)} %slice.848) | copy-start | bytes 12292
  1006.9 52.0 %copy-start.37 = (pred[8]{0:T(512)(128)(4,1)S(1)}, pred[8]{0:T(512)(128)(4,1)}, u32[]{:S(2)}) copy-start(pred[8]{0:T(512)(128)(4,1)} %get-tuple-element.951) | copy-start | bytes 28
  1067.3 161.2 %copy-start.19 = (f32[8,2048]{1,0:T(8,128)S(1)}, f32[8,2048]{1,0:T(8,128)}, u32[]{:S(2)}) copy-start(f32[8,2048]{1,0:T(8,128)} %get-tuple-element.931) | copy-start | bytes 196612
  1067.3 161.2 %copy-start.20 = (f32[8,2048]{1,0:T(8,128)S(1)}, f32[8,2048]{1,0:T(8,128)}, u32[]{:S(2)}) copy-start(f32[8,2048]{1,0:T(8,128)} %get-tuple-element.932) | copy-start | bytes 196612
  1096.4 49.1 %copy-start.16 = (bf16[64,8,256]{2,1,0:T(8,128)(2,1)}, bf16[64,8,256]{2,1,0:T(8,128)(2,1)S(1)}, u32[]{:S(2)}) copy-start(bf16[64,8,256]{2,1,0:T(8,128)(2,1)S(1)} %all-gather.15) | copy-start | bytes 786436
  (30 other events, 258.9 us)
Sparse Core Ops, SparseCore 0:
  16.4 88.8 all-gather.24
  112.8 83.5 all-gather.26
  203.8 83.5 all-gather.28
  294.9 83.5 all-gather.30
  381.1 76.4 all-gather.32
  460.8 76.6 all-reduce.6
  608.7 78.3 all-gather.34
  828.7 78.2 all-gather.36
  977.3 74.0 all-gather.38
  1154.3 74.1 all-reduce.4
where the time goes:
time: 1250 us; the launch traced here: 1240 us
  waiting for transfers between devices  566 us (45%)
  blocking collectives  425 us (34%)
  local copies, waits for them, and re-layouts  96.7 us (8%)
  other arithmetic  79.3 us (6%)
  between operations  38.8 us (3%)
  matrix products  30.2 us (2%)
    all_gather x12, blocking collectives, merged(): lax.all_gather(a.astype(kind), axis)  312 us
    all_gather x4, waiting for transfers between devices, migrate_here(): every_state = lax.all_gather(out_state[None], 'inst', axis=0, tiled=True)  277 us
    psum x2, waiting for transfers between devices, add_branch(): return residual + lax.psum(partial_value, 'tp')  145 us
    all_gather x4, waiting for transfers between devices, migrate_here(): every_pages = lax.all_gather(out_pages[None], 'inst', axis=0, tiled=True)  144 us
    all_gather x4, blocking collectives, attend_local(): lax.all_gather(queries, 'tp', axis=1, tiled=True).reshape(row_count, -1, HD)  113 us
  transfers between devices with their start and end apart: 10, of which 9 were waited for; matrix products, arithmetic and copies ran while one was open for 7% of the time, Pallas kernels for 0%

commit v1 on v0

v1 whole, which is shorter than its diff:
```python
import jax
import jax.numpy as jnp
from jax import lax
from jax.experimental import pallas as pl
from jax.experimental.pallas import tpu as pltpu
from jax.sharding import PartitionSpec as P

F32 = jnp.float32
BF16 = jnp.bfloat16
STEPS = 4
SLOTS = 8
INSTS = 32
PARTS = 8
OWN = 32
ROWS = 48
DK = 128
HD = 256
D = 2048

I_LEN = 256
I_TAB = 512
I_ME = 576

T_SLOT = 0
T_FROM = 128
T_ITEM = 256
T_TOK = 384
T_OWN = 640
T_IN = 644
T_NEW = 648
T_RLEN = 656
T_OLEN = 664
T_SIZE = 768

FIRST = (0, 0, 1, 3)

SMEM = pl.BlockSpec(memory_space=pltpu.SMEM)
VMEM = pl.BlockSpec(memory_space=pltpu.VMEM)
PARAMS = pltpu.CompilerParams(vmem_limit_bytes=48 * 1024 * 1024)


def call(kernel, ins, outs, scratch=(), out_specs=None):
    return pl.pallas_call(
        kernel,
        in_specs=list(ins),
        out_specs=[VMEM] * len(outs) if out_specs is None else out_specs,
        out_shape=list(outs),
        scratch_shapes=list(scratch),
        compiler_params=PARAMS,
    )


def rms(values, gain):
    return values * lax.rsqrt(jnp.mean(values * values, axis=-1, keepdims=True) + 1e-06) * gain


def unit(values):
    return values * lax.rsqrt(jnp.sum(values * values, axis=-1, keepdims=True) + 1e-06)


def pack_kernel(ints, state, pages, tokens, out, tab, tok_scr, row_scr):
    def note(i, carry):
        s = lax.shift_right_logical(i, 4)
        a, c, e, f = (ints[i * 4 + n] for n in range(4))
        source, target = a * SLOTS + c, e * SLOTS + f
        tab[T_SLOT + s * INSTS + a] = source
        tab[T_FROM + s * INSTS + a] = -1
        tab[T_SLOT + s * INSTS + e] = target
        tab[T_FROM + s * INSTS + e] = source
        return carry

    lax.fori_loop(0, 64, note, 0)
    me = ints[I_ME]

    def trace(e, s, at_row):
        cur = jnp.maximum(tab[T_FROM + s * INSTS + e], 0)
        hop = jnp.int32(s)
        fresh = {}
        for t in range(s - 1, -1, -1):
            h = lax.shift_right_logical(cur, 3)
            at_row(t, h, hop)
            slot, origin = tab[T_SLOT + t * INSTS + h], tab[T_FROM + t * INSTS + h]
            hit = slot == cur
            fresh[t] = jnp.logical_and(hit, origin < 0)
            moved = jnp.logical_and(hit, origin >= 0)
            cur = jnp.where(moved, origin, cur)
            hop = jnp.where(moved, t, hop)
        return cur, hop, fresh

    def route(e, carry):
        tab[T_TOK + e * 8 + 6] = 0
        tab[T_TOK + e * 8 + 7] = 0
        for s in range(STEPS):

            def at_row(t, h, hop, s=s):
                first = lax.shift_right_logical(hop * (hop - 1), 1)
                tab[T_TOK + e * 8 + FIRST[s] + t] = h * 8 + first + t

            cur, hop, _ = trace(e, s, at_row)
            tab[T_ITEM + e * 4 + s] = lax.shift_right_logical(cur, 3) * 5 + hop
        return carry

    lax.fori_loop(0, INSTS, route, 0)

    held = [ints[I_LEN + me * SLOTS + b] for b in range(SLOTS)]
    for s in range(STEPS):
        slot = tab[T_SLOT + s * INSTS + me] & 7
        moved_in = tab[T_FROM + s * INSTS + me] >= 0
        tab[T_OWN + s] = slot
        tab[T_IN + s] = moved_in.astype(jnp.int32)
        root, _, fresh = trace(me, s, lambda t, h, hop: None)
        length = ints[I_LEN + root]
        for t in range(s):
            length = jnp.where(fresh[t], -t, length)
            tab[T_NEW + FIRST[s] + t] = fresh[t].astype(jnp.int32)
            tab[T_RLEN + FIRST[s] + t] = length + t
        arriving = jnp.where(moved_in, length, -s)
        for b in range(SLOTS):
            held[b] = jnp.where(slot == b, arriving, held[b])
            tab[T_OLEN + s * SLOTS + b] = held[b] + s

    for s in range(STEPS):
        tok_scr[s * 8 : s * 8 + 8, :] = tokens[s].astype(F32)
    row_scr[...] = jnp.zeros_like(row_scr)
    for s in range(STEPS):
        slot = tab[T_OWN + s]
        for t in range(s):
            row_scr[FIRST[s] + t : FIRST[s] + t + 1, :] = tok_scr[pl.ds(t * 8 + slot, 1), :]
    for s in range(STEPS):
        slot = tab[T_OWN + s]
        for i in range(INSTS):
            page = ints[I_TAB + slot * 8 + i // 4]
            half = (i % 2) * 128
            a = state[slot, i // 16, (i % 16) * 8 : (i % 16) * 8 + 8, :]
            b = pages[page, (i // 2) % 2, :, half : half + 128].astype(F32)
            out[i, s] = jnp.concatenate([a, b], axis=0).astype(BF16)
    blank = jnp.zeros((8, 128), F32)
    for i in range(INSTS):
        a = row_scr[:, i * 128 : i * 128 + 128] if i < 16 else blank
        out[i, 4] = jnp.concatenate([a, blank], axis=0).astype(BF16)


def select_kernel(tab, got, out, in_scr, out_scr):
    for h in range(INSTS):
        in_scr[h * 8 : h * 8 + 8, :] = got[h * 5 + 4].astype(F32)[:8]
    out_scr[...] = jnp.zeros_like(out_scr)

    def pick(e, carry):
        for s in range(STEPS):
            out[e * 5 + s] = got[tab[T_ITEM + e * 4 + s]]
        for r in range(6):
            out_scr[pl.ds(e * 16 + r, 1), :] = in_scr[pl.ds(tab[T_TOK + e * 8 + r], 1), :]
        return carry

    lax.fori_loop(0, INSTS, pick, 0)
    for e in range(INSTS):
        out[e * 5 + 4] = out_scr[e * 16 : e * 16 + 16, :].astype(BF16)


def norm_kernel(tokens, got, gain, out, scr):
    for s in range(STEPS):
        scr[s * 8 : s * 8 + 8, :] = tokens[s].astype(F32)
    for i in range(16):
        scr[32:48, i * 128 : i * 128 + 128] = got[i, 4].astype(F32)
    out[...] = rms(scr[...], gain[...].astype(F32)).astype(BF16)


def delta_kernel(tab, qk, vz, ba, a_log, dt_bias, head_gain, w_out, state, got, out, final, o_scr):
    q = unit(qk[0]) * DK ** (-0.5)
    k = unit(qk[1])
    kq = jnp.broadcast_to(jnp.sum(k * q, axis=-1, keepdims=True), (ROWS, 128))
    q_cols, k_cols = q.T, k.T
    rate = jax.nn.sigmoid(ba[0])
    x = ba[1] + dt_bias[...]
    softplus = jnp.maximum(x, 0.0) + jnp.log1p(jnp.exp(-jnp.abs(x)))
    decay = jnp.exp(-jnp.exp(a_log[...]) * softplus)
    rates = [jnp.broadcast_to(rate[:, m : m + 1], (ROWS, 128)) for m in range(2)]
    decays = [jnp.broadcast_to(decay[:, m : m + 1], (ROWS, 128)) for m in range(2)]
    values = [vz[0, :, m * 128 : m * 128 + 128] for m in range(2)]

    def update(held, row, m):
        at = slice(row, row + 1)
        k_col, q_col = k_cols[:, at], q_cols[:, at]
        d = decays[m][at]
        u = rates[m][at] * (values[m][at] - d * jnp.sum(held * k_col, axis=0, keepdims=True))
        o = d * jnp.sum(held * q_col, axis=0, keepdims=True) + kq[at] * u
        o_scr[at, m * 128 : m * 128 + 128] = o
        return held * d + k_col * u

    o_scr[...] = jnp.zeros_like(o_scr)
    final[...] = state[...]
    for s in range(STEPS):
        slot = tab[T_OWN + s]

        @pl.when(tab[T_IN + s] == 0)
        def _():
            final[slot] = jnp.zeros((2, 128, 128), F32)

        @pl.when(tab[T_IN + s] == 1)
        def _():
            for m in range(2):
                held = jnp.concatenate(
                    [got[m * 16 + i, s].astype(F32)[:8] for i in range(16)], axis=0
                )
                for t in range(s):
                    r = FIRST[s] + t
                    held = jnp.where(tab[T_NEW + r] == 1, 0.0, held)
                    held = update(held, OWN + r, m)
                final[slot, m] = held

        for b in range(SLOTS):
            for m in range(2):
                final[b, m] = update(final[b, m], s * SLOTS + b, m)

    y = [
        rms(o_scr[:, m * 128 : m * 128 + 128], head_gain[...].astype(F32))
        * jax.nn.silu(vz[1, :, m * 128 : m * 128 + 128])
        for m in range(2)
    ]
    y = jnp.concatenate(y, axis=1).astype(BF16)
    part = jnp.dot(y, w_out[...], preferred_element_type=F32).astype(BF16)
    for n in range(PARTS):
        out[n] = part


def hidden_kernel(rows, got, gain, w_q, q_gain, hidden, normed, query):
    total = rows[...]
    for n in range(PARTS):
        total = total + got[n].astype(F32)
    hidden[...] = total[:OWN]
    n2 = rms(total, gain[...].astype(F32)).astype(BF16)
    normed[...] = n2
    q = jnp.dot(n2[:OWN], w_q[...], preferred_element_type=F32)
    q = rms(q, q_gain[0:1, :].astype(F32)).astype(BF16)
    for n in range(PARTS):
        query[n] = q


def pages_kernel(ints, tab, pages, got, query, kv, kv_gain, out, final, key, val, new, q_scr, o_scr):
    part = ints[I_ME + 1]
    new[0] = rms(kv[0], kv_gain[1:2, :].astype(F32)).astype(BF16).astype(F32)
    new[1] = kv[1].astype(BF16).astype(F32)
    q_scr[...] = query[...].astype(F32)
    for i in range(64):
        page = ints[I_TAB + i]
        key[i] = pages[page, 0].astype(F32)
        val[i] = pages[page, 1].astype(F32)

    def write(slot, length, row):
        offset = length & 63
        block = slot * 8 + lax.shift_right_logical(length, 6)

        @pl.when(lax.shift_right_logical(offset, 3) == part)
        def _():
            at = pl.ds(offset & 7, 1)
            key[block, at, :] = new[0, row : row + 1, :]
            val[block, at, :] = new[1, row : row + 1, :]

    column = lax.broadcasted_iota(jnp.int32, (1, 512), 1)
    column_slot = lax.shift_right_logical(column, 6)
    position = (lax.shift_right_logical(column, 3) & 7) * 64 + part * 8 + (column & 7)
    row_slot = lax.broadcasted_iota(jnp.int32, (64, 512), 0) & 7
    same = row_slot == lax.broadcasted_iota(jnp.int32, (64, 512), 1) // 64
    lane = lax.broadcasted_iota(jnp.int32, (64, 128), 1)
    for s in range(STEPS):
        slot = tab[T_OWN + s]

        @pl.when(tab[T_IN + s] == 1)
        def _():
            for i in range(INSTS):
                half = (i % 2) * 128
                rows = got[i, s].astype(F32)[8:]
                to = key if (i // 2) % 2 == 0 else val
                to[slot * 8 + i // 4, :, half : half + 128] = rows
            for t in range(s):
                write(slot, tab[T_RLEN + FIRST[s] + t], OWN + FIRST[s] + t)

        lengths = jnp.zeros((1, 512), jnp.int32)
        for b in range(SLOTS):
            length = tab[T_OLEN + s * SLOTS + b]
            write(b, length, s * SLOTS + b)
            lengths = jnp.where(column_slot == b, length, lengths)
        visible = jnp.logical_and(same, position <= lengths)
        q = q_scr[:, s * 8 : s * 8 + 8, :].reshape(64, HD).astype(BF16)
        k = key[...].reshape(512, HD).astype(BF16)
        v = val[...].reshape(512, HD).astype(BF16)
        scores = lax.dot_general(
            q, k, (((1,), (1,)), ((), ())), preferred_element_type=F32
        ) * (float(HD) ** -0.5)
        scores = jnp.where(visible, scores, -1e30)
        top = jnp.max(scores, axis=-1, keepdims=True).astype(BF16).astype(F32)
        weights = jnp.where(visible, jnp.exp(scores - top), 0.0)
        total = jnp.sum(weights, axis=-1, keepdims=True)
        high = total.astype(BF16).astype(F32)
        low = total - high
        mixed = jnp.dot(weights.astype(BF16), v, preferred_element_type=F32)
        stats = jnp.where(lane == 0, top, jnp.where(lane == 1, high, jnp.where(lane == 2, low, 0.0)))
        mixed = jnp.concatenate([mixed, stats], axis=1)
        o_scr[:, s * 8 : s * 8 + 8, :] = mixed.reshape(PARTS, 8, 384)
    out[...] = o_scr[...].astype(BF16)
    for i in range(64):
        page = ints[I_TAB + i]
        final[page, 0] = key[i].astype(BF16)
        final[page, 1] = val[i].astype(BF16)


def merge_kernel(got, w_o, out):
    shares = [got[n].astype(F32) for n in range(PARTS)]
    tops = [x[:, 256:257] for x in shares]
    top = tops[0]
    for x in tops[1:]:
        top = jnp.maximum(top, x)
    total = jnp.zeros((OWN, 1), F32)
    mixed = jnp.zeros((OWN, HD), F32)
    for x, own in zip(shares, tops, strict=True):
        scale = jnp.exp(own - top)
        total = total + (x[:, 257:258] + x[:, 258:259]) * scale
        mixed = mixed + x[:, :256] * scale
    head = (mixed / total).astype(BF16)
    part = jnp.dot(head, w_o[...], preferred_element_type=F32).astype(BF16)
    for n in range(PARTS):
        out[n] = part


def last_kernel(hidden, got, out):
    total = hidden[...]
    for n in range(PARTS):
        total = total + got[n].astype(F32)
    for s in range(STEPS):
        out[s] = total[s * 8 : s * 8 + 8].astype(BF16)


def body(
    step_tokens,
    delta_state,
    kv_pages,
    page_table,
    lengths,
    moves,
    delta_norm,
    head_norm,
    w_qk,
    w_vz,
    w_ba,
    a_log,
    dt_bias,
    w_out,
    att_norm,
    qk_norm,
    w_q,
    w_kv,
    w_o,
):
    shape = jax.ShapeDtypeStruct
    me = jnp.stack([lax.axis_index("inst"), lax.axis_index("tp")]).astype(jnp.int32)
    ints = jnp.concatenate([moves.reshape(-1), lengths, page_table.reshape(-1), me])

    packed, tab = call(
        pack_kernel,
        [SMEM, VMEM, VMEM, VMEM],
        [shape((INSTS, 5, 16, 128), BF16), shape((T_SIZE,), jnp.int32)],
        [pltpu.VMEM((OWN, D), F32), pltpu.VMEM((8, D), F32)],
        [VMEM, SMEM],
    )(ints, delta_state, kv_pages, step_tokens)
    got = lax.all_to_all(packed.reshape(INSTS, 80, 128), "inst", 0, 0)
    (picked,) = call(
        select_kernel,
        [SMEM, VMEM],
        [shape((INSTS * 5, 16, 128), BF16)],
        [pltpu.VMEM((INSTS * 8, 128), F32), pltpu.VMEM((INSTS * 16, 128), F32)],
    )(tab, got.reshape(INSTS * 5, 16, 128))
    got = lax.all_to_all(picked.reshape(INSTS, 80, 128), "inst", 0, 0)
    got = got.reshape(INSTS, 5, 16, 128)

    n1, rows = call(
        norm_kernel,
        [VMEM] * 3,
        [shape((ROWS, D), BF16), shape((ROWS, D), F32)],
    )(step_tokens, got, delta_norm.reshape(1, D))
    qk = jnp.einsum("bd,dtc->tbc", n1, w_qk, preferred_element_type=F32)
    vz = jnp.einsum("bd,dtc->tbc", n1, w_vz, preferred_element_type=F32)
    ba = jnp.einsum("bd,dtc->tbc", n1, w_ba, preferred_element_type=F32)
    part, final_state = call(
        delta_kernel,
        [SMEM] + [VMEM] * 9,
        [shape((PARTS, ROWS, D), BF16), shape(delta_state.shape, F32)],
        [pltpu.VMEM((ROWS, 256), F32)],
    )(
        tab,
        qk,
        vz,
        ba,
        a_log.reshape(1, 2),
        dt_bias.reshape(1, 2),
        head_norm.reshape(1, 128),
        w_out,
        delta_state,
        got,
    )
    parts = lax.all_to_all(part, "tp", 0, 0)
    hidden, n2, query = call(
        hidden_kernel,
        [VMEM] * 5,
        [shape((OWN, D), F32), shape((ROWS, D), BF16), shape((PARTS, OWN, HD), BF16)],
    )(rows, parts, att_norm.reshape(1, D), w_q, qk_norm)
    queries = lax.all_to_all(query, "tp", 0, 0)
    kv = jnp.einsum("bd,dtc->tbc", n2, w_kv, preferred_element_type=F32)
    shares, final_pages = call(
        pages_kernel,
        [SMEM, SMEM] + [VMEM] * 5,
        [shape((PARTS, OWN, 384), BF16), shape(kv_pages.shape, BF16)],
        [
            pltpu.VMEM((64, 8, HD), F32),
            pltpu.VMEM((64, 8, HD), F32),
            pltpu.VMEM((2, ROWS, HD), F32),
            pltpu.VMEM((PARTS, OWN, HD), F32),
            pltpu.VMEM((PARTS, OWN, 384), F32),
        ],
    )(ints, tab, kv_pages, got, queries, kv, qk_norm)
    shares = lax.all_to_all(shares, "tp", 0, 0)
    (part,) = call(merge_kernel, [VMEM] * 2, [shape((PARTS, OWN, D), BF16)])(shares, w_o)
    parts = lax.all_to_all(part, "tp", 0, 0)
    (mixed,) = call(last_kernel, [VMEM] * 2, [shape(step_tokens.shape, BF16)])(hidden, parts)
    return (mixed, final_state, final_pages)


def solution(mesh):
    in_specs = (
        P(None, "inst", None),
        P("inst", "tp", None, None),
        P("inst", None, "tp", None),
        P("inst", None),
        P(),
        P(),
        P(),
        P(),
        P(None, None, "tp"),
        P(None, None, "tp"),
        P(None, None, "tp"),
        P("tp"),
        P("tp"),
        P("tp", None),
        P(),
        P(),
        P(None, "tp"),
        P(),
        P("tp", None),
    )
    out_specs = (P(None, "inst", None), P("inst", "tp", None, None), P("inst", None, "tp", None))
    return jax.shard_map(body, mesh=mesh, in_specs=in_specs, out_specs=out_specs, check_vma=False)
```

time: 1250 us -> 152 us (0.12)
  waiting for transfers between devices: 566 us -> 47.3 us
  blocking collectives: 425 us -> 58 us
  local copies, waits for them, and re-layouts: 96.7 us -> 9.59 us
  other arithmetic: 79.3 us -> 0 us
  between operations: 38.8 us -> 0.86 us
  matrix products: 30.2 us -> 4.6 us
  Pallas kernels: 0 us -> 18.5 us
    all_gather x16 -> x0, blocking collectives: 425 us -> none  [the longest x12 312 us: merged(): lax.all_gather(a.astype(kind), axis)]
    all_gather x8 -> x0, waiting for transfers between devices: 421 us -> none  [the longest x4 277 us: migrate_here(): every_state = lax.all_gather(out_state[None], 'inst', axis=0, tiled=True)]
    psum x2 -> x0, waiting for transfers between devices: 145 us -> none  [add_branch(): return residual + lax.psum(partial_value, 'tp')]
    all_to_all x0 -> x3, blocking collectives: none -> 58 us  [the longest x1 33.2 us: body(): got = lax.all_to_all(packed.reshape(INSTS, 80, 128), 'inst', 0, 0)]
    all_to_all x0 -> x3, waiting for transfers between devices: none -> 47.3 us  [the longest x1 22.1 us: body(): got = lax.all_to_all(picked.reshape(INSTS, 80, 128), 'inst', 0, 0)]
    gather x24 -> x0, local copies, waits for them, and re-layouts: 38.3 us -> none  [the longest x4 12.9 us: attend_local(): context_kv = kv_pool[page_table]]
    scatter x23 -> x0, local copies, waits for them, and re-layouts: 36 us -> none  [the longest x8 17.2 us: migrate_here(): kv_pool.at[target_pages]]
    add x65 -> x0, other arithmetic: 27.8 us -> none  [the longest x28 23.8 us: combine_parts(): first[2] * first_scale[..., None] + second[2] * second_scale[..., None]]
  transfers between devices with their start and end apart: 10 -> 3, of which waited for: 9 -> 3; matrix products, arithmetic and copies ran while one was open for 7% -> 1% of each run, Pallas kernels for 0% -> 0%
where the time goes in v1:
time: 152 us; the launch traced here: 151 us
  blocking collectives  58 us (38%)
  waiting for transfers between devices  47.3 us (31%)
  Pallas kernels  18.5 us (12%)
  starting transfers between devices  12 us (8%)
  local copies, waits for them, and re-layouts  9.59 us (6%)
  matrix products  4.6 us (3%)
    all_to_all x1, blocking collectives, body(): got = lax.all_to_all(packed.reshape(INSTS, 80, 128), 'inst', 0, 0)  33.2 us
    all_to_all x1, waiting for transfers between devices, body(): got = lax.all_to_all(picked.reshape(INSTS, 80, 128), 'inst', 0, 0)  22.1 us
    all_to_all x1, waiting for transfers between devices, body(): parts = lax.all_to_all(part, 'tp', 0, 0)  20.7 us
    all_to_all x1, blocking collectives, body(): parts = lax.all_to_all(part, 'tp', 0, 0)  15.5 us
    all_to_all x1, blocking collectives, body(): shares = lax.all_to_all(shares, 'tp', 0, 0)  9.35 us
    unnamed x43, local copies, waits for them, and re-layouts  7.94 us
    pallas_call x1, Pallas kernels, body(): call(pack_kernel, [SMEM, VMEM, VMEM, VMEM], [shape((INSTS, 5, 16, 128), B...  4.83 us
    all_to_all x1, starting transfers between devices, body(): parts = lax.all_to_all(part, 'tp', 0, 0)  4.63 us
  transfers between devices with their start and end apart: 3, of which 3 were waited for; matrix products, arithmetic and copies ran while one was open for 1% of the time, Pallas kernels for 0%

profile of v1, /device:TPU:32, one launch (start us, length us, event | category | flops | bytes accessed | tf_op | source)
XLA Modules:
  0.0 150.9 jit_solution(15841237019092296701)
XLA Ops:
  0.6 0.9 copy.26
  1.7 0.8 reshape.40
  3.2 1.2 copy-done.1
  4.5 1.0 copy-done.3
  5.5 0.9 copy-done.9
  6.4 4.8 %shard_map.202 = (bf16[32,5,16,128]{3,2,1,0:T(8,128)(2,1)S(1)}, s32[768]{0:T(1024)S(1)}) custom-call(s32[578]{0:T(1024)S(1)} %concatenate.3.ints, f32[8,2,128,128]{3,2,1,0:T(8,128)S(1)} %copy-done.1, bf16[64,2,8,256]{3,2,1,0:T(8,128)(2,1)S(1)} %copy-done.3, bf16[4,8,2048]{2,1,0:T(8,128)(2,1)S(1)} %copy-done.9), custom_call_target="tpu_custom_call" | custom-call | tf_op jit(solution)/shard_map/pallas_call | solution.py:358
  11.3 33.2 %all_to_all.30 = bf16[32,80,128]{2,1,0:T(8,128)(2,1)S(1)} all-to-all(bf16[32,80,128]{2,1,0:T(8,128)(2,1)S(1)} %bitcast.32), channel_id=1, replica_groups=mesh['inst'=32,'tp'=8] {'inst'}, dimensions={0} | all-to-all | bytes 1310720 | tf_op jit(solution)/shard_map/all_to_all | solution.py:365
  44.5 1.9 %shard_map.203 = bf16[160,16,128]{2,1,0:T(8,128)(2,1)} custom-call(s32[768]{0:T(1024)S(1)} %get-tuple-element.14.tab, bf16[160,16,128]{2,1,0:T(8,128)(2,1)S(1)} %bitcast.31), custom_call_target="tpu_custom_call" | custom-call | tf_op jit(solution)/shard_map/pallas_call | solution.py:366
  46.4 4.0 %all-to-all-start.1 = ((bf16[32,80,128]{2,1,0:T(8,128)(2,1)}), bf16[32,80,128]{2,1,0:T(8,128)(2,1)S(1)}, u32[]{:S(2)}, u32[]{:S(2)}) async-start(bf16[32,80,128]{2,1,0:T(8,128)(2,1)} %bitcast.4), calls=%async_computation.1 | async-start | bytes 1310720 | tf_op jit(solution)/shard_map/all_to_all | solution.py:372
  50.4 22.1 %all-to-all-done.1 = bf16[32,80,128]{2,1,0:T(8,128)(2,1)S(1)} async-done(((bf16[32,80,128]{2,1,0:T(8,128)(2,1)}), bf16[32,80,128]{2,1,0:T(8,128)(2,1)S(1)}, u32[]{:S(2)}, u32[]{:S(2)}) %all-to-all-start.1) | async-done | bytes 655392 | tf_op jit(solution)/shard_map/all_to_all | solution.py:372
  72.8 1.7 %convolution_bitcast_fusion.1.qk = f32[2,48,128]{2,1,0:T(8,128)S(1)} fusion(bf16[2048,2,128]{2,1,0:T(2,128)(2,1)} %param.27, bf16[48,2048]{1,0:T(8,128)(2,1)S(1)} %get-tuple-element.17), kind=kOutput, calls=%fused_computation.7 | convolution fusion | flops 50331648 | bytes 1294336 | tf_op jit(solution)/shard_map/bd,dtc->tbc/dot_general | solution.py:380
  75.3 4.1 %shard_map.205 = (bf16[8,48,2048]{2,1,0:T(8,128)(2,1)S(1)}, f32[8,2,128,128]{3,2,1,0:T(8,128)}) custom-call(s32[768]{0:T(1024)S(1)} %get-tuple-element.14.tab, f32[2,48,128]{2,1,0:T(8,128)S(1)} %convolution_bitcast_fusion.1.qk, f32[2,48,256]{2,1,0:T(8,128)S(1)} %fusion.4.vz, f32[2,48,2]{2,1,0:T(8,128)S(1)} %convolution_bitcast_fusion.ba, ...), custom_call_target="tpu_custom_call" | custom-call | tf_op jit(solution)/shard_map/pallas_call | solution.py:383
  79.4 1.1 copy-done.5
  80.6 4.6 %all-to-all-start.2 = ((bf16[8,48,2048]{2,1,0:T(8,128)(2,1)}), bf16[8,48,2048]{2,1,0:T(8,128)(2,1)}, u32[]{:S(2)}, u32[]{:S(2)}) async-start(bf16[8,48,2048]{2,1,0:T(8,128)(2,1)} %copy-done.5), calls=%async_computation.2 | async-start | bytes 3145728 | tf_op jit(solution)/shard_map/all_to_all | solution.py:400
  85.2 20.7 %all-to-all-done.2.got = bf16[8,48,2048]{2,1,0:T(8,128)(2,1)} async-done(((bf16[8,48,2048]{2,1,0:T(8,128)(2,1)}), bf16[8,48,2048]{2,1,0:T(8,128)(2,1)}, u32[]{:S(2)}, u32[]{:S(2)}) %all-to-all-start.2) | async-done | bytes 1572896 | tf_op jit(solution)/shard_map/all_to_all | solution.py:400
  106.0 1.2 copy-done.7
  107.2 2.6 %shard_map.206 = (f32[32,2048]{1,0:T(8,128)S(1)}, bf16[48,2048]{1,0:T(8,128)(2,1)S(1)}, bf16[8,32,256]{2,1,0:T(8,128)(2,1)}) custom-call(f32[48,2048]{1,0:T(8,128)S(1)} %get-tuple-element.16.rows, bf16[8,48,2048]{2,1,0:T(8,128)(2,1)} %all-to-all-done.2.got, bf16[1,2048]{1,0:T(2,128)(2,1)S(1)} %reshape.49.gain, bf16[2048,256]{1,0:T(8,128)(2,1)S(1)} %copy-done.7, ...), custom_call_target="tpu_custom_call" | custom-call | tf_op jit(solution)/shard_map/pallas_call | solution.py:401
  111.2 3.4 %all-to-all-start.3 = ((bf16[8,32,256]{2,1,0:T(8,128)(2,1)}), bf16[8,32,256]{2,1,0:T(8,128)(2,1)S(1)}, u32[]{:S(2)}, u32[]{:S(2)}) async-start(bf16[8,32,256]{2,1,0:T(8,128)(2,1)} %get-tuple-element.20), calls=%async_computation.3 | async-start | bytes 262144 | tf_op jit(solution)/shard_map/all_to_all | solution.py:406
  114.6 2.2 %fusion.7.kv = f32[2,48,256]{2,1,0:T(8,128)S(1)} fusion(bf16[2048,2,256]{2,1,0:T(2,128)(2,1)} %param.36, bf16[48,2048]{1,0:T(8,128)(2,1)} %copy-done.17), kind=kOutput, calls=%fused_computation.5 | convolution fusion | flops 100663296 | bytes 2392064 | tf_op jit(solution)/shard_map/bd,dtc->tbc/dot_general | solution.py:407
  116.7 4.4 %all-to-all-done.3.query = bf16[8,32,256]{2,1,0:T(8,128)(2,1)S(1)} async-done(((bf16[8,32,256]{2,1,0:T(8,128)(2,1)}), bf16[8,32,256]{2,1,0:T(8,128)(2,1)S(1)}, u32[]{:S(2)}, u32[]{:S(2)}) %all-to-all-start.3) | async-done | bytes 131104 | tf_op jit(solution)/shard_map/all_to_all | solution.py:406
  121.2 3.6 %shard_map.207 = (bf16[8,32,384]{2,1,0:T(8,128)(2,1)S(1)}, bf16[64,2,8,256]{3,2,1,0:T(8,128)(2,1)}) custom-call(s32[578]{0:T(1024)S(1)} %concatenate.3.ints, s32[768]{0:T(1024)S(1)} %get-tuple-element.14.tab, bf16[64,2,8,256]{3,2,1,0:T(8,128)(2,1)S(1)} %copy-done.4, bf16[32,5,16,128]{3,2,1,0:T(8,128)(2,1)S(1)} %bitcast.30, ...), custom_call_target="tpu_custom_call" | custom-call | tf_op jit(solution)/shard_map/pallas_call | solution.py:408
  124.8 9.3 %all_to_all.31.got = bf16[8,32,384]{2,1,0:T(8,128)(2,1)S(1)} all-to-all(bf16[8,32,384]{2,1,0:T(8,128)(2,1)S(1)} %get-tuple-element.22), channel_id=1, replica_groups=mesh['inst'=32,'tp'=8] {'tp'}, dimensions={0} | all-to-all | bytes 393216 | tf_op jit(solution)/shard_map/all_to_all | solution.py:420
  134.6 15.5 %all_to_all.32.got = bf16[8,32,2048]{2,1,0:T(8,128)(2,1)S(1)} all-to-all(bf16[8,32,2048]{2,1,0:T(8,128)(2,1)S(1)} %shard_map.208), channel_id=1, replica_groups=mesh['inst'=32,'tp'=8] {'tp'}, dimensions={0} | all-to-all | bytes 2097152 | tf_op jit(solution)/shard_map/all_to_all | solution.py:422
  150.1 0.8 shard_map.209
  (45 shorter events, 3.7 us)
Async XLA Ops:
  0.6 73.8 %copy-start = (bf16[2048,2,256]{2,1,0:T(2,128)(2,1)S(1)}, bf16[2048,2,256]{2,1,0:T(2,128)(2,1)}, u32[]{:S(2)}) copy-start(bf16[2048,2,256]{2,1,0:T(2,128)(2,1)} %param.28) | copy-start | bytes 6291460
  3.2 1.2 copy-start.1
  4.4 1.0 copy-start.3
  5.5 0.9 copy-start.9
  11.2 39.1 %copy-start.18 = (bf16[2048]{0:T(1024)(128)(2,1)S(1)}, bf16[2048]{0:T(1024)(128)(2,1)}, u32[]{:S(2)}) copy-start(bf16[2048]{0:T(1024)(128)(2,1)} %param.25) | copy-start | bytes 12292
  11.2 61.3 %copy-start.10 = (bf16[4,8,2048]{2,1,0:T(8,128)(2,1)S(1)}, bf16[4,8,2048]{2,1,0:T(8,128)(2,1)}, u32[]{:S(2)}) copy-start(bf16[4,8,2048]{2,1,0:T(8,128)(2,1)} %tokens.3) | copy-start | bytes 393220
  46.4 26.2 %all-to-all-start.1 = ((bf16[32,80,128]{2,1,0:T(8,128)(2,1)}), bf16[32,80,128]{2,1,0:T(8,128)(2,1)S(1)}, u32[]{:S(2)}, u32[]{:S(2)}) async-start(bf16[32,80,128]{2,1,0:T(8,128)(2,1)} %bitcast.4), calls=%async_computation.1 | async-start | bytes 1310720 | tf_op jit(solution)/shard_map/all_to_all | solution.py:372
  72.6 2.4 %copy-start.20 = (bf16[2048,2,2]{0,2,1:T(2,128)(2,1)S(1)}, bf16[2048,2,2]{0,2,1:T(2,128)(2,1)}, u32[]{:S(2)}) copy-start(bf16[2048,2,2]{0,2,1:T(2,128)(2,1)} %param.29) | copy-start | bytes 49156
  72.7 2.5 %copy-start.2 = (f32[8,2,128,128]{3,2,1,0:T(8,128)S(1)}, f32[8,2,128,128]{3,2,1,0:T(8,128)}, u32[]{:S(2)}) copy-start(f32[8,2,128,128]{3,2,1,0:T(8,128)} %state.3) | copy-start | bytes 3145732
  72.7 2.5 %copy-start.6 = (bf16[256,2048]{1,0:T(8,128)(2,1)S(1)}, bf16[256,2048]{1,0:T(8,128)(2,1)}, u32[]{:S(2)}) copy-start(bf16[256,2048]{1,0:T(8,128)(2,1)} %w_out.1) | copy-start | bytes 3145732
  72.7 2.5 %copy-start.14 = (f32[2]{0:T(128)S(1)}, f32[2]{0:T(128)}, u32[]{:S(2)}) copy-start(f32[2]{0:T(128)} %param.30) | copy-start | bytes 28
  72.8 2.5 %copy-start.15 = (f32[2]{0:T(128)S(1)}, f32[2]{0:T(128)}, u32[]{:S(2)}) copy-start(f32[2]{0:T(128)} %param.31) | copy-start | bytes 28
  72.8 2.5 %copy-start.16 = (bf16[128]{0:T(256)(128)(2,1)S(1)}, bf16[128]{0:T(256)(128)(2,1)}, u32[]{:S(2)}) copy-start(bf16[128]{0:T(256)(128)(2,1)} %param.26) | copy-start | bytes 772
  79.4 1.1 copy-start.5
  80.6 4.6 %copy-start.19 = (bf16[2048]{0:T(1024)(128)(2,1)S(1)}, bf16[2048]{0:T(1024)(128)(2,1)}, u32[]{:S(2)}) copy-start(bf16[2048]{0:T(1024)(128)(2,1)} %param.33) | copy-start | bytes 12292
  80.6 25.4 %copy-start.13 = (bf16[2,256]{1,0:T(2,128)(2,1)S(1)}, bf16[2,256]{1,0:T(2,128)(2,1)}, u32[]{:S(2)}) copy-start(bf16[2,256]{1,0:T(2,128)(2,1)} %kv_gain.1) | copy-start | bytes 3076
  80.6 25.3 %all-to-all-start.2 = ((bf16[8,48,2048]{2,1,0:T(8,128)(2,1)}), bf16[8,48,2048]{2,1,0:T(8,128)(2,1)}, u32[]{:S(2)}, u32[]{:S(2)}) async-start(bf16[8,48,2048]{2,1,0:T(8,128)(2,1)} %copy-done.5), calls=%async_computation.2 | async-start | bytes 3145728 | tf_op jit(solution)/shard_map/all_to_all | solution.py:400
  105.9 1.2 copy-start.7
  109.8 0.7 copy-start.11
  110.5 0.7 copy-start.17
  110.5 10.7 %copy-start.4 = (bf16[64,2,8,256]{3,2,1,0:T(8,128)(2,1)S(1)}, bf16[64,2,8,256]{3,2,1,0:T(8,128)(2,1)}, u32[]{:S(2)}) copy-start(bf16[64,2,8,256]{3,2,1,0:T(8,128)(2,1)} %pages.3) | copy-start | bytes 1572868
  111.2 10.0 %all-to-all-start.3 = ((bf16[8,32,256]{2,1,0:T(8,128)(2,1)}), bf16[8,32,256]{2,1,0:T(8,128)(2,1)S(1)}, u32[]{:S(2)}, u32[]{:S(2)}) async-start(bf16[8,32,256]{2,1,0:T(8,128)(2,1)} %get-tuple-element.20), calls=%async_computation.3 | async-start | bytes 262144 | tf_op jit(solution)/shard_map/all_to_all | solution.py:406
  121.2 13.0 %copy-start.8 = (bf16[256,2048]{1,0:T(8,128)(2,1)S(1)}, bf16[256,2048]{1,0:T(8,128)(2,1)}, u32[]{:S(2)}) copy-start(bf16[256,2048]{1,0:T(8,128)(2,1)} %w_o.1) | copy-start | bytes 3145732
  134.1 15.9 %copy-start.12 = (f32[32,2048]{1,0:T(8,128)S(1)}, f32[32,2048]{1,0:T(8,128)}, u32[]{:S(2)}) copy-start(f32[32,2048]{1,0:T(8,128)} %copy-done.11) | copy-start | bytes 786436

commit v2 on v1

v2 whole, which is shorter than its diff:
```python
import jax
import jax.numpy as jnp
from jax import lax
from jax.experimental import pallas as pl
from jax.experimental.pallas import tpu as pltpu
from jax.sharding import PartitionSpec as P

F32 = jnp.float32
BF16 = jnp.bfloat16
STEPS = 4
SLOTS = 8
INSTS = 32
PARTS = 8
OWN = 32
ROWS = 48
EXTRA = 16
PIECE = 72
DK = 128
HD = 256
D = 2048

T_SLOT = 0
T_FROM = 128
T_ITEM = 256
T_TOK = 384
T_OWN = 640
T_IN = 644
T_NEW = 648
T_RLEN = 656
T_OLEN = 664
T_SIZE = 768

FIRST = (0, 0, 1, 3)
LATE = (6, 10, 13, 15)

SMEM = pl.BlockSpec(memory_space=pltpu.SMEM)
VMEM = pl.BlockSpec(memory_space=pltpu.VMEM)
HBM = pl.BlockSpec(memory_space=pltpu.HBM)
ANY = pl.BlockSpec(memory_space=pl.ANY)
PARAMS = pltpu.CompilerParams(vmem_limit_bytes=48 * 1024 * 1024)


def call(kernel, ins, outs, scratch=(), out_specs=None):
    return pl.pallas_call(
        kernel,
        in_specs=list(ins),
        out_specs=[VMEM] * len(outs) if out_specs is None else out_specs,
        out_shape=list(outs),
        scratch_shapes=list(scratch),
        compiler_params=PARAMS,
    )


def rms(values, gain):
    return values * lax.rsqrt(jnp.mean(values * values, axis=-1, keepdims=True) + 1e-06) * gain


def unit(values):
    return values * lax.rsqrt(jnp.sum(values * values, axis=-1, keepdims=True) + 1e-06)


def own_slots(moves, me):
    slots = []
    for s in range(STEPS):
        slot = jnp.int32(0)
        for p in range(16):
            slot = jnp.where(moves[s, 0, p] == me, moves[s, 1, p], slot)
            slot = jnp.where(moves[s, 2, p] == me, moves[s, 3, p], slot)
        slots.append(slot)
    return slots


def pack_kernel(
    moves, place, table, state, pages, tokens, out, st_scr, pg_scr, bf_scr, tok_scr, row_scr, sem
):
    slots = own_slots(moves, place[0])
    token_copy = pltpu.make_async_copy(tokens, bf_scr, sem.at[36])
    token_copy.start()
    copies = []
    for s in range(STEPS):
        copies.append(pltpu.make_async_copy(state.at[slots[s]], st_scr.at[s], sem.at[32 + s]))
        for j in range(8):
            at = s * 8 + j
            copies.append(
                pltpu.make_async_copy(pages.at[table[slots[s], j]], pg_scr.at[at], sem.at[at])
            )
    for copy in copies:
        copy.start()
    token_copy.wait()
    for s in range(STEPS):
        tok_scr[s * 8 : s * 8 + 8, :] = bf_scr[s].astype(F32)
    row_scr[...] = jnp.zeros_like(row_scr)
    for s in range(STEPS):
        for t in range(s):
            row_scr[FIRST[s] + t : FIRST[s] + t + 1, :] = tok_scr[pl.ds(t * 8 + slots[s], 1), :]
    for copy in copies:
        copy.wait()
    blank = jnp.zeros((8, 128), F32)
    for i in range(INSTS):
        at, half = (i % 16) * 8, (i % 2) * 128
        tiles = [st_scr[s, i // 16, at : at + 8, :] for s in range(STEPS)]
        for s in range(STEPS):
            page = pg_scr[s * 8 + i // 4, (i // 2) % 2].astype(F32)
            tiles.append(page[:, half : half + 128])
        tiles.append(row_scr[:, i * 128 : i * 128 + 128] if i < 16 else blank)
        out[i] = jnp.concatenate(tiles, axis=0).astype(BF16)


def table_kernel(moves, place, lens, tab):
    for s in range(STEPS):
        for p in range(16):
            a, c, e, f = (moves[s, n, p] for n in range(4))
            source, target = a * SLOTS + c, e * SLOTS + f
            tab[T_SLOT + s * INSTS + a] = source
            tab[T_FROM + s * INSTS + a] = -1
            tab[T_SLOT + s * INSTS + e] = target
            tab[T_FROM + s * INSTS + e] = source
    me = place[0]

    def trace(e, s, at_row):
        cur = jnp.maximum(tab[T_FROM + s * INSTS + e], 0)
        hop = jnp.int32(s)
        fresh = {}
        for t in range(s - 1, -1, -1):
            h = lax.shift_right_logical(cur, 3)
            at_row(t, h, hop)
            slot, origin = tab[T_SLOT + t * INSTS + h], tab[T_FROM + t * INSTS + h]
            hit = slot == cur
            fresh[t] = jnp.logical_and(hit, origin < 0)
            moved = jnp.logical_and(hit, origin >= 0)
            cur = jnp.where(moved, origin, cur)
            hop = jnp.where(moved, t, hop)
        return cur, hop, fresh

    def route(e, carry):
        for s in range(STEPS):

            def at_row(t, h, hop, s=s):
                first = lax.shift_right_logical(hop * (hop - 1), 1)
                tab[T_TOK + e * 8 + FIRST[s] + t] = h * PIECE + 64 + first + t

            cur, hop, _ = trace(e, s, at_row)
            tab[T_ITEM + e * 4 + s] = lax.shift_right_logical(cur, 3) * PIECE + hop * 8
        return carry

    lax.fori_loop(0, INSTS, route, 0)

    held = [lens[me * SLOTS + b] for b in range(SLOTS)]
    for s in range(STEPS):
        slot = tab[T_SLOT + s * INSTS + me] & 7
        moved_in = tab[T_FROM + s * INSTS + me] >= 0
        tab[T_OWN + s] = slot
        tab[T_IN + s] = moved_in.astype(jnp.int32)
        root, _, fresh = trace(me, s, lambda t, h, hop: None)
        length = lens[root]
        for t in range(s):
            length = jnp.where(fresh[t], -t, length)
            tab[T_NEW + FIRST[s] + t] = fresh[t].astype(jnp.int32)
            tab[T_RLEN + FIRST[s] + t] = length + t
        arriving = jnp.where(moved_in, length, -s)
        for b in range(SLOTS):
            held[b] = jnp.where(slot == b, arriving, held[b])
            tab[T_OLEN + s * SLOTS + b] = held[b] + s


def select_kernel(tab, got, early, out, in_scr, out_scr):
    for h in range(INSTS):
        in_scr[h * PIECE : (h + 1) * PIECE, :] = got[h].astype(F32)
    for e in range(INSTS):
        out_scr[e * PIECE + 64 : (e + 1) * PIECE, :] = jnp.zeros((8, 128), F32)

    def pick(e, carry):
        base = e * PIECE
        for s in range(STEPS):
            item = tab[T_ITEM + e * 4 + s]
            for n in (0, 32):
                at = pl.ds(pl.multiple_of(item + n, 8), 8)
                to = pl.ds(pl.multiple_of(base + (s * 8 + n), 8), 8)
                out_scr[to, :] = in_scr[at, :]
        for r in range(6):
            out_scr[pl.ds(base + (64 + r), 1), :] = in_scr[pl.ds(tab[T_TOK + e * 8 + r], 1), :]
        return carry

    lax.fori_loop(0, INSTS, pick, 0, unroll=4)
    for e in range(INSTS):
        out[e] = out_scr[e * PIECE : (e + 1) * PIECE, :].astype(BF16)


def norm_kernel(tokens, gain, out, scr):
    for s in range(STEPS):
        scr[s * 8 : s * 8 + 8, :] = tokens[s].astype(F32)
    out[...] = rms(scr[...], gain[...].astype(F32)).astype(BF16)


def late_norm_kernel(got, gain, out, rows):
    rows[...] = jnp.zeros_like(rows)
    for i in range(16):
        rows[0:8, i * 128 : i * 128 + 128] = got[i].astype(F32)[64:]
    out[...] = rms(rows[...], gain[...].astype(F32)).astype(BF16)


def updater(qk, vz, ba, a_log, dt_bias, o_scr):
    rows = qk.shape[1]
    q = unit(qk[0]) * DK ** (-0.5)
    k = unit(qk[1])
    kq = jnp.broadcast_to(jnp.sum(k * q, axis=-1, keepdims=True), (rows, 128))
    q_cols, k_cols = q.T, k.T
    rate = jax.nn.sigmoid(ba[0])
    x = ba[1] + dt_bias[...]
    softplus = jnp.maximum(x, 0.0) + jnp.log1p(jnp.exp(-jnp.abs(x)))
    decay = jnp.exp(-jnp.exp(a_log[...]) * softplus)
    rates = [jnp.broadcast_to(rate[:, m : m + 1], (rows, 128)) for m in range(2)]
    decays = [jnp.broadcast_to(decay[:, m : m + 1], (rows, 128)) for m in range(2)]
    values = [vz[0, :, m * 128 : m * 128 + 128] for m in range(2)]

    def update(held, row, m):
        at = slice(row, row + 1)
        k_col, q_col = k_cols[:, at], q_cols[:, at]
        d = decays[m][at]
        u = rates[m][at] * (values[m][at] - d * jnp.sum(held * k_col, axis=0, keepdims=True))
        o = d * jnp.sum(held * q_col, axis=0, keepdims=True) + kq[at] * u
        o_scr[at, m * 128 : m * 128 + 128] = o
        return held * d + k_col * u

    return update


def gated(o_scr, z, gain, w_out):
    y = [
        rms(o_scr[:, m * 128 : m * 128 + 128], gain[...].astype(F32))
        * jax.nn.silu(z[:, m * 128 : m * 128 + 128])
        for m in range(2)
    ]
    y = jnp.concatenate(y, axis=1).astype(BF16)
    return jnp.dot(y, w_out[...], preferred_element_type=F32).astype(BF16)


def early_kernel(tab, qk, vz, ba, a_log, dt_bias, head_gain, w_out, state, out, final, o_scr):
    update = updater(qk, vz, ba, a_log, dt_bias, o_scr)
    final[...] = state[...]
    for s in range(STEPS):
        slot = tab[T_OWN + s]

        @pl.when(tab[T_IN + s] == 0)
        def _():
            final[slot] = jnp.zeros((2, 128, 128), F32)

        for b in range(SLOTS):
            for m in range(2):
                final[b, m] = update(final[b, m], s * SLOTS + b, m)
    out[...] = gated(o_scr, vz[1], head_gain, w_out)


def late_kernel(
    tab,
    qk,
    vz,
    ba,
    qk_in,
    vz_in,
    ba_in,
    a_log,
    dt_bias,
    head_gain,
    w_out,
    got,
    out,
    states,
    qk_scr,
    vz_scr,
    ba_scr,
    o_scr,
):
    for scr, new, old in ((qk_scr, qk_in, qk), (vz_scr, vz_in, vz), (ba_scr, ba_in, ba)):
        for n in range(2):
            scr[n, 0:8, :] = new[n, 0:8, :]
            for s in range(STEPS):
                for t in range(s, STEPS):
                    row = LATE[s] + t - s
                    scr[n, row : row + 1, :] = old[n, pl.ds(t * 8 + tab[T_OWN + s], 1), :]
    update = updater(qk_scr, vz_scr, ba_scr, a_log, dt_bias, o_scr)
    o_scr[...] = jnp.zeros_like(o_scr)
    for s in range(STEPS):
        slot = tab[T_OWN + s]

        @pl.when(tab[T_IN + s] == 1)
        def _():
            for m in range(2):
                held = jnp.concatenate(
                    [got[m * 16 + i].astype(F32)[s * 8 : s * 8 + 8] for i in range(16)], axis=0
                )
                for t in range(s):
                    r = FIRST[s] + t
                    held = jnp.where(tab[T_NEW + r] == 1, 0.0, held)
                    held = update(held, r, m)
                for t in range(s, STEPS):
                    if t > s:
                        leaves = jnp.logical_and(tab[T_OWN + t] == slot, tab[T_IN + t] == 0)
                        held = jnp.where(leaves, 0.0, held)
                    held = update(held, LATE[s] + t - s, m)
                states[s, m] = held

    part = gated(o_scr, vz_scr[1], head_gain, w_out)
    for n in range(PARTS):
        out[n] = part


def states_kernel(tab, early, late, final):
    final[...] = early[...]
    for s in range(STEPS):

        @pl.when(tab[T_IN + s] == 1)
        def _():
            final[tab[T_OWN + s]] = late[s]


def hidden_kernel(
    tab, tokens, early, rows, got, gain, w_q, q_gain, hidden, normed, query, all_scr, tok_scr, late
):
    total = got[0].astype(F32)
    for n in range(1, PARTS):
        total = total + got[n].astype(F32)
    late[...] = total
    for s in range(STEPS):
        at = slice(s * 8, s * 8 + 8)
        tok_scr[at, :] = tokens[s].astype(F32)
        all_scr[at, :] = tok_scr[at, :] + early[at, :]
    all_scr[OWN:, :] = rows[...] + total
    for s in range(STEPS):

        @pl.when(tab[T_IN + s] == 1)
        def _():
            for t in range(s, STEPS):
                at = pl.ds(t * 8 + tab[T_OWN + s], 1)
                row = LATE[s] + t - s
                all_scr[at, :] = tok_scr[at, :] + late[row : row + 1, :]

    total = all_scr[...]
    hidden[...] = total[:OWN]
    n2 = rms(total, gain[...].astype(F32)).astype(BF16)
    normed[...] = n2
    q = jnp.dot(n2[:OWN], w_q[...], preferred_element_type=F32)
    q = rms(q, q_gain[0:1, :].astype(F32)).astype(BF16)
    for n in range(PARTS):
        query[n] = q


def pages_kernel(place, table, tab, pages, got, query, kv, kv_gain, out, final, key, val, new, q_scr, o_scr):
    part = place[1]
    new[0] = rms(kv[0], kv_gain[1:2, :].astype(F32)).astype(BF16).astype(F32)
    new[1] = kv[1].astype(BF16).astype(F32)
    q_scr[...] = query[...].astype(F32)
    for i in range(64):
        page = table[i // 8, i % 8]
        key[i] = pages[page, 0].astype(F32)
        val[i] = pages[page, 1].astype(F32)

    def write(slot, length, row):
        offset = length & 63
        block = slot * 8 + lax.shift_right_logical(length, 6)

        @pl.when(lax.shift_right_logical(offset, 3) == part)
        def _():
            at = pl.ds(offset & 7, 1)
            key[block, at, :] = new[0, row : row + 1, :]
            val[block, at, :] = new[1, row : row + 1, :]

    column = lax.broadcasted_iota(jnp.int32, (1, 512), 1)
    column_slot = lax.shift_right_logical(column, 6)
    position = (lax.shift_right_logical(column, 3) & 7) * 64 + part * 8 + (column & 7)
    row_slot = lax.broadcasted_iota(jnp.int32, (64, 512), 0) & 7
    same = row_slot == lax.broadcasted_iota(jnp.int32, (64, 512), 1) // 64
    lane = lax.broadcasted_iota(jnp.int32, (64, 128), 1)
    for s in range(STEPS):
        slot = tab[T_OWN + s]

        @pl.when(tab[T_IN + s] == 1)
        def _():
            for i in range(INSTS):
                half = (i % 2) * 128
                rows = got[i].astype(F32)[32 + s * 8 : 40 + s * 8]
                to = key if (i // 2) % 2 == 0 else val
                to[slot * 8 + i // 4, :, half : half + 128] = rows
            for t in range(s):
                write(slot, tab[T_RLEN + FIRST[s] + t], OWN + FIRST[s] + t)

        lengths = jnp.zeros((1, 512), jnp.int32)
        for b in range(SLOTS):
            length = tab[T_OLEN + s * SLOTS + b]
            write(b, length, s * SLOTS + b)
            lengths = jnp.where(column_slot == b, length, lengths)
        visible = jnp.logical_and(same, position <= lengths)
        q = q_scr[:, s * 8 : s * 8 + 8, :].reshape(64, HD).astype(BF16)
        k = key[...].reshape(512, HD).astype(BF16)
        v = val[...].reshape(512, HD).astype(BF16)
        scores = lax.dot_general(
            q, k, (((1,), (1,)), ((), ())), preferred_element_type=F32
        ) * (float(HD) ** -0.5)
        scores = jnp.where(visible, scores, -1e30)
        top = jnp.max(scores, axis=-1, keepdims=True).astype(BF16).astype(F32)
        weights = jnp.where(visible, jnp.exp(scores - top), 0.0)
        total = jnp.sum(weights, axis=-1, keepdims=True)
        high = total.astype(BF16).astype(F32)
        low = total - high
        mixed = jnp.dot(weights.astype(BF16), v, preferred_element_type=F32)
        stats = jnp.where(lane == 0, top, jnp.where(lane == 1, high, jnp.where(lane == 2, low, 0.0)))
        mixed = jnp.concatenate([mixed, stats], axis=1)
        o_scr[:, s * 8 : s * 8 + 8, :] = mixed.reshape(PARTS, 8, 384)
    out[...] = o_scr[...].astype(BF16)
    for i in range(64):
        page = table[i // 8, i % 8]
        final[page, 0] = key[i].astype(BF16)
        final[page, 1] = val[i].astype(BF16)


def merge_kernel(got, w_o, out):
    shares = [got[n].astype(F32) for n in range(PARTS)]
    tops = [x[:, 256:257] for x in shares]
    top = tops[0]
    for x in tops[1:]:
        top = jnp.maximum(top, x)
    total = jnp.zeros((OWN, 1), F32)
    mixed = jnp.zeros((OWN, HD), F32)
    for x, own in zip(shares, tops, strict=True):
        scale = jnp.exp(own - top)
        total = total + (x[:, 257:258] + x[:, 258:259]) * scale
        mixed = mixed + x[:, :256] * scale
    head = (mixed / total).astype(BF16)
    part = jnp.dot(head, w_o[...], preferred_element_type=F32).astype(BF16)
    for n in range(PARTS):
        out[n] = part


def last_kernel(hidden, got, out):
    total = hidden[...]
    for n in range(PARTS):
        total = total + got[n].astype(F32)
    for s in range(STEPS):
        out[s] = total[s * 8 : s * 8 + 8].astype(BF16)


def body(
    step_tokens,
    delta_state,
    kv_pages,
    page_table,
    lengths,
    moves,
    delta_norm,
    head_norm,
    w_qk,
    w_vz,
    w_ba,
    a_log,
    dt_bias,
    w_out,
    att_norm,
    qk_norm,
    w_q,
    w_kv,
    w_o,
):
    shape = jax.ShapeDtypeStruct
    place = jnp.stack([lax.axis_index("inst"), lax.axis_index("tp")]).astype(jnp.int32)
    moves = moves.transpose(0, 2, 1)

    gain = delta_norm.reshape(1, D)
    heads = (a_log.reshape(1, 2), dt_bias.reshape(1, 2), head_norm.reshape(1, 128), w_out)

    def project(rows):
        return [
            jnp.einsum("bd,dtc->tbc", rows, w, preferred_element_type=F32)
            for w in (w_qk, w_vz, w_ba)
        ]

    (packed,) = call(
        pack_kernel,
        [SMEM, SMEM, SMEM, HBM, HBM, HBM],
        [shape((INSTS, PIECE, 128), BF16)],
        [
            pltpu.VMEM((STEPS, 2, 128, 128), F32),
            pltpu.VMEM((32, 2, 8, HD), BF16),
            pltpu.VMEM((STEPS, SLOTS, D), BF16),
            pltpu.VMEM((OWN, D), F32),
            pltpu.VMEM((8, D), F32),
            pltpu.SemaphoreType.DMA((37,)),
        ],
    )(moves, place, page_table, delta_state, kv_pages, step_tokens)
    got = lax.all_to_all(packed, "inst", 0, 0)

    (tab,) = call(
        table_kernel, [SMEM] * 3, [shape((T_SIZE,), jnp.int32)], out_specs=[SMEM]
    )(moves, place, lengths)
    (n1,) = call(
        norm_kernel, [VMEM] * 2, [shape((OWN, D), BF16)], [pltpu.VMEM((OWN, D), F32)]
    )(step_tokens, gain)
    rows_own = project(n1)
    early, early_state = call(
        early_kernel,
        [SMEM] + [VMEM] * 8,
        [shape((OWN, D), BF16), shape(delta_state.shape, F32)],
        [pltpu.VMEM((OWN, 256), F32)],
    )(tab, *rows_own, *heads, delta_state)

    (picked,) = call(
        select_kernel,
        [SMEM, VMEM, ANY],
        [shape((INSTS, PIECE, 128), BF16)],
        [pltpu.VMEM((INSTS * PIECE, 128), F32)] * 2,
    )(tab, got, early)
    got = lax.all_to_all(picked, "inst", 0, 0)

    for bit in (1, 2, 4):
        other = lax.ppermute(early, "tp", [(i, i ^ bit) for i in range(PARTS)])
        early = early.astype(F32) + other.astype(F32)
        if bit < 4:
            early = early.astype(BF16)

    n1, rows = call(
        late_norm_kernel,
        [VMEM] * 2,
        [shape((EXTRA, D), BF16), shape((EXTRA, D), F32)],
    )(got, gain)
    part, late_state = call(
        late_kernel,
        [SMEM] + [VMEM] * 11,
        [shape((PARTS, EXTRA, D), BF16), shape((STEPS, 2, 128, 128), F32)],
        [
            pltpu.VMEM((2, EXTRA, 128), F32),
            pltpu.VMEM((2, EXTRA, 256), F32),
            pltpu.VMEM((2, EXTRA, 2), F32),
            pltpu.VMEM((EXTRA, 256), F32),
        ],
    )(tab, *rows_own, *project(n1), *heads, got)
    parts = lax.all_to_all(part, "tp", 0, 0)
    (final_state,) = call(states_kernel, [SMEM, VMEM, VMEM], [shape(delta_state.shape, F32)])(
        tab, early_state, late_state
    )
    hidden, n2, query = call(
        hidden_kernel,
        [SMEM] + [VMEM] * 7,
        [shape((OWN, D), F32), shape((ROWS, D), BF16), shape((PARTS, OWN, HD), BF16)],
        [pltpu.VMEM((ROWS, D), F32), pltpu.VMEM((OWN, D), F32), pltpu.VMEM((EXTRA, D), F32)],
    )(tab, step_tokens, early, rows, parts, att_norm.reshape(1, D), w_q, qk_norm)
    queries = lax.all_to_all(query, "tp", 0, 0)
    kv = jnp.einsum("bd,dtc->tbc", n2, w_kv, preferred_element_type=F32)
    shares, final_pages = call(
        pages_kernel,
        [SMEM, SMEM, SMEM] + [VMEM] * 5,
        [shape((PARTS, OWN, 384), BF16), shape(kv_pages.shape, BF16)],
        [
            pltpu.VMEM((64, 8, HD), F32),
            pltpu.VMEM((64, 8, HD), F32),
            pltpu.VMEM((2, ROWS, HD), F32),
            pltpu.VMEM((PARTS, OWN, HD), F32),
            pltpu.VMEM((PARTS, OWN, 384), F32),
        ],
    )(place, page_table, tab, kv_pages, got, queries, kv, qk_norm)
    shares = lax.all_to_all(shares, "tp", 0, 0)
    (part,) = call(merge_kernel, [VMEM] * 2, [shape((PARTS, OWN, D), BF16)])(shares, w_o)
    parts = lax.all_to_all(part, "tp", 0, 0)
    (mixed,) = call(last_kernel, [VMEM] * 2, [shape(step_tokens.shape, BF16)])(hidden, parts)
    return (mixed, final_state, final_pages)


def solution(mesh):
    in_specs = (
        P(None, "inst", None),
        P("inst", "tp", None, None),
        P("inst", None, "tp", None),
        P("inst", None),
        P(),
        P(),
        P(),
        P(),
        P(None, None, "tp"),
        P(None, None, "tp"),
        P(None, None, "tp"),
        P("tp"),
        P("tp"),
        P("tp", None),
        P(),
        P(),
        P(None, "tp"),
        P(),
        P("tp", None),
    )
    out_specs = (P(None, "inst", None), P("inst", "tp", None, None), P("inst", None, "tp", None))
    return jax.shard_map(body, mesh=mesh, in_specs=in_specs, out_specs=out_specs, check_vma=False)
```

time: 152 us -> 136 us (0.89)
  blocking collectives: 58 us -> 9.35 us
  starting transfers between devices: 12 us -> 32.4 us
  local copies, waits for them, and re-layouts: 9.59 us -> 16 us
  Pallas kernels: 18.5 us -> 23.6 us
  waiting for transfers between devices: 47.3 us -> 43.2 us
  other arithmetic: 0 us -> 2.5 us
  matrix products: 4.6 us -> 6.6 us
    all_to_all x2 -> x0, blocking collectives: 48.7 us -> none  [the longest x1 33.2 us: body(): got = lax.all_to_all(packed.reshape(INSTS, 80, 128), 'inst', 0, 0)]
    all_to_all x1 -> x2, starting transfers between devices: 3.99 us -> 15.4 us  [the longest x1 11.2 us: body(): got = lax.all_to_all(packed, 'inst', 0, 0)]
    unnamed x43 -> x70, local copies, waits for them, and re-layouts: 7.94 us -> 16 us
    all_to_all x1 -> x2, waiting for transfers between devices: 20.7 us -> 14.6 us  [body(): parts = lax.all_to_all(part, 'tp', 0, 0)]
    ppermute x0 -> x3, starting transfers between devices: none -> 5.45 us  [body(): other = lax.ppermute(early, 'tp', [(i, i ^ bit) for i in range(PARTS)])]
    pallas_call x6 -> x10, Pallas kernels: 17.3 us -> 22.4 us  [the longest x1 4.51 us: body(): call(table_kernel, [SMEM] * 3, [shape((T_SIZE,), jnp.int32)], out_specs=[...]
    ppermute x0 -> x3, waiting for transfers between devices: none -> 3.97 us  [body(): other = lax.ppermute(early, 'tp', [(i, i ^ bit) for i in range(PARTS)])]
    all_to_all x1 -> x2, starting transfers between devices: 4.63 us -> 8.19 us  [body(): parts = lax.all_to_all(part, 'tp', 0, 0)]
  transfers between devices with their start and end apart: 3 -> 8, of which waited for: 3 -> 6; matrix products, arithmetic and copies ran while one was open for 1% -> 7% of each run, Pallas kernels for 0% -> 10%
where the time goes in v2:
time: 136 us; the launch traced here: 135 us
  waiting for transfers between devices  43.2 us (32%)
  starting transfers between devices  32.4 us (24%)
  Pallas kernels  23.6 us (17%)
  local copies, waits for them, and re-layouts  16 us (12%)
  blocking collectives  9.35 us (7%)
  matrix products  6.6 us (5%)
  other arithmetic  2.5 us (2%)
    unnamed x70, local copies, waits for them, and re-layouts  16 us
    all_to_all x2, waiting for transfers between devices, body(): parts = lax.all_to_all(part, 'tp', 0, 0)  14.6 us
    all_to_all x1, starting transfers between devices, body(): got = lax.all_to_all(packed, 'inst', 0, 0)  11.2 us
    all_to_all x1, waiting for transfers between devices, body(): got = lax.all_to_all(picked, 'inst', 0, 0)  11.2 us
    all_to_all x1, blocking collectives, body(): shares = lax.all_to_all(shares, 'tp', 0, 0)  9.35 us
    all_to_all x1, waiting for transfers between devices, body(): got = lax.all_to_all(packed, 'inst', 0, 0)  8.97 us
    all_to_all x2, starting transfers between devices, body(): parts = lax.all_to_all(part, 'tp', 0, 0)  8.19 us
    ppermute x3, starting transfers between devices, body(): other = lax.ppermute(early, 'tp', [(i, i ^ bit) for i in range(PARTS)])  5.45 us
  transfers between devices with their start and end apart: 8, of which 6 were waited for; matrix products, arithmetic and copies ran while one was open for 7% of the time, Pallas kernels for 10%

profile of v2, /device:TPU:32, one launch (start us, length us, event | category | flops | bytes accessed | tf_op | source)
XLA Modules:
  0.0 134.6 jit_solution(3174170108524943662)
XLA Ops:
  5.4 3.5 %shard_map.205 = bf16[32,72,128]{2,1,0:T(8,128)(2,1)} custom-call(s32[4,4,16]{2,1,0:T(4,128)S(1)} %bitcast.39, s32[2]{0:T(128)S(1)} %pad_add_fusion.place, s32[8,8]{1,0:T(8,128)S(1)} %copy-done.24, f32[8,2,128,128]{3,2,1,0:T(8,128)S(1)} %copy-done.1, bf16[64,2,8,256]{3,2,1,0:T(8,128)(2,1)S(1)} %copy-done.6, bf16[4,8,2048]{2,1,0:T(8,128)(2,1)S(1)} %copy-done.10), custom_call_target="tpu_custom_call" | custom-call | tf_op jit(solution)/shard_map/pallas_call | solution.py:476
  8.9 11.2 %all-to-all-start = ((bf16[32,72,128]{2,1,0:T(8,128)(2,1)}), bf16[32,72,128]{2,1,0:T(8,128)(2,1)S(1)}, u32[]{:S(2)}, u32[]{:S(2)}) async-start(bf16[32,72,128]{2,1,0:T(8,128)(2,1)} %shard_map.205), calls=%async_computation | async-start | bytes 1179648 | tf_op jit(solution)/shard_map/all_to_all | solution.py:489
  20.2 4.5 %shard_map.202.tab = s32[768]{0:T(1024)S(1)} custom-call(s32[4,4,16]{2,1,0:T(4,128)S(1)} %bitcast.40, s32[2]{0:T(128)S(1)} %pad_add_fusion.place, s32[256]{0:T(256)S(1)} %copy-done.30), custom_call_target="tpu_custom_call" | custom-call | tf_op jit(solution)/shard_map/pallas_call | solution.py:491
  27.3 3.0 %shard_map.204 = (bf16[32,2048]{1,0:T(8,128)(2,1)S(1)}, f32[8,2,128,128]{3,2,1,0:T(8,128)S(1)}) custom-call(s32[768]{0:T(1024)S(1)} %shard_map.202.tab, f32[2,32,128]{2,1,0:T(8,128)S(1)} %convolution_bitcast_fusion.1.qk, f32[2,32,256]{2,1,0:T(8,128)S(1)} %fusion.9.vz, f32[2,32,2]{2,1,0:T(8,128)S(1)} %convolution_bitcast_fusion.ba, f32[1,2]{1,0:T(1,128)S(1)} %bitcast.41, ...), custom_call_target="tpu_custom_call" | custom-call | tf_op jit(solution)/shard_map/pallas_call | solution.py:498
  31.8 9.0 %all-to-all-done.got = bf16[32,72,128]{2,1,0:T(8,128)(2,1)S(1)} async-done(((bf16[32,72,128]{2,1,0:T(8,128)(2,1)}), bf16[32,72,128]{2,1,0:T(8,128)(2,1)S(1)}, u32[]{:S(2)}, u32[]{:S(2)}) %all-to-all-start) | async-done | bytes 589856 | tf_op jit(solution)/shard_map/all_to_all | solution.py:489
  40.8 1.9 %shard_map.206 = bf16[32,72,128]{2,1,0:T(8,128)(2,1)} custom-call(s32[768]{0:T(1024)S(1)} %shard_map.202.tab, bf16[32,72,128]{2,1,0:T(8,128)(2,1)S(1)} %all-to-all-done.got, bf16[32,2048]{1,0:T(8,128)(2,1)S(1)} %get-tuple-element.14.early), custom_call_target="tpu_custom_call" | custom-call | tf_op jit(solution)/shard_map/pallas_call | solution.py:505
  42.7 4.2 %all-to-all-start.1 = ((bf16[32,72,128]{2,1,0:T(8,128)(2,1)}), bf16[32,72,128]{2,1,0:T(8,128)(2,1)S(1)}, u32[]{:S(2)}, u32[]{:S(2)}) async-start(bf16[32,72,128]{2,1,0:T(8,128)(2,1)} %shard_map.206), calls=%async_computation.1 | async-start | bytes 1179648 | tf_op jit(solution)/shard_map/all_to_all | solution.py:511
  46.9 1.7 %collective-permute-start.1 = (bf16[32,2048]{1,0:T(8,128)(2,1)S(1)}, bf16[32,2048]{1,0:T(8,128)(2,1)S(1)}, u32[]{:S(2)}, u32[]{:S(2)}) collective-permute-start(bf16[32,2048]{1,0:T(8,128)(2,1)S(1)} %add_convert_fusion.1), channel_id=1, source_target_pairs={{0,2},{1,3},{2,0},{3,1},{4,6},{5,7},{6,4},{7,5},{8,10},{9,11},{10,... | collective-permute-start | bytes 393224 | tf_op jit(solution)/shard_map/ppermute | solution.py:514
  48.6 4.0 %collective-permute-done.1 = bf16[32,2048]{1,0:T(8,128)(2,1)S(1)} collective-permute-done((bf16[32,2048]{1,0:T(8,128)(2,1)S(1)}, bf16[32,2048]{1,0:T(8,128)(2,1)S(1)}, u32[]{:S(2)}, u32[]{:S(2)}) %collective-permute-start.1) | collective-permute-done | bytes 131104 | tf_op jit(solution)/shard_map/ppermute | solution.py:514
  53.2 3.2 %collective-permute-start.2 = (bf16[32,2048]{1,0:T(8,128)(2,1)}, bf16[32,2048]{1,0:T(8,128)(2,1)}, u32[]{:S(2)}, u32[]{:S(2)}) collective-permute-start(bf16[32,2048]{1,0:T(8,128)(2,1)} %add_convert_fusion), channel_id=1, source_target_pairs={{0,4},{1,5},{2,6},{3,7},{4,0},{5,1},{6,2},{7,3},{8,12},{9,13},{10,... | collective-permute-start | bytes 393224 | tf_op jit(solution)/shard_map/ppermute | solution.py:514
  56.4 11.2 %all-to-all-done.1.got = bf16[32,72,128]{2,1,0:T(8,128)(2,1)S(1)} async-done(((bf16[32,72,128]{2,1,0:T(8,128)(2,1)}), bf16[32,72,128]{2,1,0:T(8,128)(2,1)S(1)}, u32[]{:S(2)}, u32[]{:S(2)}) %all-to-all-start.1) | async-done | bytes 589856 | tf_op jit(solution)/shard_map/all_to_all | solution.py:511
  69.9 2.1 %shard_map.208 = (bf16[8,16,2048]{2,1,0:T(8,128)(2,1)S(1)}, f32[4,2,128,128]{3,2,1,0:T(8,128)S(1)}) custom-call(s32[768]{0:T(1024)S(1)} %shard_map.202.tab, f32[2,32,128]{2,1,0:T(8,128)S(1)} %convolution_bitcast_fusion.1.qk, f32[2,32,256]{2,1,0:T(8,128)S(1)} %fusion.9.vz, f32[2,32,2]{2,1,0:T(8,128)S(1)} %convolution_bitcast_fusion.ba, ...), custom_call_target="tpu_custom_call" | custom-call | tf_op jit(solution)/shard_map/pallas_call | solution.py:524
  73.6 4.5 %all-to-all-start.2 = ((bf16[8,16,2048]{2,1,0:T(8,128)(2,1)}), bf16[8,16,2048]{2,1,0:T(8,128)(2,1)S(1)}, u32[]{:S(2)}, u32[]{:S(2)}) async-start(bf16[8,16,2048]{2,1,0:T(8,128)(2,1)} %copy-done.19), calls=%async_computation.2 | async-start | bytes 1048576 | tf_op jit(solution)/shard_map/all_to_all | solution.py:535
  78.1 1.7 %convert_add_fusion.early = f32[32,2048]{1,0:T(8,128)} fusion(bf16[32,2048]{1,0:T(8,128)(2,1)} %collective-permute-done.2, bf16[32,2048]{1,0:T(8,128)(2,1)} %add_convert_fusion), kind=kLoop, calls=%fused_computation.15 | loop fusion | flops 196608 | bytes 524288 | tf_op jit(solution)/shard_map/add | solution.py:515
  79.8 7.1 %all-to-all-done.2.got = bf16[8,16,2048]{2,1,0:T(8,128)(2,1)S(1)} async-done(((bf16[8,16,2048]{2,1,0:T(8,128)(2,1)}), bf16[8,16,2048]{2,1,0:T(8,128)(2,1)S(1)}, u32[]{:S(2)}, u32[]{:S(2)}) %all-to-all-start.2) | async-done | bytes 524320 | tf_op jit(solution)/shard_map/all_to_all | solution.py:535
  90.9 1.9 %shard_map.209 = (f32[32,2048]{1,0:T(8,128)S(1)}, bf16[48,2048]{1,0:T(8,128)(2,1)S(1)}, bf16[8,32,256]{2,1,0:T(8,128)(2,1)}) custom-call(s32[768]{0:T(1024)S(1)} %shard_map.202.tab, bf16[4,8,2048]{2,1,0:T(8,128)(2,1)S(1)} %copy-done.11, f32[32,2048]{1,0:T(8,128)S(1)} %copy-done.16, f32[16,2048]{1,0:T(8,128)S(1)} %get-tuple-element.15.rows, ...), custom_call_target="tpu_custom_call" | custom-call | tf_op jit(solution)/shard_map/pallas_call | solution.py:539
  94.1 3.4 %all-to-all-start.3 = ((bf16[8,32,256]{2,1,0:T(8,128)(2,1)}), bf16[8,32,256]{2,1,0:T(8,128)(2,1)S(1)}, u32[]{:S(2)}, u32[]{:S(2)}) async-start(bf16[8,32,256]{2,1,0:T(8,128)(2,1)} %get-tuple-element.19), calls=%async_computation.3 | async-start | bytes 262144 | tf_op jit(solution)/shard_map/all_to_all | solution.py:545
  97.5 2.2 %fusion.6.kv = f32[2,48,256]{2,1,0:T(8,128)S(1)} fusion(bf16[2048,2,256]{2,1,0:T(2,128)(2,1)} %param.36, bf16[48,2048]{1,0:T(8,128)(2,1)} %copy-done.31), kind=kOutput, calls=%fused_computation.6 | convolution fusion | flops 100663296 | bytes 2392064 | tf_op jit(solution)/shard_map/bd,dtc->tbc/dot_general | solution.py:546
  99.7 4.4 %all-to-all-done.3.query = bf16[8,32,256]{2,1,0:T(8,128)(2,1)S(1)} async-done(((bf16[8,32,256]{2,1,0:T(8,128)(2,1)}), bf16[8,32,256]{2,1,0:T(8,128)(2,1)S(1)}, u32[]{:S(2)}, u32[]{:S(2)}) %all-to-all-start.3) | async-done | bytes 131104 | tf_op jit(solution)/shard_map/all_to_all | solution.py:545
  104.1 3.7 %shard_map.210 = (bf16[8,32,384]{2,1,0:T(8,128)(2,1)S(1)}, bf16[64,2,8,256]{3,2,1,0:T(8,128)(2,1)}) custom-call(s32[2]{0:T(128)S(1)} %pad_add_fusion.place, s32[8,8]{1,0:T(8,128)S(1)} %copy-done.25, s32[768]{0:T(1024)S(1)} %shard_map.202.tab, bf16[64,2,8,256]{3,2,1,0:T(8,128)(2,1)S(1)} %copy-done.7, bf16[32,72,128]{2,1,0:T(8,128)(2,1)S(1)} %all-to-all-done.1.got, ...), custom_call_target="tpu_custom_call" | custom-call | tf_op jit(solution)/shard_map/pallas_call | solution.py:547
  107.8 9.3 %all_to_all.30.got = bf16[8,32,384]{2,1,0:T(8,128)(2,1)S(1)} all-to-all(bf16[8,32,384]{2,1,0:T(8,128)(2,1)S(1)} %get-tuple-element.21), channel_id=1, replica_groups=mesh['inst'=32,'tp'=8] {'tp'}, dimensions={0} | all-to-all | bytes 393216 | tf_op jit(solution)/shard_map/all_to_all | solution.py:559
  118.6 3.7 %all-to-all-start.5 = ((bf16[8,32,2048]{2,1,0:T(8,128)(2,1)}), bf16[8,32,2048]{2,1,0:T(8,128)(2,1)S(1)}, u32[]{:S(2)}, u32[]{:S(2)}) async-start(bf16[8,32,2048]{2,1,0:T(8,128)(2,1)} %copy-done.5), calls=%async_computation.5 | async-start | bytes 2097152 | tf_op jit(solution)/shard_map/all_to_all | solution.py:561
  124.6 1.7 %shard_map.213 = f32[8,2,128,128]{3,2,1,0:T(8,128)} custom-call(s32[768]{0:T(1024)S(1)} %shard_map.202.tab, f32[8,2,128,128]{3,2,1,0:T(8,128)S(1)} %copy-done.13, f32[4,2,128,128]{3,2,1,0:T(8,128)S(1)} %copy-done.18), custom_call_target="tpu_custom_call" | custom-call | tf_op jit(solution)/shard_map/pallas_call | solution.py:536
  126.2 7.5 %all-to-all-done.5.got = bf16[8,32,2048]{2,1,0:T(8,128)(2,1)S(1)} async-done(((bf16[8,32,2048]{2,1,0:T(8,128)(2,1)}), bf16[8,32,2048]{2,1,0:T(8,128)(2,1)S(1)}, u32[]{:S(2)}, u32[]{:S(2)}) %all-to-all-start.5) | async-done | bytes 1048608 | tf_op jit(solution)/shard_map/all_to_all | solution.py:561
  (88 shorter events, 23.3 us)
Async XLA Ops:
  0.6 26.1 %copy-start = (bf16[2048,2,256]{2,1,0:T(2,128)(2,1)S(1)}, bf16[2048,2,256]{2,1,0:T(2,128)(2,1)}, u32[]{:S(2)}) copy-start(bf16[2048,2,256]{2,1,0:T(2,128)(2,1)} %param.28) | copy-start | bytes 6291460
  0.6 19.5 %copy-start.23 = (s32[4,16,4]{1,2,0:T(4,128)S(1)}, s32[4,16,4]{1,2,0:T(4,128)}, u32[]{:S(2)}) copy-start(s32[4,16,4]{1,2,0:T(4,128)} %param.24) | copy-start | bytes 3076
  0.7 19.5 %copy-start.30 = (s32[256]{0:T(256)S(1)}, s32[256]{0:T(256)}, u32[]{:S(2)}) copy-start(s32[256]{0:T(256)} %lens.1) | copy-start | bytes 3076
  0.7 24.1 %copy-start.32 = (bf16[2048]{0:T(1024)(128)(2,1)S(1)}, bf16[2048]{0:T(1024)(128)(2,1)}, u32[]{:S(2)}) copy-start(bf16[2048]{0:T(1024)(128)(2,1)} %param.25) | copy-start | bytes 12292
  5.4 19.3 %copy-start.11 = (bf16[4,8,2048]{2,1,0:T(8,128)(2,1)S(1)}, bf16[4,8,2048]{2,1,0:T(8,128)(2,1)}, u32[]{:S(2)}) copy-start(bf16[4,8,2048]{2,1,0:T(8,128)(2,1)} %tokens.5) | copy-start | bytes 393220
  5.4 19.5 %copy-start.34 = (bf16[2048,2,2]{0,2,1:T(2,128)(2,1)S(1)}, bf16[2048,2,2]{0,2,1:T(2,128)(2,1)}, u32[]{:S(2)}) copy-start(bf16[2048,2,2]{0,2,1:T(2,128)(2,1)} %param.29) | copy-start | bytes 49156
  8.9 31.9 %all-to-all-start = ((bf16[32,72,128]{2,1,0:T(8,128)(2,1)}), bf16[32,72,128]{2,1,0:T(8,128)(2,1)S(1)}, u32[]{:S(2)}, u32[]{:S(2)}) async-start(bf16[32,72,128]{2,1,0:T(8,128)(2,1)} %shard_map.205), calls=%async_computation | async-start | bytes 1179648 | tf_op jit(solution)/shard_map/all_to_all | solution.py:489
  20.2 7.0 %copy-start.2 = (f32[8,2,128,128]{3,2,1,0:T(8,128)S(1)}, f32[8,2,128,128]{3,2,1,0:T(8,128)}, u32[]{:S(2)}) copy-start(f32[8,2,128,128]{3,2,1,0:T(8,128)} %state.3) | copy-start | bytes 3145732
  20.2 7.0 %copy-start.3 = (bf16[256,2048]{1,0:T(8,128)(2,1)S(1)}, bf16[256,2048]{1,0:T(8,128)(2,1)}, u32[]{:S(2)}) copy-start(bf16[256,2048]{1,0:T(8,128)(2,1)} %w_out.3) | copy-start | bytes 3145732
  20.2 7.0 %copy-start.27 = (f32[2]{0:T(128)S(1)}, f32[2]{0:T(128)}, u32[]{:S(2)}) copy-start(f32[2]{0:T(128)} %param.30) | copy-start | bytes 28
  20.2 7.0 %copy-start.28 = (f32[2]{0:T(128)S(1)}, f32[2]{0:T(128)}, u32[]{:S(2)}) copy-start(f32[2]{0:T(128)} %param.31) | copy-start | bytes 28
  27.2 21.3 %copy-start.33 = (bf16[2048]{0:T(1024)(128)(2,1)S(1)}, bf16[2048]{0:T(1024)(128)(2,1)}, u32[]{:S(2)}) copy-start(bf16[2048]{0:T(1024)(128)(2,1)} %param.33) | copy-start | bytes 12292
  31.2 15.6 %collective-permute-start = (bf16[32,2048]{1,0:T(8,128)(2,1)S(1)}, bf16[32,2048]{1,0:T(8,128)(2,1)S(1)}, u32[]{:S(2)}, u32[]{:S(2)}) collective-permute-start(bf16[32,2048]{1,0:T(8,128)(2,1)S(1)} %get-tuple-element.14.early), channel_id=1, source_target_pairs={{0,1},{1,0},{2,3},{3,2},{4,5},{5,4},{6,7},{7,6},{8,9},{9,8},{10,11... | collective-permute-start | bytes 393224 | tf_op jit(solution)/shard_map/ppermute | solution.py:514
  42.7 24.9 %all-to-all-start.1 = ((bf16[32,72,128]{2,1,0:T(8,128)(2,1)}), bf16[32,72,128]{2,1,0:T(8,128)(2,1)S(1)}, u32[]{:S(2)}, u32[]{:S(2)}) async-start(bf16[32,72,128]{2,1,0:T(8,128)(2,1)} %shard_map.206), calls=%async_computation.1 | async-start | bytes 1179648 | tf_op jit(solution)/shard_map/all_to_all | solution.py:511
  46.9 5.6 %collective-permute-start.1 = (bf16[32,2048]{1,0:T(8,128)(2,1)S(1)}, bf16[32,2048]{1,0:T(8,128)(2,1)S(1)}, u32[]{:S(2)}, u32[]{:S(2)}) collective-permute-start(bf16[32,2048]{1,0:T(8,128)(2,1)S(1)} %add_convert_fusion.1), channel_id=1, source_target_pairs={{0,2},{1,3},{2,0},{3,1},{4,6},{5,7},{6,4},{7,5},{8,10},{9,11},{10,... | collective-permute-start | bytes 393224 | tf_op jit(solution)/shard_map/ppermute | solution.py:514
  53.2 24.9 %collective-permute-start.2 = (bf16[32,2048]{1,0:T(8,128)(2,1)}, bf16[32,2048]{1,0:T(8,128)(2,1)}, u32[]{:S(2)}, u32[]{:S(2)}) collective-permute-start(bf16[32,2048]{1,0:T(8,128)(2,1)} %add_convert_fusion), channel_id=1, source_target_pairs={{0,4},{1,5},{2,6},{3,7},{4,0},{5,1},{6,2},{7,3},{8,12},{9,13},{10,... | collective-permute-start | bytes 393224 | tf_op jit(solution)/shard_map/ppermute | solution.py:514
  69.6 18.0 %copy-start.26 = (bf16[2,256]{1,0:T(2,128)(2,1)S(1)}, bf16[2,256]{1,0:T(2,128)(2,1)}, u32[]{:S(2)}) copy-start(bf16[2,256]{1,0:T(2,128)(2,1)} %kv_gain.1) | copy-start | bytes 3076
  73.6 13.3 %all-to-all-start.2 = ((bf16[8,16,2048]{2,1,0:T(8,128)(2,1)}), bf16[8,16,2048]{2,1,0:T(8,128)(2,1)S(1)}, u32[]{:S(2)}, u32[]{:S(2)}) async-start(bf16[8,16,2048]{2,1,0:T(8,128)(2,1)} %copy-done.19), calls=%async_computation.2 | async-start | bytes 1048576 | tf_op jit(solution)/shard_map/all_to_all | solution.py:535
  90.9 13.2 %copy-start.7 = (bf16[64,2,8,256]{3,2,1,0:T(8,128)(2,1)S(1)}, bf16[64,2,8,256]{3,2,1,0:T(8,128)(2,1)}, u32[]{:S(2)}) copy-start(bf16[64,2,8,256]{3,2,1,0:T(8,128)(2,1)} %pages.3) | copy-start | bytes 1572868
  90.9 13.2 %copy-start.25 = (s32[8,8]{1,0:T(8,128)S(1)}, s32[8,8]{1,0:T(8,128)}, u32[]{:S(2)}) copy-start(s32[8,8]{1,0:T(8,128)} %table.3) | copy-start | bytes 772
  94.1 10.0 %all-to-all-start.3 = ((bf16[8,32,256]{2,1,0:T(8,128)(2,1)}), bf16[8,32,256]{2,1,0:T(8,128)(2,1)S(1)}, u32[]{:S(2)}, u32[]{:S(2)}) async-start(bf16[8,32,256]{2,1,0:T(8,128)(2,1)} %get-tuple-element.19), calls=%async_computation.3 | async-start | bytes 262144 | tf_op jit(solution)/shard_map/all_to_all | solution.py:545
  104.1 13.0 %copy-start.14 = (bf16[256,2048]{1,0:T(8,128)(2,1)S(1)}, bf16[256,2048]{1,0:T(8,128)(2,1)}, u32[]{:S(2)}) copy-start(bf16[256,2048]{1,0:T(8,128)(2,1)} %w_o.1) | copy-start | bytes 3145732
  118.6 15.2 %copy-start.21 = (f32[32,2048]{1,0:T(8,128)S(1)}, f32[32,2048]{1,0:T(8,128)}, u32[]{:S(2)}) copy-start(f32[32,2048]{1,0:T(8,128)} %copy-done.20) | copy-start | bytes 786436
  118.6 15.2 %all-to-all-start.5 = ((bf16[8,32,2048]{2,1,0:T(8,128)(2,1)}), bf16[8,32,2048]{2,1,0:T(8,128)(2,1)S(1)}, u32[]{:S(2)}, u32[]{:S(2)}) async-start(bf16[8,32,2048]{2,1,0:T(8,128)(2,1)} %copy-done.5), calls=%async_computation.5 | async-start | bytes 2097152 | tf_op jit(solution)/shard_map/all_to_all | solution.py:561
  (19 other events, 25.3 us)

commit v3 on v2

--- a/solution.py
+++ b/solution.py
@@ -34,20 +34,22 @@
 LATE = (6, 10, 13, 15)
 
 SMEM = pl.BlockSpec(memory_space=pltpu.SMEM)
-VMEM = pl.BlockSpec(memory_space=pltpu.VMEM)
-HBM = pl.BlockSpec(memory_space=pltpu.HBM)
+VMEM = pl.BlockSpec()
 ANY = pl.BlockSpec(memory_space=pl.ANY)
-PARAMS = pltpu.CompilerParams(vmem_limit_bytes=48 * 1024 * 1024)
-
-
-def call(kernel, ins, outs, scratch=(), out_specs=None):
+
+
+SOME, MOST = 16_000_000, 62_500_000
+NEARLY = 62_000_000
+
+
+def call(kernel, ins, outs, scratch=(), out_specs=None, vmem=SOME):
     return pl.pallas_call(
         kernel,
         in_specs=list(ins),
         out_specs=[VMEM] * len(outs) if out_specs is None else out_specs,
         out_shape=list(outs),
         scratch_shapes=list(scratch),
-        compiler_params=PARAMS,
+        compiler_params=pltpu.CompilerParams(vmem_limit_bytes=vmem),
     )
 
 
@@ -71,9 +73,9 @@
 
 
 def pack_kernel(
-    moves, place, table, state, pages, tokens, out, st_scr, pg_scr, bf_scr, tok_scr, row_scr, sem
+    moves, table, state, pages, tokens, out, st_scr, pg_scr, bf_scr, tok_scr, row_scr, sem
 ):
-    slots = own_slots(moves, place[0])
+    slots = own_slots(moves, lax.axis_index("inst"))
     token_copy = pltpu.make_async_copy(tokens, bf_scr, sem.at[36])
     token_copy.start()
     copies = []
@@ -315,7 +317,21 @@
 
 
 def hidden_kernel(
-    tab, tokens, early, rows, got, gain, w_q, q_gain, hidden, normed, query, all_scr, tok_scr, late
+    tab,
+    done,
+    tokens,
+    early,
+    rows,
+    got,
+    gain,
+    w_q,
+    q_gain,
+    hidden,
+    normed,
+    query,
+    all_scr,
+    tok_scr,
+    late,
 ):
     total = got[0].astype(F32)
     for n in range(1, PARTS):
@@ -475,7 +491,7 @@
 
     (packed,) = call(
         pack_kernel,
-        [SMEM, SMEM, SMEM, HBM, HBM, HBM],
+        [SMEM, SMEM, ANY, ANY, ANY],
         [shape((INSTS, PIECE, 128), BF16)],
         [
             pltpu.VMEM((STEPS, 2, 128, 128), F32),
@@ -485,7 +501,8 @@
             pltpu.VMEM((8, D), F32),
             pltpu.SemaphoreType.DMA((37,)),
         ],
-    )(moves, place, page_table, delta_state, kv_pages, step_tokens)
+        vmem=MOST,
+    )(moves, page_table, delta_state, kv_pages, step_tokens)
     got = lax.all_to_all(packed, "inst", 0, 0)
 
     (tab,) = call(
@@ -538,10 +555,11 @@
     )
     hidden, n2, query = call(
         hidden_kernel,
-        [SMEM] + [VMEM] * 7,
+        [SMEM, ANY] + [VMEM] * 7,
         [shape((OWN, D), F32), shape((ROWS, D), BF16), shape((PARTS, OWN, HD), BF16)],
         [pltpu.VMEM((ROWS, D), F32), pltpu.VMEM((OWN, D), F32), pltpu.VMEM((EXTRA, D), F32)],
-    )(tab, step_tokens, early, rows, parts, att_norm.reshape(1, D), w_q, qk_norm)
+        vmem=NEARLY,
+    )(tab, final_state, step_tokens, early, rows, parts, att_norm.reshape(1, D), w_q, qk_norm)
     queries = lax.all_to_all(query, "tp", 0, 0)
     kv = jnp.einsum("bd,dtc->tbc", n2, w_kv, preferred_element_type=F32)
     shares, final_pages = call(

time: 136 us -> 125 us (0.919)
  blocking collectives: 9.35 us -> 23.3 us
  waiting for transfers between devices: 43.2 us -> 31.1 us
  local copies, waits for them, and re-layouts: 16 us -> 5.72 us
  starting transfers between devices: 32.4 us -> 28.9 us
    all_to_all x0 -> x1, blocking collectives: none -> 14 us  [body(): parts = lax.all_to_all(part, 'tp', 0, 0)]
    unnamed x70 -> x56, local copies, waits for them, and re-layouts: 16 us -> 5.11 us
    all_to_all x2 -> x1, waiting for transfers between devices: 14.6 us -> 4.46 us  [body(): parts = lax.all_to_all(part, 'tp', 0, 0)]
    all_to_all x2 -> x1, starting transfers between devices: 8.19 us -> 4.5 us  [body(): parts = lax.all_to_all(part, 'tp', 0, 0)]
    all_to_all x1, waiting for transfers between devices: 8.97 us -> 7.09 us  [body(): got = lax.all_to_all(packed, 'inst', 0, 0)]
  transfers between devices with their start and end apart: 8 -> 7, of which waited for: 6 -> 5; matrix products, arithmetic and copies ran while one was open for 7% -> 7% of each run, Pallas kernels for 10% -> 11%
where the time goes in v3:
time: 125 us; the launch traced here: 123 us
  waiting for transfers between devices  31.1 us (25%)
  starting transfers between devices  28.9 us (23%)
  Pallas kernels  24.8 us (20%)
  blocking collectives  23.3 us (19%)
  matrix products  6.67 us (5%)
  local copies, waits for them, and re-layouts  5.72 us (5%)
  other arithmetic  1.8 us (1%)
    all_to_all x1, blocking collectives, body(): parts = lax.all_to_all(part, 'tp', 0, 0)  14 us
    all_to_all x1, waiting for transfers between devices, body(): got = lax.all_to_all(picked, 'inst', 0, 0)  11.7 us
    all_to_all x1, starting transfers between devices, body(): got = lax.all_to_all(packed, 'inst', 0, 0)  11.2 us
    all_to_all x1, blocking collectives, body(): shares = lax.all_to_all(shares, 'tp', 0, 0)  9.35 us
    all_to_all x1, waiting for transfers between devices, body(): got = lax.all_to_all(packed, 'inst', 0, 0)  7.09 us
    ppermute x3, starting transfers between devices, body(): other = lax.ppermute(early, 'tp', [(i, i ^ bit) for i in range(PARTS)])  5.54 us
    unnamed x56, local copies, waits for them, and re-layouts  5.11 us
    pallas_call x1, Pallas kernels, body(): call(table_kernel, [SMEM] * 3, [shape((T_SIZE,), jnp.int32)], out_specs=[...  4.51 us
  transfers between devices with their start and end apart: 7, of which 5 were waited for; matrix products, arithmetic and copies ran while one was open for 7% of the time, Pallas kernels for 11%

profile of v3, /device:TPU:32, one launch (start us, length us, event | category | flops | bytes accessed | tf_op | source)
XLA Modules:
  0.0 123.3 jit_solution(5307918455324709546)
XLA Ops:
  0.7 3.6 %shard_map.205 = bf16[32,72,128]{2,1,0:T(8,128)(2,1)} custom-call(s32[4,4,16]{2,1,0:T(4,128)} %bitcast.39, s32[8,8]{1,0:T(8,128)} %table.3, f32[8,2,128,128]{3,2,1,0:T(8,128)} %state.3, bf16[64,2,8,256]{3,2,1,0:T(8,128)(2,1)} %pages.3, bf16[4,8,2048]{2,1,0:T(8,128)(2,1)} %tokens.5), custom_call_target="tpu_custom_call" | custom-call | tf_op jit(solution)/shard_map/pallas_call | solution.py:492
  4.3 11.2 %all-to-all-start = ((bf16[32,72,128]{2,1,0:T(8,128)(2,1)}), bf16[32,72,128]{2,1,0:T(8,128)(2,1)}, u32[]{:S(2)}, u32[]{:S(2)}) async-start(bf16[32,72,128]{2,1,0:T(8,128)(2,1)} %shard_map.205), calls=%async_computation | async-start | bytes 1179648 | tf_op jit(solution)/shard_map/all_to_all | solution.py:506
  15.8 4.5 %shard_map.202.tab = s32[768]{0:T(1024)S(1)} custom-call(s32[4,4,16]{2,1,0:T(4,128)S(1)} %bitcast.40, s32[2]{0:T(128)S(1)} %pad_add_fusion.place, s32[256]{0:T(256)S(1)} %copy-done.23), custom_call_target="tpu_custom_call" | custom-call | tf_op jit(solution)/shard_map/pallas_call | solution.py:508
  24.6 3.1 %shard_map.204 = (bf16[32,2048]{1,0:T(8,128)(2,1)S(1)}, f32[8,2,128,128]{3,2,1,0:T(8,128)S(1)}) custom-call(s32[768]{0:T(1024)S(1)} %shard_map.202.tab, f32[2,32,128]{2,1,0:T(8,128)S(1)} %convolution_bitcast_fusion.1.qk, f32[2,32,256]{2,1,0:T(8,128)S(1)} %fusion.9.vz, f32[2,32,2]{2,1,0:T(8,128)S(1)} %convolution_bitcast_fusion.ba, f32[1,2]{1,0:T(1,128)S(1)} %bitcast.41, ...), custom_call_target="tpu_custom_call" | custom-call | tf_op jit(solution)/shard_map/pallas_call | solution.py:515
  29.3 7.1 %all-to-all-done.got = bf16[32,72,128]{2,1,0:T(8,128)(2,1)} async-done(((bf16[32,72,128]{2,1,0:T(8,128)(2,1)}), bf16[32,72,128]{2,1,0:T(8,128)(2,1)}, u32[]{:S(2)}, u32[]{:S(2)}) %all-to-all-start) | async-done | bytes 589856 | tf_op jit(solution)/shard_map/all_to_all | solution.py:506
  36.4 2.4 %shard_map.206 = bf16[32,72,128]{2,1,0:T(8,128)(2,1)} custom-call(s32[768]{0:T(1024)S(1)} %shard_map.202.tab, bf16[32,72,128]{2,1,0:T(8,128)(2,1)} %all-to-all-done.got, bf16[32,2048]{1,0:T(8,128)(2,1)S(1)} %get-tuple-element.15.early), custom_call_target="tpu_custom_call" | custom-call | tf_op jit(solution)/shard_map/pallas_call | solution.py:522
  38.7 4.1 %all-to-all-start.1 = ((bf16[32,72,128]{2,1,0:T(8,128)(2,1)}), bf16[32,72,128]{2,1,0:T(8,128)(2,1)S(1)}, u32[]{:S(2)}, u32[]{:S(2)}) async-start(bf16[32,72,128]{2,1,0:T(8,128)(2,1)} %shard_map.206), calls=%async_computation.1 | async-start | bytes 1179648 | tf_op jit(solution)/shard_map/all_to_all | solution.py:528
  42.9 1.7 %collective-permute-start.1 = (bf16[32,2048]{1,0:T(8,128)(2,1)S(1)}, bf16[32,2048]{1,0:T(8,128)(2,1)S(1)}, u32[]{:S(2)}, u32[]{:S(2)}) collective-permute-start(bf16[32,2048]{1,0:T(8,128)(2,1)S(1)} %add_convert_fusion.1), channel_id=1, source_target_pairs={{0,2},{1,3},{2,0},{3,1},{4,6},{5,7},{6,4},{7,5},{8,10},{9,11},{10,... | collective-permute-start | bytes 393224 | tf_op jit(solution)/shard_map/ppermute | solution.py:531
  45.1 3.4 %collective-permute-done.1 = bf16[32,2048]{1,0:T(8,128)(2,1)S(1)} collective-permute-done((bf16[32,2048]{1,0:T(8,128)(2,1)S(1)}, bf16[32,2048]{1,0:T(8,128)(2,1)S(1)}, u32[]{:S(2)}, u32[]{:S(2)}) %collective-permute-start.1) | collective-permute-done | bytes 131104 | tf_op jit(solution)/shard_map/ppermute | solution.py:531
  48.6 3.3 %collective-permute-start.2 = (bf16[32,2048]{1,0:T(8,128)(2,1)S(1)}, bf16[32,2048]{1,0:T(8,128)(2,1)}, u32[]{:S(2)}, u32[]{:S(2)}) collective-permute-start(bf16[32,2048]{1,0:T(8,128)(2,1)S(1)} %add_convert_fusion), channel_id=1, source_target_pairs={{0,4},{1,5},{2,6},{3,7},{4,0},{5,1},{6,2},{7,3},{8,12},{9,13},{10,... | collective-permute-start | bytes 393224 | tf_op jit(solution)/shard_map/ppermute | solution.py:531
  51.8 11.7 %all-to-all-done.1.got = bf16[32,72,128]{2,1,0:T(8,128)(2,1)S(1)} async-done(((bf16[32,72,128]{2,1,0:T(8,128)(2,1)}), bf16[32,72,128]{2,1,0:T(8,128)(2,1)S(1)}, u32[]{:S(2)}, u32[]{:S(2)}) %all-to-all-start.1) | async-done | bytes 589856 | tf_op jit(solution)/shard_map/all_to_all | solution.py:528
  63.7 1.6 %convolution_bitcast_fusion.3.qk_in = f32[2,16,128]{2,1,0:T(8,128)S(1)} fusion(bf16[2048,2,128]{2,1,0:T(2,128)(2,1)} %param.27, bf16[16,2048]{1,0:T(8,128)(2,1)S(1)} %get-tuple-element.16), kind=kOutput, calls=%fused_computation.12 | convolution fusion | flops 16777216 | bytes 1130496 | tf_op jit(solution)/shard_map/bd,dtc->tbc/dot_general | solution.py:488
  66.0 1.7 %shard_map.208 = (bf16[8,16,2048]{2,1,0:T(8,128)(2,1)S(1)}, f32[4,2,128,128]{3,2,1,0:T(8,128)S(1)}) custom-call(s32[768]{0:T(1024)S(1)} %shard_map.202.tab, f32[2,32,128]{2,1,0:T(8,128)S(1)} %convolution_bitcast_fusion.1.qk, f32[2,32,256]{2,1,0:T(8,128)S(1)} %fusion.9.vz, f32[2,32,2]{2,1,0:T(8,128)S(1)} %convolution_bitcast_fusion.ba, ...), custom_call_target="tpu_custom_call" | custom-call | tf_op jit(solution)/shard_map/pallas_call | solution.py:541
  68.5 4.5 %all-to-all-start.2 = ((bf16[8,16,2048]{2,1,0:T(8,128)(2,1)}), bf16[8,16,2048]{2,1,0:T(8,128)(2,1)}, u32[]{:S(2)}, u32[]{:S(2)}) async-start(bf16[8,16,2048]{2,1,0:T(8,128)(2,1)} %copy-done.9), calls=%async_computation.2 | async-start | bytes 1048576 | tf_op jit(solution)/shard_map/all_to_all | solution.py:552
  73.0 1.7 %convert_add_fusion.early = f32[32,2048]{1,0:T(8,128)} fusion(bf16[32,2048]{1,0:T(8,128)(2,1)} %collective-permute-done.2, bf16[32,2048]{1,0:T(8,128)(2,1)S(1)} %add_convert_fusion), kind=kLoop, calls=%fused_computation.15 | loop fusion | flops 196608 | bytes 524288 | tf_op jit(solution)/shard_map/add | solution.py:532
  75.9 1.7 %shard_map.209.done = f32[8,2,128,128]{3,2,1,0:T(8,128)} custom-call(s32[768]{0:T(1024)S(1)} %shard_map.202.tab, f32[8,2,128,128]{3,2,1,0:T(8,128)S(1)} %copy-done.7, f32[4,2,128,128]{3,2,1,0:T(8,128)S(1)} %get-tuple-element.17.late), custom_call_target="tpu_custom_call" | custom-call | tf_op jit(solution)/shard_map/pallas_call | solution.py:553
  77.6 4.5 %all-to-all-done.2.got = bf16[8,16,2048]{2,1,0:T(8,128)(2,1)} async-done(((bf16[8,16,2048]{2,1,0:T(8,128)(2,1)}), bf16[8,16,2048]{2,1,0:T(8,128)(2,1)}, u32[]{:S(2)}, u32[]{:S(2)}) %all-to-all-start.2) | async-done | bytes 524320 | tf_op jit(solution)/shard_map/all_to_all | solution.py:552
  82.0 2.8 %shard_map.210 = (f32[32,2048]{1,0:T(8,128)}, bf16[48,2048]{1,0:T(8,128)(2,1)}, bf16[8,32,256]{2,1,0:T(8,128)(2,1)}) custom-call(s32[768]{0:T(1024)} %copy-done.11, f32[8,2,128,128]{3,2,1,0:T(8,128)} %shard_map.209.done, bf16[4,8,2048]{2,1,0:T(8,128)(2,1)} %tokens.5, f32[32,2048]{1,0:T(8,128)} %convert_add_fusion.early, f32[16,2048]{1,0:T(8,128)} %copy-done.13, ...), custom_call_target="tpu_custom_call" | custom-call | tf_op jit(solution)/shard_map/pallas_call | solution.py:556
  84.8 3.5 %all-to-all-start.3 = ((bf16[8,32,256]{2,1,0:T(8,128)(2,1)}), bf16[8,32,256]{2,1,0:T(8,128)(2,1)S(1)}, u32[]{:S(2)}, u32[]{:S(2)}) async-start(bf16[8,32,256]{2,1,0:T(8,128)(2,1)} %get-tuple-element.21), calls=%async_computation.3 | async-start | bytes 262144 | tf_op jit(solution)/shard_map/all_to_all | solution.py:563
  88.4 2.2 %fusion.6.kv = f32[2,48,256]{2,1,0:T(8,128)S(1)} fusion(bf16[2048,2,256]{2,1,0:T(2,128)(2,1)} %param.36, bf16[48,2048]{1,0:T(8,128)(2,1)} %get-tuple-element.22), kind=kOutput, calls=%fused_computation.6 | convolution fusion | flops 100663296 | bytes 2392064 | tf_op jit(solution)/shard_map/bd,dtc->tbc/dot_general | solution.py:564
  90.5 4.4 %all-to-all-done.3.query = bf16[8,32,256]{2,1,0:T(8,128)(2,1)S(1)} async-done(((bf16[8,32,256]{2,1,0:T(8,128)(2,1)}), bf16[8,32,256]{2,1,0:T(8,128)(2,1)S(1)}, u32[]{:S(2)}, u32[]{:S(2)}) %all-to-all-start.3) | async-done | bytes 131104 | tf_op jit(solution)/shard_map/all_to_all | solution.py:563
  95.0 3.7 %shard_map.211 = (bf16[8,32,384]{2,1,0:T(8,128)(2,1)S(1)}, bf16[64,2,8,256]{3,2,1,0:T(8,128)(2,1)}) custom-call(s32[2]{0:T(128)S(1)} %pad_add_fusion.place, s32[8,8]{1,0:T(8,128)S(1)} %copy-done.15, s32[768]{0:T(1024)S(1)} %copy-done.12, bf16[64,2,8,256]{3,2,1,0:T(8,128)(2,1)S(1)} %copy-done.4, bf16[32,72,128]{2,1,0:T(8,128)(2,1)S(1)} %all-to-all-done.1.got, ...), custom_call_target="tpu_custom_call" | custom-call | tf_op jit(solution)/shard_map/pallas_call | solution.py:565
  98.7 9.3 %all_to_all.30.got = bf16[8,32,384]{2,1,0:T(8,128)(2,1)S(1)} all-to-all(bf16[8,32,384]{2,1,0:T(8,128)(2,1)S(1)} %get-tuple-element.23), channel_id=1, replica_groups=mesh['inst'=32,'tp'=8] {'tp'}, dimensions={0} | all-to-all | bytes 393216 | tf_op jit(solution)/shard_map/all_to_all | solution.py:577
  108.5 14.0 %all_to_all.31.got = bf16[8,32,2048]{2,1,0:T(8,128)(2,1)S(1)} all-to-all(bf16[8,32,2048]{2,1,0:T(8,128)(2,1)S(1)} %shard_map.212), channel_id=1, replica_groups=mesh['inst'=32,'tp'=8] {'tp'}, dimensions={0} | all-to-all | bytes 2097152 | tf_op jit(solution)/shard_map/all_to_all | solution.py:579
  (73 shorter events, 10.8 us)
Async XLA Ops:
  0.6 21.5 %copy-start = (bf16[2048,2,256]{2,1,0:T(2,128)(2,1)S(1)}, bf16[2048,2,256]{2,1,0:T(2,128)(2,1)}, u32[]{:S(2)}) copy-start(bf16[2048,2,256]{2,1,0:T(2,128)(2,1)} %param.28) | copy-start | bytes 6291460
  0.6 15.2 %copy-start.14 = (s32[4,16,4]{1,2,0:T(4,128)S(1)}, s32[4,16,4]{1,2,0:T(4,128)}, u32[]{:S(2)}) copy-start(s32[4,16,4]{1,2,0:T(4,128)} %param.24) | copy-start | bytes 3076
  0.7 14.9 %copy-start.5 = (bf16[4,8,2048]{2,1,0:T(8,128)(2,1)S(1)}, bf16[4,8,2048]{2,1,0:T(8,128)(2,1)}, u32[]{:S(2)}) copy-start(bf16[4,8,2048]{2,1,0:T(8,128)(2,1)} %tokens.5) | copy-start | bytes 393220
  0.7 14.9 %copy-start.24 = (bf16[2048]{0:T(1024)(128)(2,1)S(1)}, bf16[2048]{0:T(1024)(128)(2,1)}, u32[]{:S(2)}) copy-start(bf16[2048]{0:T(1024)(128)(2,1)} %param.25) | copy-start | bytes 12292
  0.7 15.1 %copy-start.23 = (s32[256]{0:T(256)S(1)}, s32[256]{0:T(256)}, u32[]{:S(2)}) copy-start(s32[256]{0:T(256)} %lens.1) | copy-start | bytes 3076
  0.7 19.7 %copy-start.26 = (bf16[2048,2,2]{0,2,1:T(2,128)(2,1)S(1)}, bf16[2048,2,2]{0,2,1:T(2,128)(2,1)}, u32[]{:S(2)}) copy-start(bf16[2048,2,2]{0,2,1:T(2,128)(2,1)} %param.29) | copy-start | bytes 49156
  4.3 32.1 %all-to-all-start = ((bf16[32,72,128]{2,1,0:T(8,128)(2,1)}), bf16[32,72,128]{2,1,0:T(8,128)(2,1)}, u32[]{:S(2)}, u32[]{:S(2)}) async-start(bf16[32,72,128]{2,1,0:T(8,128)(2,1)} %shard_map.205), calls=%async_computation | async-start | bytes 1179648 | tf_op jit(solution)/shard_map/all_to_all | solution.py:506
  20.4 54.3 %copy-start.11 = (s32[768]{0:T(1024)}, s32[768]{0:T(1024)S(1)}, u32[]{:S(2)}) copy-start(s32[768]{0:T(1024)S(1)} %shard_map.202.tab) | copy-start | bytes 9220
  28.7 15.8 %copy-start.25 = (bf16[2048]{0:T(1024)(128)(2,1)S(1)}, bf16[2048]{0:T(1024)(128)(2,1)}, u32[]{:S(2)}) copy-start(bf16[2048]{0:T(1024)(128)(2,1)} %param.33) | copy-start | bytes 12292
  28.7 14.1 %collective-permute-start = (bf16[32,2048]{1,0:T(8,128)(2,1)S(1)}, bf16[32,2048]{1,0:T(8,128)(2,1)S(1)}, u32[]{:S(2)}, u32[]{:S(2)}) collective-permute-start(bf16[32,2048]{1,0:T(8,128)(2,1)S(1)} %get-tuple-element.15.early), channel_id=1, source_target_pairs={{0,1},{1,0},{2,3},{3,2},{4,5},{5,4},{6,7},{7,6},{8,9},{9,8},{10,11... | collective-permute-start | bytes 393224 | tf_op jit(solution)/shard_map/ppermute | solution.py:531
  38.7 24.8 %all-to-all-start.1 = ((bf16[32,72,128]{2,1,0:T(8,128)(2,1)}), bf16[32,72,128]{2,1,0:T(8,128)(2,1)S(1)}, u32[]{:S(2)}, u32[]{:S(2)}) async-start(bf16[32,72,128]{2,1,0:T(8,128)(2,1)} %shard_map.206), calls=%async_computation.1 | async-start | bytes 1179648 | tf_op jit(solution)/shard_map/all_to_all | solution.py:528
  42.9 5.6 %collective-permute-start.1 = (bf16[32,2048]{1,0:T(8,128)(2,1)S(1)}, bf16[32,2048]{1,0:T(8,128)(2,1)S(1)}, u32[]{:S(2)}, u32[]{:S(2)}) collective-permute-start(bf16[32,2048]{1,0:T(8,128)(2,1)S(1)} %add_convert_fusion.1), channel_id=1, source_target_pairs={{0,2},{1,3},{2,0},{3,1},{4,6},{5,7},{6,4},{7,5},{8,10},{9,11},{10,... | collective-permute-start | bytes 393224 | tf_op jit(solution)/shard_map/ppermute | solution.py:531
  45.1 20.6 %copy-start.27 = (bf16[2048,2,2]{0,2,1:T(2,128)(2,1)S(1)}, bf16[2048,2,2]{0,2,1:T(2,128)(2,1)}, u32[]{:S(2)}) copy-start(bf16[2048,2,2]{0,2,1:T(2,128)(2,1)} %param.29) | copy-start | bytes 49156
  48.5 17.4 %copy-start.18 = (f32[2]{0:T(128)S(1)}, f32[2]{0:T(128)}, u32[]{:S(2)}) copy-start(f32[2]{0:T(128)} %param.30) | copy-start | bytes 28
  48.5 17.4 %copy-start.20 = (f32[2]{0:T(128)S(1)}, f32[2]{0:T(128)}, u32[]{:S(2)}) copy-start(f32[2]{0:T(128)} %param.31) | copy-start | bytes 28
  48.6 17.4 %copy-start.22 = (bf16[128]{0:T(256)(128)(2,1)S(1)}, bf16[128]{0:T(256)(128)(2,1)}, u32[]{:S(2)}) copy-start(bf16[128]{0:T(256)(128)(2,1)} %param.26) | copy-start | bytes 772
  48.6 24.5 %collective-permute-start.2 = (bf16[32,2048]{1,0:T(8,128)(2,1)S(1)}, bf16[32,2048]{1,0:T(8,128)(2,1)}, u32[]{:S(2)}, u32[]{:S(2)}) collective-permute-start(bf16[32,2048]{1,0:T(8,128)(2,1)S(1)} %add_convert_fusion), channel_id=1, source_target_pairs={{0,4},{1,5},{2,6},{3,7},{4,0},{5,1},{6,2},{7,3},{8,12},{9,13},{10,... | collective-permute-start | bytes 393224 | tf_op jit(solution)/shard_map/ppermute | solution.py:531
  68.5 13.5 %all-to-all-start.2 = ((bf16[8,16,2048]{2,1,0:T(8,128)(2,1)}), bf16[8,16,2048]{2,1,0:T(8,128)(2,1)}, u32[]{:S(2)}, u32[]{:S(2)}) async-start(bf16[8,16,2048]{2,1,0:T(8,128)(2,1)} %copy-done.9), calls=%async_computation.2 | async-start | bytes 1048576 | tf_op jit(solution)/shard_map/all_to_all | solution.py:552
  84.8 10.2 %copy-start.4 = (bf16[64,2,8,256]{3,2,1,0:T(8,128)(2,1)S(1)}, bf16[64,2,8,256]{3,2,1,0:T(8,128)(2,1)}, u32[]{:S(2)}) copy-start(bf16[64,2,8,256]{3,2,1,0:T(8,128)(2,1)} %pages.3) | copy-start | bytes 1572868
  84.8 10.2 %copy-start.12 = (s32[768]{0:T(1024)S(1)}, s32[768]{0:T(1024)}, u32[]{:S(2)}) copy-start(s32[768]{0:T(1024)} %copy-done.11) | copy-start | bytes 9220
  84.8 10.2 %copy-start.15 = (s32[8,8]{1,0:T(8,128)S(1)}, s32[8,8]{1,0:T(8,128)}, u32[]{:S(2)}) copy-start(s32[8,8]{1,0:T(8,128)} %table.3) | copy-start | bytes 772
  84.8 10.1 %all-to-all-start.3 = ((bf16[8,32,256]{2,1,0:T(8,128)(2,1)}), bf16[8,32,256]{2,1,0:T(8,128)(2,1)S(1)}, u32[]{:S(2)}, u32[]{:S(2)}) async-start(bf16[8,32,256]{2,1,0:T(8,128)(2,1)} %get-tuple-element.21), calls=%async_computation.3 | async-start | bytes 262144 | tf_op jit(solution)/shard_map/all_to_all | solution.py:563
  95.0 13.0 %copy-start.8 = (bf16[256,2048]{1,0:T(8,128)(2,1)S(1)}, bf16[256,2048]{1,0:T(8,128)(2,1)}, u32[]{:S(2)}) copy-start(bf16[256,2048]{1,0:T(8,128)(2,1)} %w_o.1) | copy-start | bytes 3145732
  108.0 14.4 %copy-start.10 = (f32[32,2048]{1,0:T(8,128)S(1)}, f32[32,2048]{1,0:T(8,128)}, u32[]{:S(2)}) copy-start(f32[32,2048]{1,0:T(8,128)} %get-tuple-element.20.hidden) | copy-start | bytes 786436
  (11 other events, 33.8 us)

commit v4 on v3

--- a/solution.py
+++ b/solution.py
@@ -374,12 +374,10 @@
     def write(slot, length, row):
         offset = length & 63
         block = slot * 8 + lax.shift_right_logical(length, 6)
-
-        @pl.when(lax.shift_right_logical(offset, 3) == part)
-        def _():
-            at = pl.ds(offset & 7, 1)
-            key[block, at, :] = new[0, row : row + 1, :]
-            val[block, at, :] = new[1, row : row + 1, :]
+        block = jnp.where(lax.shift_right_logical(offset, 3) == part, block, 64)
+        at = pl.ds(offset & 7, 1)
+        key[block, at, :] = new[0, row : row + 1, :]
+        val[block, at, :] = new[1, row : row + 1, :]
 
     column = lax.broadcasted_iota(jnp.int32, (1, 512), 1)
     column_slot = lax.shift_right_logical(column, 6)
@@ -407,8 +405,8 @@
             lengths = jnp.where(column_slot == b, length, lengths)
         visible = jnp.logical_and(same, position <= lengths)
         q = q_scr[:, s * 8 : s * 8 + 8, :].reshape(64, HD).astype(BF16)
-        k = key[...].reshape(512, HD).astype(BF16)
-        v = val[...].reshape(512, HD).astype(BF16)
+        k = key[:64].reshape(512, HD).astype(BF16)
+        v = val[:64].reshape(512, HD).astype(BF16)
         scores = lax.dot_general(
             q, k, (((1,), (1,)), ((), ())), preferred_element_type=F32
         ) * (float(HD) ** -0.5)
@@ -567,8 +565,8 @@
         [SMEM, SMEM, SMEM] + [VMEM] * 5,
         [shape((PARTS, OWN, 384), BF16), shape(kv_pages.shape, BF16)],
         [
-            pltpu.VMEM((64, 8, HD), F32),
-            pltpu.VMEM((64, 8, HD), F32),
+            pltpu.VMEM((65, 8, HD), F32),
+            pltpu.VMEM((65, 8, HD), F32),
             pltpu.VMEM((2, ROWS, HD), F32),
             pltpu.VMEM((PARTS, OWN, HD), F32),
             pltpu.VMEM((PARTS, OWN, 384), F32),

time: 125 us -> 125 us (level)
  no operation moved by 1% of the time
where the time goes in v4:
time: 125 us; the launch traced here: 123 us
  waiting for transfers between devices  31.1 us (25%)
  starting transfers between devices  28.9 us (23%)
  Pallas kernels  24.7 us (20%)
  blocking collectives  23.3 us (19%)
  matrix products  6.67 us (5%)
  local copies, waits for them, and re-layouts  5.72 us (5%)
  other arithmetic  1.8 us (1%)
    all_to_all x1, blocking collectives, body(): parts = lax.all_to_all(part, 'tp', 0, 0)  14 us
    all_to_all x1, waiting for transfers between devices, body(): got = lax.all_to_all(picked, 'inst', 0, 0)  11.7 us
    all_to_all x1, starting transfers between devices, body(): got = lax.all_to_all(packed, 'inst', 0, 0)  11.2 us
    all_to_all x1, blocking collectives, body(): shares = lax.all_to_all(shares, 'tp', 0, 0)  9.35 us
    all_to_all x1, waiting for transfers between devices, body(): got = lax.all_to_all(packed, 'inst', 0, 0)  7.08 us
    ppermute x3, starting transfers between devices, body(): other = lax.ppermute(early, 'tp', [(i, i ^ bit) for i in range(PARTS)])  5.54 us
    unnamed x56, local copies, waits for them, and re-layouts  5.11 us
    pallas_call x1, Pallas kernels, body(): call(table_kernel, [SMEM] * 3, [shape((T_SIZE,), jnp.int32)], out_specs=[...  4.51 us
  transfers between devices with their start and end apart: 7, of which 5 were waited for; matrix products, arithmetic and copies ran while one was open for 7% of the time, Pallas kernels for 11%

profile of v4, /device:TPU:32, one launch (start us, length us, event | category | flops | bytes accessed | tf_op | source)
XLA Modules:
  0.0 123.1 jit_solution(13606724229482302785)
XLA Ops:
  0.7 3.6 %shard_map.205 = bf16[32,72,128]{2,1,0:T(8,128)(2,1)} custom-call(s32[4,4,16]{2,1,0:T(4,128)} %bitcast.39, s32[8,8]{1,0:T(8,128)} %table.3, f32[8,2,128,128]{3,2,1,0:T(8,128)} %state.3, bf16[64,2,8,256]{3,2,1,0:T(8,128)(2,1)} %pages.3, bf16[4,8,2048]{2,1,0:T(8,128)(2,1)} %tokens.5), custom_call_target="tpu_custom_call" | custom-call | tf_op jit(solution)/shard_map/pallas_call | solution.py:490
  4.3 11.2 %all-to-all-start = ((bf16[32,72,128]{2,1,0:T(8,128)(2,1)}), bf16[32,72,128]{2,1,0:T(8,128)(2,1)}, u32[]{:S(2)}, u32[]{:S(2)}) async-start(bf16[32,72,128]{2,1,0:T(8,128)(2,1)} %shard_map.205), calls=%async_computation | async-start | bytes 1179648 | tf_op jit(solution)/shard_map/all_to_all | solution.py:504
  15.8 4.5 %shard_map.202.tab = s32[768]{0:T(1024)S(1)} custom-call(s32[4,4,16]{2,1,0:T(4,128)S(1)} %bitcast.40, s32[2]{0:T(128)S(1)} %pad_add_fusion.place, s32[256]{0:T(256)S(1)} %copy-done.23), custom_call_target="tpu_custom_call" | custom-call | tf_op jit(solution)/shard_map/pallas_call | solution.py:506
  24.6 3.1 %shard_map.204 = (bf16[32,2048]{1,0:T(8,128)(2,1)S(1)}, f32[8,2,128,128]{3,2,1,0:T(8,128)S(1)}) custom-call(s32[768]{0:T(1024)S(1)} %shard_map.202.tab, f32[2,32,128]{2,1,0:T(8,128)S(1)} %convolution_bitcast_fusion.1.qk, f32[2,32,256]{2,1,0:T(8,128)S(1)} %fusion.9.vz, f32[2,32,2]{2,1,0:T(8,128)S(1)} %convolution_bitcast_fusion.ba, f32[1,2]{1,0:T(1,128)S(1)} %bitcast.41, ...), custom_call_target="tpu_custom_call" | custom-call | tf_op jit(solution)/shard_map/pallas_call | solution.py:513
  29.3 7.1 %all-to-all-done.got = bf16[32,72,128]{2,1,0:T(8,128)(2,1)} async-done(((bf16[32,72,128]{2,1,0:T(8,128)(2,1)}), bf16[32,72,128]{2,1,0:T(8,128)(2,1)}, u32[]{:S(2)}, u32[]{:S(2)}) %all-to-all-start) | async-done | bytes 589856 | tf_op jit(solution)/shard_map/all_to_all | solution.py:504
  36.4 2.4 %shard_map.206 = bf16[32,72,128]{2,1,0:T(8,128)(2,1)} custom-call(s32[768]{0:T(1024)S(1)} %shard_map.202.tab, bf16[32,72,128]{2,1,0:T(8,128)(2,1)} %all-to-all-done.got, bf16[32,2048]{1,0:T(8,128)(2,1)S(1)} %get-tuple-element.15.early), custom_call_target="tpu_custom_call" | custom-call | tf_op jit(solution)/shard_map/pallas_call | solution.py:520
  38.7 4.1 %all-to-all-start.1 = ((bf16[32,72,128]{2,1,0:T(8,128)(2,1)}), bf16[32,72,128]{2,1,0:T(8,128)(2,1)S(1)}, u32[]{:S(2)}, u32[]{:S(2)}) async-start(bf16[32,72,128]{2,1,0:T(8,128)(2,1)} %shard_map.206), calls=%async_computation.1 | async-start | bytes 1179648 | tf_op jit(solution)/shard_map/all_to_all | solution.py:526
  42.9 1.7 %collective-permute-start.1 = (bf16[32,2048]{1,0:T(8,128)(2,1)S(1)}, bf16[32,2048]{1,0:T(8,128)(2,1)S(1)}, u32[]{:S(2)}, u32[]{:S(2)}) collective-permute-start(bf16[32,2048]{1,0:T(8,128)(2,1)S(1)} %add_convert_fusion.1), channel_id=1, source_target_pairs={{0,2},{1,3},{2,0},{3,1},{4,6},{5,7},{6,4},{7,5},{8,10},{9,11},{10,... | collective-permute-start | bytes 393224 | tf_op jit(solution)/shard_map/ppermute | solution.py:529
  45.1 3.4 %collective-permute-done.1 = bf16[32,2048]{1,0:T(8,128)(2,1)S(1)} collective-permute-done((bf16[32,2048]{1,0:T(8,128)(2,1)S(1)}, bf16[32,2048]{1,0:T(8,128)(2,1)S(1)}, u32[]{:S(2)}, u32[]{:S(2)}) %collective-permute-start.1) | collective-permute-done | bytes 131104 | tf_op jit(solution)/shard_map/ppermute | solution.py:529
  48.6 3.3 %collective-permute-start.2 = (bf16[32,2048]{1,0:T(8,128)(2,1)S(1)}, bf16[32,2048]{1,0:T(8,128)(2,1)}, u32[]{:S(2)}, u32[]{:S(2)}) collective-permute-start(bf16[32,2048]{1,0:T(8,128)(2,1)S(1)} %add_convert_fusion), channel_id=1, source_target_pairs={{0,4},{1,5},{2,6},{3,7},{4,0},{5,1},{6,2},{7,3},{8,12},{9,13},{10,... | collective-permute-start | bytes 393224 | tf_op jit(solution)/shard_map/ppermute | solution.py:529
  51.8 11.7 %all-to-all-done.1.got = bf16[32,72,128]{2,1,0:T(8,128)(2,1)S(1)} async-done(((bf16[32,72,128]{2,1,0:T(8,128)(2,1)}), bf16[32,72,128]{2,1,0:T(8,128)(2,1)S(1)}, u32[]{:S(2)}, u32[]{:S(2)}) %all-to-all-start.1) | async-done | bytes 589856 | tf_op jit(solution)/shard_map/all_to_all | solution.py:526
  63.7 1.6 %convolution_bitcast_fusion.3.qk_in = f32[2,16,128]{2,1,0:T(8,128)S(1)} fusion(bf16[2048,2,128]{2,1,0:T(2,128)(2,1)} %param.27, bf16[16,2048]{1,0:T(8,128)(2,1)S(1)} %get-tuple-element.16), kind=kOutput, calls=%fused_computation.12 | convolution fusion | flops 16777216 | bytes 1130496 | tf_op jit(solution)/shard_map/bd,dtc->tbc/dot_general | solution.py:486
  66.0 1.8 %shard_map.208 = (bf16[8,16,2048]{2,1,0:T(8,128)(2,1)S(1)}, f32[4,2,128,128]{3,2,1,0:T(8,128)S(1)}) custom-call(s32[768]{0:T(1024)S(1)} %shard_map.202.tab, f32[2,32,128]{2,1,0:T(8,128)S(1)} %convolution_bitcast_fusion.1.qk, f32[2,32,256]{2,1,0:T(8,128)S(1)} %fusion.9.vz, f32[2,32,2]{2,1,0:T(8,128)S(1)} %convolution_bitcast_fusion.ba, ...), custom_call_target="tpu_custom_call" | custom-call | tf_op jit(solution)/shard_map/pallas_call | solution.py:539
  68.6 4.5 %all-to-all-start.2 = ((bf16[8,16,2048]{2,1,0:T(8,128)(2,1)}), bf16[8,16,2048]{2,1,0:T(8,128)(2,1)}, u32[]{:S(2)}, u32[]{:S(2)}) async-start(bf16[8,16,2048]{2,1,0:T(8,128)(2,1)} %copy-done.9), calls=%async_computation.2 | async-start | bytes 1048576 | tf_op jit(solution)/shard_map/all_to_all | solution.py:550
  73.1 1.7 %convert_add_fusion.early = f32[32,2048]{1,0:T(8,128)} fusion(bf16[32,2048]{1,0:T(8,128)(2,1)} %collective-permute-done.2, bf16[32,2048]{1,0:T(8,128)(2,1)S(1)} %add_convert_fusion), kind=kLoop, calls=%fused_computation.15 | loop fusion | flops 196608 | bytes 524288 | tf_op jit(solution)/shard_map/add | solution.py:530
  75.9 1.7 %shard_map.209.done = f32[8,2,128,128]{3,2,1,0:T(8,128)} custom-call(s32[768]{0:T(1024)S(1)} %shard_map.202.tab, f32[8,2,128,128]{3,2,1,0:T(8,128)S(1)} %copy-done.7, f32[4,2,128,128]{3,2,1,0:T(8,128)S(1)} %get-tuple-element.17.late), custom_call_target="tpu_custom_call" | custom-call | tf_op jit(solution)/shard_map/pallas_call | solution.py:551
  77.6 4.4 %all-to-all-done.2.got = bf16[8,16,2048]{2,1,0:T(8,128)(2,1)} async-done(((bf16[8,16,2048]{2,1,0:T(8,128)(2,1)}), bf16[8,16,2048]{2,1,0:T(8,128)(2,1)}, u32[]{:S(2)}, u32[]{:S(2)}) %all-to-all-start.2) | async-done | bytes 524320 | tf_op jit(solution)/shard_map/all_to_all | solution.py:550
  82.1 2.8 %shard_map.210 = (f32[32,2048]{1,0:T(8,128)}, bf16[48,2048]{1,0:T(8,128)(2,1)}, bf16[8,32,256]{2,1,0:T(8,128)(2,1)}) custom-call(s32[768]{0:T(1024)} %copy-done.11, f32[8,2,128,128]{3,2,1,0:T(8,128)} %shard_map.209.done, bf16[4,8,2048]{2,1,0:T(8,128)(2,1)} %tokens.5, f32[32,2048]{1,0:T(8,128)} %convert_add_fusion.early, f32[16,2048]{1,0:T(8,128)} %copy-done.13, ...), custom_call_target="tpu_custom_call" | custom-call | tf_op jit(solution)/shard_map/pallas_call | solution.py:554
  84.9 3.5 %all-to-all-start.3 = ((bf16[8,32,256]{2,1,0:T(8,128)(2,1)}), bf16[8,32,256]{2,1,0:T(8,128)(2,1)S(1)}, u32[]{:S(2)}, u32[]{:S(2)}) async-start(bf16[8,32,256]{2,1,0:T(8,128)(2,1)} %get-tuple-element.21), calls=%async_computation.3 | async-start | bytes 262144 | tf_op jit(solution)/shard_map/all_to_all | solution.py:561
  88.4 2.2 %fusion.6.kv = f32[2,48,256]{2,1,0:T(8,128)S(1)} fusion(bf16[2048,2,256]{2,1,0:T(2,128)(2,1)} %param.36, bf16[48,2048]{1,0:T(8,128)(2,1)} %get-tuple-element.22), kind=kOutput, calls=%fused_computation.6 | convolution fusion | flops 100663296 | bytes 2392064 | tf_op jit(solution)/shard_map/bd,dtc->tbc/dot_general | solution.py:562
  90.5 4.4 %all-to-all-done.3.query = bf16[8,32,256]{2,1,0:T(8,128)(2,1)S(1)} async-done(((bf16[8,32,256]{2,1,0:T(8,128)(2,1)}), bf16[8,32,256]{2,1,0:T(8,128)(2,1)S(1)}, u32[]{:S(2)}, u32[]{:S(2)}) %all-to-all-start.3) | async-done | bytes 131104 | tf_op jit(solution)/shard_map/all_to_all | solution.py:561
  95.0 3.5 %shard_map.211 = (bf16[8,32,384]{2,1,0:T(8,128)(2,1)S(1)}, bf16[64,2,8,256]{3,2,1,0:T(8,128)(2,1)}) custom-call(s32[2]{0:T(128)S(1)} %pad_add_fusion.place, s32[8,8]{1,0:T(8,128)S(1)} %copy-done.15, s32[768]{0:T(1024)S(1)} %copy-done.12, bf16[64,2,8,256]{3,2,1,0:T(8,128)(2,1)S(1)} %copy-done.4, bf16[32,72,128]{2,1,0:T(8,128)(2,1)S(1)} %all-to-all-done.1.got, ...), custom_call_target="tpu_custom_call" | custom-call | tf_op jit(solution)/shard_map/pallas_call | solution.py:563
  98.5 9.3 %all_to_all.30.got = bf16[8,32,384]{2,1,0:T(8,128)(2,1)S(1)} all-to-all(bf16[8,32,384]{2,1,0:T(8,128)(2,1)S(1)} %get-tuple-element.23), channel_id=1, replica_groups=mesh['inst'=32,'tp'=8] {'tp'}, dimensions={0} | all-to-all | bytes 393216 | tf_op jit(solution)/shard_map/all_to_all | solution.py:575
  108.3 14.0 %all_to_all.31.got = bf16[8,32,2048]{2,1,0:T(8,128)(2,1)S(1)} all-to-all(bf16[8,32,2048]{2,1,0:T(8,128)(2,1)S(1)} %shard_map.212), channel_id=1, replica_groups=mesh['inst'=32,'tp'=8] {'tp'}, dimensions={0} | all-to-all | bytes 2097152 | tf_op jit(solution)/shard_map/all_to_all | solution.py:577
  (73 shorter events, 10.8 us)
Async XLA Ops:
  0.6 21.5 %copy-start = (bf16[2048,2,256]{2,1,0:T(2,128)(2,1)S(1)}, bf16[2048,2,256]{2,1,0:T(2,128)(2,1)}, u32[]{:S(2)}) copy-start(bf16[2048,2,256]{2,1,0:T(2,128)(2,1)} %param.28) | copy-start | bytes 6291460
  0.6 15.2 %copy-start.14 = (s32[4,16,4]{1,2,0:T(4,128)S(1)}, s32[4,16,4]{1,2,0:T(4,128)}, u32[]{:S(2)}) copy-start(s32[4,16,4]{1,2,0:T(4,128)} %param.24) | copy-start | bytes 3076
  0.7 14.9 %copy-start.5 = (bf16[4,8,2048]{2,1,0:T(8,128)(2,1)S(1)}, bf16[4,8,2048]{2,1,0:T(8,128)(2,1)}, u32[]{:S(2)}) copy-start(bf16[4,8,2048]{2,1,0:T(8,128)(2,1)} %tokens.5) | copy-start | bytes 393220
  0.7 14.9 %copy-start.24 = (bf16[2048]{0:T(1024)(128)(2,1)S(1)}, bf16[2048]{0:T(1024)(128)(2,1)}, u32[]{:S(2)}) copy-start(bf16[2048]{0:T(1024)(128)(2,1)} %param.25) | copy-start | bytes 12292
  0.7 15.1 %copy-start.23 = (s32[256]{0:T(256)S(1)}, s32[256]{0:T(256)}, u32[]{:S(2)}) copy-start(s32[256]{0:T(256)} %lens.1) | copy-start | bytes 3076
  0.7 19.7 %copy-start.26 = (bf16[2048,2,2]{0,2,1:T(2,128)(2,1)S(1)}, bf16[2048,2,2]{0,2,1:T(2,128)(2,1)}, u32[]{:S(2)}) copy-start(bf16[2048,2,2]{0,2,1:T(2,128)(2,1)} %param.29) | copy-start | bytes 49156
  4.3 32.1 %all-to-all-start = ((bf16[32,72,128]{2,1,0:T(8,128)(2,1)}), bf16[32,72,128]{2,1,0:T(8,128)(2,1)}, u32[]{:S(2)}, u32[]{:S(2)}) async-start(bf16[32,72,128]{2,1,0:T(8,128)(2,1)} %shard_map.205), calls=%async_computation | async-start | bytes 1179648 | tf_op jit(solution)/shard_map/all_to_all | solution.py:504
  20.4 54.4 %copy-start.11 = (s32[768]{0:T(1024)}, s32[768]{0:T(1024)S(1)}, u32[]{:S(2)}) copy-start(s32[768]{0:T(1024)S(1)} %shard_map.202.tab) | copy-start | bytes 9220
  28.7 15.8 %copy-start.25 = (bf16[2048]{0:T(1024)(128)(2,1)S(1)}, bf16[2048]{0:T(1024)(128)(2,1)}, u32[]{:S(2)}) copy-start(bf16[2048]{0:T(1024)(128)(2,1)} %param.33) | copy-start | bytes 12292
  28.7 14.1 %collective-permute-start = (bf16[32,2048]{1,0:T(8,128)(2,1)S(1)}, bf16[32,2048]{1,0:T(8,128)(2,1)S(1)}, u32[]{:S(2)}, u32[]{:S(2)}) collective-permute-start(bf16[32,2048]{1,0:T(8,128)(2,1)S(1)} %get-tuple-element.15.early), channel_id=1, source_target_pairs={{0,1},{1,0},{2,3},{3,2},{4,5},{5,4},{6,7},{7,6},{8,9},{9,8},{10,11... | collective-permute-start | bytes 393224 | tf_op jit(solution)/shard_map/ppermute | solution.py:529
  38.7 24.8 %all-to-all-start.1 = ((bf16[32,72,128]{2,1,0:T(8,128)(2,1)}), bf16[32,72,128]{2,1,0:T(8,128)(2,1)S(1)}, u32[]{:S(2)}, u32[]{:S(2)}) async-start(bf16[32,72,128]{2,1,0:T(8,128)(2,1)} %shard_map.206), calls=%async_computation.1 | async-start | bytes 1179648 | tf_op jit(solution)/shard_map/all_to_all | solution.py:526
  42.9 5.6 %collective-permute-start.1 = (bf16[32,2048]{1,0:T(8,128)(2,1)S(1)}, bf16[32,2048]{1,0:T(8,128)(2,1)S(1)}, u32[]{:S(2)}, u32[]{:S(2)}) collective-permute-start(bf16[32,2048]{1,0:T(8,128)(2,1)S(1)} %add_convert_fusion.1), channel_id=1, source_target_pairs={{0,2},{1,3},{2,0},{3,1},{4,6},{5,7},{6,4},{7,5},{8,10},{9,11},{10,... | collective-permute-start | bytes 393224 | tf_op jit(solution)/shard_map/ppermute | solution.py:529
  45.1 20.6 %copy-start.27 = (bf16[2048,2,2]{0,2,1:T(2,128)(2,1)S(1)}, bf16[2048,2,2]{0,2,1:T(2,128)(2,1)}, u32[]{:S(2)}) copy-start(bf16[2048,2,2]{0,2,1:T(2,128)(2,1)} %param.29) | copy-start | bytes 49156
  48.5 17.4 %copy-start.18 = (f32[2]{0:T(128)S(1)}, f32[2]{0:T(128)}, u32[]{:S(2)}) copy-start(f32[2]{0:T(128)} %param.30) | copy-start | bytes 28
  48.5 17.4 %copy-start.20 = (f32[2]{0:T(128)S(1)}, f32[2]{0:T(128)}, u32[]{:S(2)}) copy-start(f32[2]{0:T(128)} %param.31) | copy-start | bytes 28
  48.6 17.4 %copy-start.22 = (bf16[128]{0:T(256)(128)(2,1)S(1)}, bf16[128]{0:T(256)(128)(2,1)}, u32[]{:S(2)}) copy-start(bf16[128]{0:T(256)(128)(2,1)} %param.26) | copy-start | bytes 772
  48.6 24.5 %collective-permute-start.2 = (bf16[32,2048]{1,0:T(8,128)(2,1)S(1)}, bf16[32,2048]{1,0:T(8,128)(2,1)}, u32[]{:S(2)}, u32[]{:S(2)}) collective-permute-start(bf16[32,2048]{1,0:T(8,128)(2,1)S(1)} %add_convert_fusion), channel_id=1, source_target_pairs={{0,4},{1,5},{2,6},{3,7},{4,0},{5,1},{6,2},{7,3},{8,12},{9,13},{10,... | collective-permute-start | bytes 393224 | tf_op jit(solution)/shard_map/ppermute | solution.py:529
  68.6 13.5 %all-to-all-start.2 = ((bf16[8,16,2048]{2,1,0:T(8,128)(2,1)}), bf16[8,16,2048]{2,1,0:T(8,128)(2,1)}, u32[]{:S(2)}, u32[]{:S(2)}) async-start(bf16[8,16,2048]{2,1,0:T(8,128)(2,1)} %copy-done.9), calls=%async_computation.2 | async-start | bytes 1048576 | tf_op jit(solution)/shard_map/all_to_all | solution.py:550
  84.8 10.2 %copy-start.4 = (bf16[64,2,8,256]{3,2,1,0:T(8,128)(2,1)S(1)}, bf16[64,2,8,256]{3,2,1,0:T(8,128)(2,1)}, u32[]{:S(2)}) copy-start(bf16[64,2,8,256]{3,2,1,0:T(8,128)(2,1)} %pages.3) | copy-start | bytes 1572868
  84.8 10.2 %copy-start.12 = (s32[768]{0:T(1024)S(1)}, s32[768]{0:T(1024)}, u32[]{:S(2)}) copy-start(s32[768]{0:T(1024)} %copy-done.11) | copy-start | bytes 9220
  84.8 10.2 %copy-start.15 = (s32[8,8]{1,0:T(8,128)S(1)}, s32[8,8]{1,0:T(8,128)}, u32[]{:S(2)}) copy-start(s32[8,8]{1,0:T(8,128)} %table.3) | copy-start | bytes 772
  84.9 10.1 %all-to-all-start.3 = ((bf16[8,32,256]{2,1,0:T(8,128)(2,1)}), bf16[8,32,256]{2,1,0:T(8,128)(2,1)S(1)}, u32[]{:S(2)}, u32[]{:S(2)}) async-start(bf16[8,32,256]{2,1,0:T(8,128)(2,1)} %get-tuple-element.21), calls=%async_computation.3 | async-start | bytes 262144 | tf_op jit(solution)/shard_map/all_to_all | solution.py:561
  95.0 12.8 %copy-start.8 = (bf16[256,2048]{1,0:T(8,128)(2,1)S(1)}, bf16[256,2048]{1,0:T(8,128)(2,1)}, u32[]{:S(2)}) copy-start(bf16[256,2048]{1,0:T(8,128)(2,1)} %w_o.1) | copy-start | bytes 3145732
  107.9 14.4 %copy-start.10 = (f32[32,2048]{1,0:T(8,128)S(1)}, f32[32,2048]{1,0:T(8,128)}, u32[]{:S(2)}) copy-start(f32[32,2048]{1,0:T(8,128)} %get-tuple-element.20.hidden) | copy-start | bytes 786436
  (11 other events, 33.8 us)

commit v5 on v4

--- a/solution.py
+++ b/solution.py
@@ -61,33 +61,31 @@
     return values * lax.rsqrt(jnp.sum(values * values, axis=-1, keepdims=True) + 1e-06)
 
 
-def own_slots(moves, me):
-    slots = []
-    for s in range(STEPS):
-        slot = jnp.int32(0)
-        for p in range(16):
-            slot = jnp.where(moves[s, 0, p] == me, moves[s, 1, p], slot)
-            slot = jnp.where(moves[s, 2, p] == me, moves[s, 3, p], slot)
-        slots.append(slot)
-    return slots
+def own_slot(moves, me, s):
+    slot = jnp.int32(0)
+    for p in range(16):
+        slot = jnp.where(moves[s, 0, p] == me, moves[s, 1, p], slot)
+        slot = jnp.where(moves[s, 2, p] == me, moves[s, 3, p], slot)
+    return slot
 
 
 def pack_kernel(
     moves, table, state, pages, tokens, out, st_scr, pg_scr, bf_scr, tok_scr, row_scr, sem
 ):
-    slots = own_slots(moves, lax.axis_index("inst"))
     token_copy = pltpu.make_async_copy(tokens, bf_scr, sem.at[36])
     token_copy.start()
-    copies = []
-    for s in range(STEPS):
+    me = lax.axis_index("inst")
+    copies, slots = [], []
+    for s in range(STEPS):
+        slots.append(own_slot(moves, me, s))
         copies.append(pltpu.make_async_copy(state.at[slots[s]], st_scr.at[s], sem.at[32 + s]))
         for j in range(8):
             at = s * 8 + j
             copies.append(
                 pltpu.make_async_copy(pages.at[table[slots[s], j]], pg_scr.at[at], sem.at[at])
             )
-    for copy in copies:
-        copy.start()
+        for copy in copies[s * 9 :]:
+            copy.start()
     token_copy.wait()
     for s in range(STEPS):
         tok_scr[s * 8 : s * 8 + 8, :] = bf_scr[s].astype(F32)

time: 125 us -> 125 us (level)
  no operation moved by 1% of the time
where the time goes in v5:
time: 125 us; the launch traced here: 123 us
  waiting for transfers between devices  31.1 us (25%)
  starting transfers between devices  28.9 us (23%)
  Pallas kernels  25 us (20%)
  blocking collectives  23.3 us (19%)
  matrix products  6.67 us (5%)
  local copies, waits for them, and re-layouts  5.72 us (5%)
  other arithmetic  1.8 us (1%)
    all_to_all x1, blocking collectives, body(): parts = lax.all_to_all(part, 'tp', 0, 0)  14 us
    all_to_all x1, waiting for transfers between devices, body(): got = lax.all_to_all(picked, 'inst', 0, 0)  11.7 us
    all_to_all x1, starting transfers between devices, body(): got = lax.all_to_all(packed, 'inst', 0, 0)  11.2 us
    all_to_all x1, blocking collectives, body(): shares = lax.all_to_all(shares, 'tp', 0, 0)  9.35 us
    all_to_all x1, waiting for transfers between devices, body(): got = lax.all_to_all(packed, 'inst', 0, 0)  7.09 us
    ppermute x3, starting transfers between devices, body(): other = lax.ppermute(early, 'tp', [(i, i ^ bit) for i in range(PARTS)])  5.54 us
    unnamed x56, local copies, waits for them, and re-layouts  5.11 us
    pallas_call x1, Pallas kernels, body(): call(table_kernel, [SMEM] * 3, [shape((T_SIZE,), jnp.int32)], out_specs=[...  4.51 us
  transfers between devices with their start and end apart: 7, of which 5 were waited for; matrix products, arithmetic and copies ran while one was open for 7% of the time, Pallas kernels for 11%

profile of v5, /device:TPU:32, one launch (start us, length us, event | category | flops | bytes accessed | tf_op | source)
XLA Modules:
  0.0 123.4 jit_solution(13606724229482302785)
XLA Ops:
  0.7 3.6 %shard_map.205 = bf16[32,72,128]{2,1,0:T(8,128)(2,1)} custom-call(s32[4,4,16]{2,1,0:T(4,128)} %bitcast.39, s32[8,8]{1,0:T(8,128)} %table.3, f32[8,2,128,128]{3,2,1,0:T(8,128)} %state.3, bf16[64,2,8,256]{3,2,1,0:T(8,128)(2,1)} %pages.3, bf16[4,8,2048]{2,1,0:T(8,128)(2,1)} %tokens.5), custom_call_target="tpu_custom_call" | custom-call | tf_op jit(solution)/shard_map/pallas_call | solution.py:488
  4.3 11.2 %all-to-all-start = ((bf16[32,72,128]{2,1,0:T(8,128)(2,1)}), bf16[32,72,128]{2,1,0:T(8,128)(2,1)}, u32[]{:S(2)}, u32[]{:S(2)}) async-start(bf16[32,72,128]{2,1,0:T(8,128)(2,1)} %shard_map.205), calls=%async_computation | async-start | bytes 1179648 | tf_op jit(solution)/shard_map/all_to_all | solution.py:502
  15.8 4.5 %shard_map.202.tab = s32[768]{0:T(1024)S(1)} custom-call(s32[4,4,16]{2,1,0:T(4,128)S(1)} %bitcast.40, s32[2]{0:T(128)S(1)} %pad_add_fusion.place, s32[256]{0:T(256)S(1)} %copy-done.23), custom_call_target="tpu_custom_call" | custom-call | tf_op jit(solution)/shard_map/pallas_call | solution.py:504
  24.6 3.1 %shard_map.204 = (bf16[32,2048]{1,0:T(8,128)(2,1)S(1)}, f32[8,2,128,128]{3,2,1,0:T(8,128)S(1)}) custom-call(s32[768]{0:T(1024)S(1)} %shard_map.202.tab, f32[2,32,128]{2,1,0:T(8,128)S(1)} %convolution_bitcast_fusion.1.qk, f32[2,32,256]{2,1,0:T(8,128)S(1)} %fusion.9.vz, f32[2,32,2]{2,1,0:T(8,128)S(1)} %convolution_bitcast_fusion.ba, f32[1,2]{1,0:T(1,128)S(1)} %bitcast.41, ...), custom_call_target="tpu_custom_call" | custom-call | tf_op jit(solution)/shard_map/pallas_call | solution.py:511
  29.3 7.1 %all-to-all-done.got = bf16[32,72,128]{2,1,0:T(8,128)(2,1)} async-done(((bf16[32,72,128]{2,1,0:T(8,128)(2,1)}), bf16[32,72,128]{2,1,0:T(8,128)(2,1)}, u32[]{:S(2)}, u32[]{:S(2)}) %all-to-all-start) | async-done | bytes 589856 | tf_op jit(solution)/shard_map/all_to_all | solution.py:502
  36.4 2.4 %shard_map.206 = bf16[32,72,128]{2,1,0:T(8,128)(2,1)} custom-call(s32[768]{0:T(1024)S(1)} %shard_map.202.tab, bf16[32,72,128]{2,1,0:T(8,128)(2,1)} %all-to-all-done.got, bf16[32,2048]{1,0:T(8,128)(2,1)S(1)} %get-tuple-element.15.early), custom_call_target="tpu_custom_call" | custom-call | tf_op jit(solution)/shard_map/pallas_call | solution.py:518
  38.7 4.1 %all-to-all-start.1 = ((bf16[32,72,128]{2,1,0:T(8,128)(2,1)}), bf16[32,72,128]{2,1,0:T(8,128)(2,1)S(1)}, u32[]{:S(2)}, u32[]{:S(2)}) async-start(bf16[32,72,128]{2,1,0:T(8,128)(2,1)} %shard_map.206), calls=%async_computation.1 | async-start | bytes 1179648 | tf_op jit(solution)/shard_map/all_to_all | solution.py:524
  42.9 1.7 %collective-permute-start.1 = (bf16[32,2048]{1,0:T(8,128)(2,1)S(1)}, bf16[32,2048]{1,0:T(8,128)(2,1)S(1)}, u32[]{:S(2)}, u32[]{:S(2)}) collective-permute-start(bf16[32,2048]{1,0:T(8,128)(2,1)S(1)} %add_convert_fusion.1), channel_id=1, source_target_pairs={{0,2},{1,3},{2,0},{3,1},{4,6},{5,7},{6,4},{7,5},{8,10},{9,11},{10,... | collective-permute-start | bytes 393224 | tf_op jit(solution)/shard_map/ppermute | solution.py:527
  45.1 3.4 %collective-permute-done.1 = bf16[32,2048]{1,0:T(8,128)(2,1)S(1)} collective-permute-done((bf16[32,2048]{1,0:T(8,128)(2,1)S(1)}, bf16[32,2048]{1,0:T(8,128)(2,1)S(1)}, u32[]{:S(2)}, u32[]{:S(2)}) %collective-permute-start.1) | collective-permute-done | bytes 131104 | tf_op jit(solution)/shard_map/ppermute | solution.py:527
  48.6 3.3 %collective-permute-start.2 = (bf16[32,2048]{1,0:T(8,128)(2,1)S(1)}, bf16[32,2048]{1,0:T(8,128)(2,1)}, u32[]{:S(2)}, u32[]{:S(2)}) collective-permute-start(bf16[32,2048]{1,0:T(8,128)(2,1)S(1)} %add_convert_fusion), channel_id=1, source_target_pairs={{0,4},{1,5},{2,6},{3,7},{4,0},{5,1},{6,2},{7,3},{8,12},{9,13},{10,... | collective-permute-start | bytes 393224 | tf_op jit(solution)/shard_map/ppermute | solution.py:527
  51.8 11.7 %all-to-all-done.1.got = bf16[32,72,128]{2,1,0:T(8,128)(2,1)S(1)} async-done(((bf16[32,72,128]{2,1,0:T(8,128)(2,1)}), bf16[32,72,128]{2,1,0:T(8,128)(2,1)S(1)}, u32[]{:S(2)}, u32[]{:S(2)}) %all-to-all-start.1) | async-done | bytes 589856 | tf_op jit(solution)/shard_map/all_to_all | solution.py:524
  63.7 1.6 %convolution_bitcast_fusion.3.qk_in = f32[2,16,128]{2,1,0:T(8,128)S(1)} fusion(bf16[2048,2,128]{2,1,0:T(2,128)(2,1)} %param.27, bf16[16,2048]{1,0:T(8,128)(2,1)S(1)} %get-tuple-element.16), kind=kOutput, calls=%fused_computation.12 | convolution fusion | flops 16777216 | bytes 1130496 | tf_op jit(solution)/shard_map/bd,dtc->tbc/dot_general | solution.py:484
  66.0 2.0 %shard_map.208 = (bf16[8,16,2048]{2,1,0:T(8,128)(2,1)S(1)}, f32[4,2,128,128]{3,2,1,0:T(8,128)S(1)}) custom-call(s32[768]{0:T(1024)S(1)} %shard_map.202.tab, f32[2,32,128]{2,1,0:T(8,128)S(1)} %convolution_bitcast_fusion.1.qk, f32[2,32,256]{2,1,0:T(8,128)S(1)} %fusion.9.vz, f32[2,32,2]{2,1,0:T(8,128)S(1)} %convolution_bitcast_fusion.ba, ...), custom_call_target="tpu_custom_call" | custom-call | tf_op jit(solution)/shard_map/pallas_call | solution.py:537
  68.8 4.5 %all-to-all-start.2 = ((bf16[8,16,2048]{2,1,0:T(8,128)(2,1)}), bf16[8,16,2048]{2,1,0:T(8,128)(2,1)}, u32[]{:S(2)}, u32[]{:S(2)}) async-start(bf16[8,16,2048]{2,1,0:T(8,128)(2,1)} %copy-done.9), calls=%async_computation.2 | async-start | bytes 1048576 | tf_op jit(solution)/shard_map/all_to_all | solution.py:548
  73.4 1.7 %convert_add_fusion.early = f32[32,2048]{1,0:T(8,128)} fusion(bf16[32,2048]{1,0:T(8,128)(2,1)} %collective-permute-done.2, bf16[32,2048]{1,0:T(8,128)(2,1)S(1)} %add_convert_fusion), kind=kLoop, calls=%fused_computation.15 | loop fusion | flops 196608 | bytes 524288 | tf_op jit(solution)/shard_map/add | solution.py:528
  76.2 1.7 %shard_map.209.done = f32[8,2,128,128]{3,2,1,0:T(8,128)} custom-call(s32[768]{0:T(1024)S(1)} %shard_map.202.tab, f32[8,2,128,128]{3,2,1,0:T(8,128)S(1)} %copy-done.7, f32[4,2,128,128]{3,2,1,0:T(8,128)S(1)} %get-tuple-element.17.late), custom_call_target="tpu_custom_call" | custom-call | tf_op jit(solution)/shard_map/pallas_call | solution.py:549
  77.9 4.5 %all-to-all-done.2.got = bf16[8,16,2048]{2,1,0:T(8,128)(2,1)} async-done(((bf16[8,16,2048]{2,1,0:T(8,128)(2,1)}), bf16[8,16,2048]{2,1,0:T(8,128)(2,1)}, u32[]{:S(2)}, u32[]{:S(2)}) %all-to-all-start.2) | async-done | bytes 524320 | tf_op jit(solution)/shard_map/all_to_all | solution.py:548
  82.4 2.8 %shard_map.210 = (f32[32,2048]{1,0:T(8,128)}, bf16[48,2048]{1,0:T(8,128)(2,1)}, bf16[8,32,256]{2,1,0:T(8,128)(2,1)}) custom-call(s32[768]{0:T(1024)} %copy-done.11, f32[8,2,128,128]{3,2,1,0:T(8,128)} %shard_map.209.done, bf16[4,8,2048]{2,1,0:T(8,128)(2,1)} %tokens.5, f32[32,2048]{1,0:T(8,128)} %convert_add_fusion.early, f32[16,2048]{1,0:T(8,128)} %copy-done.13, ...), custom_call_target="tpu_custom_call" | custom-call | tf_op jit(solution)/shard_map/pallas_call | solution.py:552
  85.2 3.5 %all-to-all-start.3 = ((bf16[8,32,256]{2,1,0:T(8,128)(2,1)}), bf16[8,32,256]{2,1,0:T(8,128)(2,1)S(1)}, u32[]{:S(2)}, u32[]{:S(2)}) async-start(bf16[8,32,256]{2,1,0:T(8,128)(2,1)} %get-tuple-element.21), calls=%async_computation.3 | async-start | bytes 262144 | tf_op jit(solution)/shard_map/all_to_all | solution.py:559
  88.7 2.2 %fusion.6.kv = f32[2,48,256]{2,1,0:T(8,128)S(1)} fusion(bf16[2048,2,256]{2,1,0:T(2,128)(2,1)} %param.36, bf16[48,2048]{1,0:T(8,128)(2,1)} %get-tuple-element.22), kind=kOutput, calls=%fused_computation.6 | convolution fusion | flops 100663296 | bytes 2392064 | tf_op jit(solution)/shard_map/bd,dtc->tbc/dot_general | solution.py:560
  90.9 4.4 %all-to-all-done.3.query = bf16[8,32,256]{2,1,0:T(8,128)(2,1)S(1)} async-done(((bf16[8,32,256]{2,1,0:T(8,128)(2,1)}), bf16[8,32,256]{2,1,0:T(8,128)(2,1)S(1)}, u32[]{:S(2)}, u32[]{:S(2)}) %all-to-all-start.3) | async-done | bytes 131104 | tf_op jit(solution)/shard_map/all_to_all | solution.py:559
  95.4 3.5 %shard_map.211 = (bf16[8,32,384]{2,1,0:T(8,128)(2,1)S(1)}, bf16[64,2,8,256]{3,2,1,0:T(8,128)(2,1)}) custom-call(s32[2]{0:T(128)S(1)} %pad_add_fusion.place, s32[8,8]{1,0:T(8,128)S(1)} %copy-done.15, s32[768]{0:T(1024)S(1)} %copy-done.12, bf16[64,2,8,256]{3,2,1,0:T(8,128)(2,1)S(1)} %copy-done.4, bf16[32,72,128]{2,1,0:T(8,128)(2,1)S(1)} %all-to-all-done.1.got, ...), custom_call_target="tpu_custom_call" | custom-call | tf_op jit(solution)/shard_map/pallas_call | solution.py:561
  98.8 9.3 %all_to_all.30.got = bf16[8,32,384]{2,1,0:T(8,128)(2,1)S(1)} all-to-all(bf16[8,32,384]{2,1,0:T(8,128)(2,1)S(1)} %get-tuple-element.23), channel_id=1, replica_groups=mesh['inst'=32,'tp'=8] {'tp'}, dimensions={0} | all-to-all | bytes 393216 | tf_op jit(solution)/shard_map/all_to_all | solution.py:573
  108.6 14.0 %all_to_all.31.got = bf16[8,32,2048]{2,1,0:T(8,128)(2,1)S(1)} all-to-all(bf16[8,32,2048]{2,1,0:T(8,128)(2,1)S(1)} %shard_map.212), channel_id=1, replica_groups=mesh['inst'=32,'tp'=8] {'tp'}, dimensions={0} | all-to-all | bytes 2097152 | tf_op jit(solution)/shard_map/all_to_all | solution.py:575
  (73 shorter events, 10.8 us)
Async XLA Ops:
  0.6 21.5 %copy-start = (bf16[2048,2,256]{2,1,0:T(2,128)(2,1)S(1)}, bf16[2048,2,256]{2,1,0:T(2,128)(2,1)}, u32[]{:S(2)}) copy-start(bf16[2048,2,256]{2,1,0:T(2,128)(2,1)} %param.28) | copy-start | bytes 6291460
  0.6 15.2 %copy-start.14 = (s32[4,16,4]{1,2,0:T(4,128)S(1)}, s32[4,16,4]{1,2,0:T(4,128)}, u32[]{:S(2)}) copy-start(s32[4,16,4]{1,2,0:T(4,128)} %param.24) | copy-start | bytes 3076
  0.7 14.9 %copy-start.5 = (bf16[4,8,2048]{2,1,0:T(8,128)(2,1)S(1)}, bf16[4,8,2048]{2,1,0:T(8,128)(2,1)}, u32[]{:S(2)}) copy-start(bf16[4,8,2048]{2,1,0:T(8,128)(2,1)} %tokens.5) | copy-start | bytes 393220
  0.7 14.9 %copy-start.24 = (bf16[2048]{0:T(1024)(128)(2,1)S(1)}, bf16[2048]{0:T(1024)(128)(2,1)}, u32[]{:S(2)}) copy-start(bf16[2048]{0:T(1024)(128)(2,1)} %param.25) | copy-start | bytes 12292
  0.7 15.1 %copy-start.23 = (s32[256]{0:T(256)S(1)}, s32[256]{0:T(256)}, u32[]{:S(2)}) copy-start(s32[256]{0:T(256)} %lens.1) | copy-start | bytes 3076
  0.7 19.7 %copy-start.26 = (bf16[2048,2,2]{0,2,1:T(2,128)(2,1)S(1)}, bf16[2048,2,2]{0,2,1:T(2,128)(2,1)}, u32[]{:S(2)}) copy-start(bf16[2048,2,2]{0,2,1:T(2,128)(2,1)} %param.29) | copy-start | bytes 49156
  4.3 32.1 %all-to-all-start = ((bf16[32,72,128]{2,1,0:T(8,128)(2,1)}), bf16[32,72,128]{2,1,0:T(8,128)(2,1)}, u32[]{:S(2)}, u32[]{:S(2)}) async-start(bf16[32,72,128]{2,1,0:T(8,128)(2,1)} %shard_map.205), calls=%async_computation | async-start | bytes 1179648 | tf_op jit(solution)/shard_map/all_to_all | solution.py:502
  20.4 54.7 %copy-start.11 = (s32[768]{0:T(1024)}, s32[768]{0:T(1024)S(1)}, u32[]{:S(2)}) copy-start(s32[768]{0:T(1024)S(1)} %shard_map.202.tab) | copy-start | bytes 9220
  28.7 15.8 %copy-start.25 = (bf16[2048]{0:T(1024)(128)(2,1)S(1)}, bf16[2048]{0:T(1024)(128)(2,1)}, u32[]{:S(2)}) copy-start(bf16[2048]{0:T(1024)(128)(2,1)} %param.33) | copy-start | bytes 12292
  28.7 14.1 %collective-permute-start = (bf16[32,2048]{1,0:T(8,128)(2,1)S(1)}, bf16[32,2048]{1,0:T(8,128)(2,1)S(1)}, u32[]{:S(2)}, u32[]{:S(2)}) collective-permute-start(bf16[32,2048]{1,0:T(8,128)(2,1)S(1)} %get-tuple-element.15.early), channel_id=1, source_target_pairs={{0,1},{1,0},{2,3},{3,2},{4,5},{5,4},{6,7},{7,6},{8,9},{9,8},{10,11... | collective-permute-start | bytes 393224 | tf_op jit(solution)/shard_map/ppermute | solution.py:527
  38.7 24.8 %all-to-all-start.1 = ((bf16[32,72,128]{2,1,0:T(8,128)(2,1)}), bf16[32,72,128]{2,1,0:T(8,128)(2,1)S(1)}, u32[]{:S(2)}, u32[]{:S(2)}) async-start(bf16[32,72,128]{2,1,0:T(8,128)(2,1)} %shard_map.206), calls=%async_computation.1 | async-start | bytes 1179648 | tf_op jit(solution)/shard_map/all_to_all | solution.py:524
  42.9 5.6 %collective-permute-start.1 = (bf16[32,2048]{1,0:T(8,128)(2,1)S(1)}, bf16[32,2048]{1,0:T(8,128)(2,1)S(1)}, u32[]{:S(2)}, u32[]{:S(2)}) collective-permute-start(bf16[32,2048]{1,0:T(8,128)(2,1)S(1)} %add_convert_fusion.1), channel_id=1, source_target_pairs={{0,2},{1,3},{2,0},{3,1},{4,6},{5,7},{6,4},{7,5},{8,10},{9,11},{10,... | collective-permute-start | bytes 393224 | tf_op jit(solution)/shard_map/ppermute | solution.py:527
  45.1 20.6 %copy-start.27 = (bf16[2048,2,2]{0,2,1:T(2,128)(2,1)S(1)}, bf16[2048,2,2]{0,2,1:T(2,128)(2,1)}, u32[]{:S(2)}) copy-start(bf16[2048,2,2]{0,2,1:T(2,128)(2,1)} %param.29) | copy-start | bytes 49156
  48.5 17.4 %copy-start.18 = (f32[2]{0:T(128)S(1)}, f32[2]{0:T(128)}, u32[]{:S(2)}) copy-start(f32[2]{0:T(128)} %param.30) | copy-start | bytes 28
  48.5 17.4 %copy-start.20 = (f32[2]{0:T(128)S(1)}, f32[2]{0:T(128)}, u32[]{:S(2)}) copy-start(f32[2]{0:T(128)} %param.31) | copy-start | bytes 28
  48.6 17.4 %copy-start.22 = (bf16[128]{0:T(256)(128)(2,1)S(1)}, bf16[128]{0:T(256)(128)(2,1)}, u32[]{:S(2)}) copy-start(bf16[128]{0:T(256)(128)(2,1)} %param.26) | copy-start | bytes 772
  48.6 24.8 %collective-permute-start.2 = (bf16[32,2048]{1,0:T(8,128)(2,1)S(1)}, bf16[32,2048]{1,0:T(8,128)(2,1)}, u32[]{:S(2)}, u32[]{:S(2)}) collective-permute-start(bf16[32,2048]{1,0:T(8,128)(2,1)S(1)} %add_convert_fusion), channel_id=1, source_target_pairs={{0,4},{1,5},{2,6},{3,7},{4,0},{5,1},{6,2},{7,3},{8,12},{9,13},{10,... | collective-permute-start | bytes 393224 | tf_op jit(solution)/shard_map/ppermute | solution.py:527
  68.8 13.5 %all-to-all-start.2 = ((bf16[8,16,2048]{2,1,0:T(8,128)(2,1)}), bf16[8,16,2048]{2,1,0:T(8,128)(2,1)}, u32[]{:S(2)}, u32[]{:S(2)}) async-start(bf16[8,16,2048]{2,1,0:T(8,128)(2,1)} %copy-done.9), calls=%async_computation.2 | async-start | bytes 1048576 | tf_op jit(solution)/shard_map/all_to_all | solution.py:548
  85.2 10.2 %copy-start.4 = (bf16[64,2,8,256]{3,2,1,0:T(8,128)(2,1)S(1)}, bf16[64,2,8,256]{3,2,1,0:T(8,128)(2,1)}, u32[]{:S(2)}) copy-start(bf16[64,2,8,256]{3,2,1,0:T(8,128)(2,1)} %pages.3) | copy-start | bytes 1572868
  85.2 10.2 %copy-start.12 = (s32[768]{0:T(1024)S(1)}, s32[768]{0:T(1024)}, u32[]{:S(2)}) copy-start(s32[768]{0:T(1024)} %copy-done.11) | copy-start | bytes 9220
  85.2 10.2 %copy-start.15 = (s32[8,8]{1,0:T(8,128)S(1)}, s32[8,8]{1,0:T(8,128)}, u32[]{:S(2)}) copy-start(s32[8,8]{1,0:T(8,128)} %table.3) | copy-start | bytes 772
  85.2 10.1 %all-to-all-start.3 = ((bf16[8,32,256]{2,1,0:T(8,128)(2,1)}), bf16[8,32,256]{2,1,0:T(8,128)(2,1)S(1)}, u32[]{:S(2)}, u32[]{:S(2)}) async-start(bf16[8,32,256]{2,1,0:T(8,128)(2,1)} %get-tuple-element.21), calls=%async_computation.3 | async-start | bytes 262144 | tf_op jit(solution)/shard_map/all_to_all | solution.py:559
  95.3 12.8 %copy-start.8 = (bf16[256,2048]{1,0:T(8,128)(2,1)S(1)}, bf16[256,2048]{1,0:T(8,128)(2,1)}, u32[]{:S(2)}) copy-start(bf16[256,2048]{1,0:T(8,128)(2,1)} %w_o.1) | copy-start | bytes 3145732
  108.2 14.4 %copy-start.10 = (f32[32,2048]{1,0:T(8,128)S(1)}, f32[32,2048]{1,0:T(8,128)}, u32[]{:S(2)}) copy-start(f32[32,2048]{1,0:T(8,128)} %get-tuple-element.20.hidden) | copy-start | bytes 786436
  (11 other events, 33.8 us)
